TPU v7x, 256 devices: a whole 4x4x8 slice. The times are simulated.
256 devices in a mesh: tm: 16 (over z, x_hi), rows: 16 (over x_lo, y, core).
Axes of the slice: x: 4 (x_hi: 2, x_lo: 2; x = x_hi * 2 + x_lo), y: 4, z: 8, core: 2. Of those that a mesh axis runs over, the one named last changes fastest.
Arguments:
- slc_stack: bfloat16 [64, 2, 128, 2048], P('tm', None, 'rows'), may hold values from -6 to 6
- partner_count: int32 [64], P('tm'), may hold values from 2 to 6, as said below
- look_sizes: int32 [64, 2], P('tm'), may hold values from 1 to 8, as said below
Outputs:
- interferogram: bfloat16 [64, 6, 2, 128, 2048], P('tm', None, None, 'rows')
- coherence: bfloat16 [64, 6, 128, 2048], P('tm', None, 'rows')
Inputs may be any that keep to these rules, and one draw needn't show every extreme that they name: `partner_count`: some acquisition has 6 partners and some has 2. `look_sizes`: Half-heights run from 1 to 2, half-widths from 2 to 8; some acquisition has (2, 8) and some (1, 2).
All inputs are finite; a program needn't handle non-finite values.
Results may differ from a plain program's by a relative error of at most 0.0049.
Values may be sent and summed in bfloat16 or wider, within the bound.
No kernel may reach another device: no remote copies, remote signals or barrier semaphores. Data moves between devices by JAX's collectives and lax.ppermute only.
A program may use at most 64 MiB of HBM per device.

v0:
```python
import jax
import jax.numpy as jnp
import numpy as np
from jax import lax
from jax.sharding import PartitionSpec as P

MAXP = 6
HR = 2


epsilon = 1e-06


def extended_2(block, sides, width):
    for axis, dim in sides:
        count = lax.axis_size(axis)
        forward = [(i, i + 1) for i in range(count - 1)]
        backward = [(target, source) for source, target in forward]
        low = lax.ppermute(
            lax.slice_in_dim(block, block.shape[dim] - width, None, axis=dim), axis, forward
        )
        high = lax.ppermute(lax.slice_in_dim(block, 0, width, axis=dim), axis, backward)
        block = jnp.concatenate([low, block, high], axis=dim)
    return block


def passed_along(block, axis, distance):
    devices = range(lax.axis_size(axis))
    route = [(i - distance, i) for i in devices if i - distance in devices]
    return lax.ppermute(block, axis, route)


def window_rows(fields, half_rows):
    row_count = fields.shape[-2] - 2 * HR
    shape_tail = (1,) * (fields.ndim - 1)
    total = jnp.zeros(fields.shape[:-2] + (row_count, fields.shape[-1]), jnp.float32)
    for offset in range(-HR, HR + 1):
        weight = (
            (jnp.abs(offset) <= half_rows)
            .astype(jnp.float32)
            .reshape((fields.shape[0],) + shape_tail)
        )
        total = total + weight * fields[..., HR + offset : HR + offset + row_count, :]
    return total


def make_bands(half_cols):
    inner = jnp.arange(384, dtype=jnp.int32)
    outer = jnp.arange(256, dtype=jnp.int32)
    distance = jnp.abs(inner[:, None] - 64 - outer[None, :])
    band = (distance[None] <= half_cols[:, None, None]).astype(jnp.bfloat16)
    return (band[:, :256], band[:, 256:])


def window_cols(summed, band_lead, band_tail):
    col_count = summed.shape[-1]
    blocks = col_count // 256
    padded = jnp.pad(summed, [(0, 0)] * (summed.ndim - 1) + [(64, 192)])
    lead_part = padded[..., :col_count].reshape(summed.shape[:-1] + (blocks, 256))
    tail_part = padded[..., 256 : col_count + 256].reshape(summed.shape[:-1] + (blocks, 256))[
        ..., :128
    ]
    result = jnp.einsum(
        "p...i,pij->p...j", lead_part, band_lead, preferred_element_type=jnp.float32
    )
    result = result + jnp.einsum(
        "p...i,pij->p...j", tail_part, band_tail, preferred_element_type=jnp.float32
    )
    return result.reshape(summed.shape)


def slot_fields(own_data, partners, half_rows, band_lead, band_tail, boxed_own, area):
    partner_data = partners.astype(jnp.float32)
    real_part = (
        own_data[:, :, 0] * partner_data[:, :, 0] + own_data[:, :, 1] * partner_data[:, :, 1]
    )
    imag_part = (
        own_data[:, :, 1] * partner_data[:, :, 0] - own_data[:, :, 0] * partner_data[:, :, 1]
    )
    power = (
        partner_data[:, :, 0] * partner_data[:, :, 0]
        + partner_data[:, :, 1] * partner_data[:, :, 1]
    )
    terms = jnp.stack([real_part, imag_part, power], 2)
    boxed = window_cols(window_rows(terms, half_rows).astype(jnp.bfloat16), band_lead, band_tail)
    ifg = boxed[:, :, :2] / area[:, None, None, None, None]
    magnitude = jnp.sqrt(boxed[:, :, 0] * boxed[:, :, 0] + boxed[:, :, 1] * boxed[:, :, 1])
    coh = magnitude * lax.rsqrt(boxed_own * boxed[:, :, 2] + epsilon)
    return (ifg, coh)


def local(slc_stack, partner_count, look_sizes):
    per_dev = slc_stack.shape[0]
    haloed = extended_2(slc_stack, (("rows", 2),), HR)
    nearby = passed_along(haloed, "tm", -1)
    farther = passed_along(haloed, "tm", -2)
    extended = jnp.concatenate([haloed, nearby, farther], 0)
    half_rows = look_sizes[:, 0]
    half_cols = look_sizes[:, 1]
    band_lead, band_tail = make_bands(half_cols)
    area = ((2 * half_rows + 1) * (2 * half_cols + 1)).astype(jnp.float32)
    own_data = haloed.astype(jnp.float32)
    own_power = (own_data[:, 0] * own_data[:, 0] + own_data[:, 1] * own_data[:, 1])[:, None]
    boxed_own = window_cols(
        window_rows(own_power, half_rows).astype(jnp.bfloat16), band_lead, band_tail
    )
    acq_total = lax.axis_size("tm") * per_dev
    global_index = lax.axis_index("tm") * per_dev + jnp.arange(per_dev, dtype=jnp.int32)
    offsets = jnp.arange(1, MAXP + 1, dtype=jnp.int32)
    static_index = (np.arange(per_dev)[:, None] + np.arange(1, MAXP + 1)[None, :]).reshape(-1)
    partners = extended[static_index].reshape((per_dev, MAXP) + extended.shape[1:])
    ifg, coh = slot_fields(
        own_data[:, None], partners, half_rows, band_lead, band_tail, boxed_own, area
    )
    live = (offsets[None, :] <= partner_count[:, None]) & (
        global_index[:, None] + offsets[None, :] < acq_total
    )
    interferogram = jnp.where(live[:, :, None, None, None], ifg, 0.0).astype(jnp.bfloat16)
    coherence = jnp.where(live[:, :, None, None], coh, 0.0).astype(jnp.bfloat16)
    return (interferogram, coherence)


def solution(mesh):
    return jax.shard_map(
        local,
        mesh=mesh,
        in_specs=(P("tm", None, "rows", None), P("tm"), P("tm", None)),
        out_specs=(P("tm", None, None, "rows", None), P("tm", None, "rows", None)),
        check_vma=False,
    )
```

profile of v0, /device:TPU:102, one launch (start us, length us, event | category | flops | bytes accessed | tf_op | source)
XLA Modules:
  0.0 79.8 jit_solution(8140253536304411444)
XLA Ops:
  0.6 1.2 %fusion.43 = (bf16[4,2,2,2048]{3,2,1,0:T(2,128)(2,1)S(1)}, bf16[4,2,2,2048]{3,2,1,0:T(2,128)(2,1)S(1)}) fusion(bf16[4,2,8,2048]{3,2,1,0:T(8,128)(2,1)} %param.5), kind=kLoop, calls=%fused_computation.89 | loop fusion | bytes 262144 | tf_op jit(solution)/shard_map/slice | solution.py:20
  1.8 1.9 %collective-permute-start = (bf16[4,2,2,2048]{3,2,1,0:T(2,128)(2,1)S(1)}, bf16[4,2,2,2048]{3,2,1,0:T(2,128)(2,1)S(1)}, u32[]{:S(2)}, u32[]{:S(2)}) collective-permute-start(bf16[4,2,2,2048]{3,2,1,0:T(2,128)(2,1)S(1)} %get-tuple-element.11), channel_id=1, source_target_pairs={{0,1},{1,2},{2,3},{3,4},{4,5},{5,6},{6,7},{7,8},{8,9},{9,10},{10,1... | collective-permute-start | bytes 196616 | tf_op jit(solution)/shard_map/ppermute | solution.py:19
  3.7 5.8 %collective-permute-start.1 = (bf16[4,2,2,2048]{3,2,1,0:T(2,128)(2,1)S(1)}, bf16[4,2,2,2048]{3,2,1,0:T(2,128)(2,1)S(1)}, u32[]{:S(2)}, u32[]{:S(2)}) collective-permute-start(bf16[4,2,2,2048]{3,2,1,0:T(2,128)(2,1)S(1)} %get-tuple-element.12), channel_id=1, source_target_pairs={{1,0},{2,1},{3,2},{4,3},{5,4},{6,5},{7,6},{8,7},{9,8},{10,9},{11,1... | collective-permute-start | bytes 196616 | tf_op jit(solution)/shard_map/ppermute | solution.py:22
  9.5 0.8 fusion.41
  10.3 0.7 slice_bitcast_fusion.7
  10.9 0.7 fusion.38
  11.8 0.3 broadcast_compare_fusion
  12.0 0.7 fusion.37
  12.8 0.7 pad_clamp_fusion
  13.4 1.2 %fusion.42 = (f32[4,2,12,2048]{3,2,1,0:T(8,128)S(1)}, bf16[4,2,12,2048]{3,2,1,0:T(8,128)(2,1)S(1)}) fusion(bf16[4,2,2,2048]{3,2,1,0:T(2,128)(2,1)S(1)} %collective-permute-done.1, bf16[4,2,8,2048]{3,2,1,0:T(8,128)(2,1)} %param.5, bf16[4,2,2,2048]{3,2,1,0:T(2,128)(2,1)S(1)} %collective-permute-done), kind=kLoop, calls=%fused_computation.88 | loop fusion | flops 1376256 | bytes 1572864 | tf_op jit(solution)/shard_map/convert_element_type | solution.py:102
  14.6 2.1 %collective-permute-start.3 = (bf16[4,2,12,2048]{3,2,1,0:T(8,128)(2,1)S(1)}, bf16[4,2,12,2048]{3,2,1,0:T(8,128)(2,1)S(1)}, u32[]{:S(2)}, u32[]{:S(2)}) collective-permute-start(bf16[4,2,12,2048]{3,2,1,0:T(8,128)(2,1)S(1)} %get-tuple-element.10), channel_id=1, source_target_pairs={{32,0},{48,16},{64,32},{80,48},{96,64},{112,80},{128,96},{144,112}... | collective-permute-start | bytes 1179656 | tf_op jit(solution)/shard_map/ppermute | solution.py:30
  16.8 3.3 %collective-permute-start.2 = (bf16[4,2,12,2048]{3,2,1,0:T(8,128)(2,1)S(1)}, bf16[4,2,12,2048]{3,2,1,0:T(8,128)(2,1)}, u32[]{:S(2)}, u32[]{:S(2)}) collective-permute-start(bf16[4,2,12,2048]{3,2,1,0:T(8,128)(2,1)S(1)} %get-tuple-element.10), channel_id=1, source_target_pairs={{16,0},{32,16},{48,32},{64,48},{80,64},{96,80},{112,96},{128,112},... | collective-permute-start | bytes 1179656 | tf_op jit(solution)/shard_map/ppermute | solution.py:30
  20.6 0.3 fusion.20
  21.1 0.7 mul.204
  21.8 0.2 maximum_convert_fusion
  22.1 7.6 %collective-permute-done.3 = bf16[4,2,12,2048]{3,2,1,0:T(8,128)(2,1)S(1)} collective-permute-done((bf16[4,2,12,2048]{3,2,1,0:T(8,128)(2,1)S(1)}, bf16[4,2,12,2048]{3,2,1,0:T(8,128)(2,1)S(1)}, u32[]{:S(2)}, u32[]{:S(2)}) %collective-permute-start.3) | collective-permute-done | bytes 393248 | tf_op jit(solution)/shard_map/ppermute | solution.py:30
  29.7 0.8 copy-done.3
  30.5 11.4 %collective-permute-done.2 = bf16[4,2,12,2048]{3,2,1,0:T(8,128)(2,1)} collective-permute-done((bf16[4,2,12,2048]{3,2,1,0:T(8,128)(2,1)S(1)}, bf16[4,2,12,2048]{3,2,1,0:T(8,128)(2,1)}, u32[]{:S(2)}, u32[]{:S(2)}) %collective-permute-start.2) | collective-permute-done | bytes 393248 | tf_op jit(solution)/shard_map/ppermute | solution.py:30
  41.9 1.5 %pad_maximum_fusion.1 = bf16[12,2,12,2048]{3,2,1,0:T(8,128)(2,1)S(1)} fusion(bf16[4,2,12,2048]{3,2,1,0:T(8,128)(2,1)} %copy-done.3, bf16[4,2,12,2048]{3,2,1,0:T(8,128)(2,1)} %collective-permute-done.2, bf16[4,2,2,2048]{3,2,1,0:T(2,128)(2,1)S(1)} %collective-permute-done.1, bf16[4,2,8,2048]{3,2,1,0:T(8,128)(2,1)S(1)} %copy-done.1, ...), kind=kLoop, calls=%fused_computation.35 | loop fusion | flops 5898240 | bytes 2359296 | tf_op jit(solution)/shard_map/concatenate | solution.py:97
  43.5 2.5 %gather_fusion = bf16[24,2,12,2048]{3,2,1,0:T(8,128)(2,1)} fusion(bf16[12,2,12,2048]{3,2,1,0:T(8,128)(2,1)S(1)} %pad_maximum_fusion.1, s32[1024]{0:T(1024)S(1)} %pad_clamp_fusion), kind=kCustom, calls=%fused_computation | custom fusion | bytes 4718688 | tf_op jit(solution)/shard_map/gather | solution.py:111
  46.0 2.7 %convert.4 = f32[4,6,2,12,2048]{4,3,2,1,0:T(8,128)S(1)} convert(bf16[4,6,2,12,2048]{4,3,2,1,0:T(8,128)(2,1)} %bitcast.115) | non-fusion elementwise | flops 1179648 | bytes 7077888 | tf_op jit(solution)/shard_map/convert_element_type | solution.py:73
  48.7 3.1 %multiply_add_fusion.1 = (f32[4,6,1,12,2048]{4,3,2,1,0:T(8,128)S(1)}, f32[4,6,1,12,2048]{4,3,2,1,0:T(8,128)S(1)}, f32[4,6,1,12,2048]{4,3,2,1,0:T(8,128)}) fusion(f32[4,6,2,12,2048]{4,3,2,1,0:T(8,128)S(1)} %convert.4, f32[4,12,2048]{2,1,0:T(8,128)S(1)} %get-tuple-element.8, f32[4,12,2048]{2,1,0:T(8,128)S(1)} %get-tuple-element.7), kind=kLoop, calls=%fused_computation.17 | loop fusion | flops 5308416 | bytes 12582912 | tf_op jit(solution)/shard_map/add | solution.py:75
  51.8 2.3 %pad_maximum_fusion = f32[4,6,3,12,2048]{4,3,2,1,0:T(8,128)S(1)} fusion(f32[4,6,1,12,2048]{4,3,2,1,0:T(8,128)} %get-tuple-element.4, f32[4,6,1,12,2048]{4,3,2,1,0:T(8,128)S(1)} %get-tuple-element.3, f32[4,6,1,12,2048]{4,3,2,1,0:T(8,128)S(1)} %get-tuple-element.2), kind=kLoop, calls=%fused_computation.1 | loop fusion | flops 3538944 | bytes 14155776 | tf_op jit(solution)/shard_map/stack | solution.py:84
  54.1 3.8 %fusion.1 = bf16[4,6,3,8,2048]{4,3,2,1,0:T(8,128)(2,1)} fusion(f32[4,6,3,12,2048]{4,3,2,1,0:T(8,128)S(1)} %pad_maximum_fusion, f32[4]{0:T(128)S(1)} %get-tuple-element.17, f32[4]{0:T(128)S(1)} %get-tuple-element.16, f32[4]{0:T(128)S(1)} %get-tuple-element.15), kind=kLoop, calls=%fused_computation.4 | loop fusion | flops 11796480 | bytes 25952304 | tf_op jit(solution)/shard_map/convert_element_type | solution.py:85
  57.9 4.7 %pad_slice_fusion.1 = (bf16[4,6,3,8,2048]{4,3,2,1,0:T(8,128)(2,1)S(1)}, bf16[4,6,3,8,2048]{4,3,2,1,0:T(8,128)(2,1)S(1)}) fusion(bf16[4,6,3,8,2048]{4,3,2,1,0:T(8,128)(2,1)} %fusion.1), kind=kLoop, calls=%fused_computation.19 | loop fusion | bytes 7077888 | tf_op jit(solution)/shard_map/slice | solution.py:59
  62.6 0.8 copy.17
  63.4 0.8 copy.18
  64.2 0.8 fusion.18
  65.0 3.0 %convolution_add_fusion = f32[4,6,3,8,8,256]{5,4,3,2,1,0:T(8,128)} fusion(f32[4,6,3,8,8,256]{5,4,3,2,1,0:T(8,128)S(1)} %fusion.18, bf16[4,6,3,8,8,256]{5,4,3,2,1,0:T(8,128)(2,1)S(1)} %bitcast.114, pred[4,384,256]{2,1,0:T(32,128)(4,1)S(1)} %broadcast_compare_fusion), kind=kOutput, calls=%fused_computation.20 | convolution fusion | flops 605159424 | bytes 12058624 | tf_op jit(solution)/shard_map/p...i,pij->p...j/dot_general | solution.py:63
  68.0 6.0 %reshape.311 = f32[4,6,3,8,2048]{4,3,2,1,0:T(8,128)} reshape(f32[4,6,3,8,8,256]{5,4,3,2,1,0:T(8,128)} %convolution_add_fusion) | data formatting | bytes 9437184 | tf_op jit(solution)/shard_map/reshape | solution.py:69
  74.0 4.2 %fusion.12 = bf16[4,6,8,2048]{3,2,1,0:T(8,128)(2,1)} fusion(f32[4,6,3,8,2048]{4,3,2,1,0:T(8,128)} %reshape.311, f32[4,8,2048]{2,1,0:T(8,128)S(1)} %copy-done.2, pred[4,6]{1,0:T(4,128)(4,1)S(1)} %fusion.37), kind=kLoop, calls=%fused_computation.27 | loop fusion | flops 3145728 | bytes 5767192 | tf_op jit(solution)/shard_map/convert_element_type | solution.py:119
  78.2 1.6 %fusion.6 = bf16[4,6,2,8,2048]{4,3,2,1,0:T(8,128)(2,1)} fusion(f32[4,6,3,8,2048]{4,3,2,1,0:T(8,128)S(1)} %copy-done, f32[4]{0:T(128)S(1)} %fusion.41, pred[4,6]{1,0:T(4,128)(4,1)S(1)} %fusion.37), kind=kLoop, calls=%fused_computation.14 | loop fusion | flops 2359296 | bytes 4718632 | tf_op jit(solution)/shard_map/convert_element_type | solution.py:118
  (19 shorter events, 0.8 us)
Async XLA Ops:
  1.8 11.6 %collective-permute-start = (bf16[4,2,2,2048]{3,2,1,0:T(2,128)(2,1)S(1)}, bf16[4,2,2,2048]{3,2,1,0:T(2,128)(2,1)S(1)}, u32[]{:S(2)}, u32[]{:S(2)}) collective-permute-start(bf16[4,2,2,2048]{3,2,1,0:T(2,128)(2,1)S(1)} %get-tuple-element.11), channel_id=1, source_target_pairs={{0,1},{1,2},{2,3},{3,4},{4,5},{5,6},{6,7},{7,8},{8,9},{9,10},{10,1... | collective-permute-start | bytes 196616 | tf_op jit(solution)/shard_map/ppermute | solution.py:19
  3.7 9.7 %collective-permute-start.1 = (bf16[4,2,2,2048]{3,2,1,0:T(2,128)(2,1)S(1)}, bf16[4,2,2,2048]{3,2,1,0:T(2,128)(2,1)S(1)}, u32[]{:S(2)}, u32[]{:S(2)}) collective-permute-start(bf16[4,2,2,2048]{3,2,1,0:T(2,128)(2,1)S(1)} %get-tuple-element.12), channel_id=1, source_target_pairs={{1,0},{2,1},{3,2},{4,3},{5,4},{6,5},{7,6},{8,7},{9,8},{10,9},{11,1... | collective-permute-start | bytes 196616 | tf_op jit(solution)/shard_map/ppermute | solution.py:22
  14.6 7.2 %copy-start.1 = (bf16[4,2,8,2048]{3,2,1,0:T(8,128)(2,1)S(1)}, bf16[4,2,8,2048]{3,2,1,0:T(8,128)(2,1)}, u32[]{:S(2)}) copy-start(bf16[4,2,8,2048]{3,2,1,0:T(8,128)(2,1)} %param.5) | copy-start | bytes 786436
  14.6 15.1 %collective-permute-start.3 = (bf16[4,2,12,2048]{3,2,1,0:T(8,128)(2,1)S(1)}, bf16[4,2,12,2048]{3,2,1,0:T(8,128)(2,1)S(1)}, u32[]{:S(2)}, u32[]{:S(2)}) collective-permute-start(bf16[4,2,12,2048]{3,2,1,0:T(8,128)(2,1)S(1)} %get-tuple-element.10), channel_id=1, source_target_pairs={{32,0},{48,16},{64,32},{80,48},{96,64},{112,80},{128,96},{144,112}... | collective-permute-start | bytes 1179656 | tf_op jit(solution)/shard_map/ppermute | solution.py:30
  16.8 25.1 %collective-permute-start.2 = (bf16[4,2,12,2048]{3,2,1,0:T(8,128)(2,1)S(1)}, bf16[4,2,12,2048]{3,2,1,0:T(8,128)(2,1)}, u32[]{:S(2)}, u32[]{:S(2)}) collective-permute-start(bf16[4,2,12,2048]{3,2,1,0:T(8,128)(2,1)S(1)} %get-tuple-element.10), channel_id=1, source_target_pairs={{16,0},{32,16},{48,32},{64,48},{80,64},{96,80},{112,96},{128,112},... | collective-permute-start | bytes 1179656 | tf_op jit(solution)/shard_map/ppermute | solution.py:30
  29.7 0.8 copy-start.3
  68.0 6.0 %copy-start.2 = (f32[4,8,2048]{2,1,0:T(8,128)S(1)}, f32[4,8,2048]{2,1,0:T(8,128)}, u32[]{:S(2)}) copy-start(f32[4,8,2048]{2,1,0:T(8,128)} %mul.204) | copy-start | bytes 786436
  74.0 4.2 %copy-start = (f32[4,6,3,8,2048]{4,3,2,1,0:T(8,128)S(1)}, f32[4,6,3,8,2048]{4,3,2,1,0:T(8,128)}, u32[]{:S(2)}) copy-start(f32[4,6,3,8,2048]{4,3,2,1,0:T(8,128)} %reshape.311) | copy-start | bytes 14155780
where the time goes:
time: 80.3 us; the launch traced here: 79.8 us
  other arithmetic  24.2 us (30%)
  waiting for transfers between devices  19 us (24%)
  local copies, waits for them, and re-layouts  18.4 us (23%)
  starting transfers between devices  13.1 us (16%)
  matrix products  4.28 us (5%)
  between operations  0.81 us (1%)
    ppermute x2, waiting for transfers between devices, passed_along(): return lax.ppermute(block, axis, route)  19 us
    reshape x1, local copies, waits for them, and re-layouts, window_cols(): return result.reshape(summed.shape)  6.01 us
    ppermute x1, starting transfers between devices, extended_2(): lax.ppermute(lax.slice_in_dim(block, 0, width, axis=dim), axis, backward)  5.75 us
    ppermute x2, starting transfers between devices, passed_along(): return lax.ppermute(block, axis, route)  5.46 us
    slice x1, local copies, waits for them, and re-layouts, window_cols(): padded[..., :col_count].reshape(summed.shape[:-1] + (blocks, 256))  4.71 us
    convert_element_type x1, other arithmetic, local(): coherence = jnp.where(live[:, :, None, None], coh, 0.0).astype(jnp.bfloat16)  4.2 us
    convert_element_type x1, other arithmetic, slot_fields(): window_rows(terms, half_rows).astype(jnp.bfloat16)  3.8 us
    dot_general x2, matrix products, window_cols(): jnp.einsum('p...i,pij->p...j', lead_part, band_lead, preferred_element_ty...  3.26 us
  transfers between devices with their start and end apart: 4, of which 2 were waited for; matrix products, arithmetic and copies ran while one was open for 7% of the time, Pallas kernels for 0%

commit v1 on v0

v1 whole, which is shorter than its diff:
```python
import functools

import jax
import jax.numpy as jnp
from jax import lax
from jax.experimental import pallas as pl
from jax.experimental.pallas import tpu as pltpu
from jax.sharding import PartitionSpec as P

MAXP = 6
ROWS = 8
HALO = 2
NEAR = 10
EDGE = 2 * NEAR
FIELDS = 160
BLOCK = 256
epsilon = 1e-06
F32 = jnp.float32
BF16 = jnp.bfloat16


def iota(shape, dim):
    return lax.broadcasted_iota(jnp.int32, shape, dim)


def place():
    row = lax.axis_index("rows")
    return row, lax.rem(row, 2), lax.axis_size("rows")


def weights_kernel(looks, row_weights, bands):
    row, core, row_total = place()
    at = iota((8, 256), 1)
    halo_at = at - 152
    inside = halo_at >= 0
    inner = halo_at >= 48
    group = lax.shift_right_arithmetic(jnp.where(inner, halo_at - 48, halo_at), 4)
    near = lax.shift_right_arithmetic(halo_at, 1) & 7
    slot_ok = (near >= 1) & (near <= 6)
    halo_field = jnp.where(
        group == 2,
        jnp.where(near <= 6, 12 + near, 99),
        jnp.where(slot_ok, 6 * group + near - 1, 99),
    )
    field = jnp.where(inside, halo_field, lax.shift_right_arithmetic(at, 3))
    above = jnp.where(inner, core, 1 - core) == 1
    edge = (halo_at & 1) + jnp.where(above, -HALO, ROWS)
    position = jnp.where(inside, edge, at & 7)
    open_edge = jnp.where(core == 0, row > 0, row < row_total - 1)
    usable = ~inside | inner | open_edge
    field = jnp.where(usable & (at < 248), field, 99)
    distance = jnp.abs(position - iota((8, 256), 0))
    for a in range(4):
        hit = distance <= looks[a, 0]
        for f in range(FIELDS // 16):
            pair = [jnp.where(hit & (field == 2 * f + i), 1.0, 0.0) for i in range(2)]
            row_weights[a, 16 * f : 16 * f + 16, :] = jnp.concatenate(pair, 0).astype(BF16)
    inner_at = iota((384, 256), 0)
    column = jnp.where(
        inner_at < 320, inner_at, inner_at - 384
    )
    spread = jnp.abs(column - iota((384, 256), 1))
    for a in range(4):
        bands[a] = jnp.where(spread <= looks[a, 1], 1.0, 0.0).astype(BF16)


def edges_kernel(own, next_1, next_2, outer, inner):
    row, core, _ = place()
    to = iota((2 * 2 * EDGE, 2 * NEAR * ROWS), 0)
    source = iota((2 * 2 * EDGE, 2 * NEAR * ROWS), 1)
    is_inner = to >= 2 * EDGE
    to = jnp.where(is_inner, to - 2 * EDGE, to)
    high = jnp.where(is_inner, 1 - core, core) == 1
    wanted = lax.shift_right_arithmetic(to, 1) * ROWS + (to & 1) + jnp.where(high, ROWS - HALO, 0)
    pick = jnp.where(source == wanted, 1.0, 0.0).astype(BF16)

    def body(n, carry):
        cols = pl.ds(pl.multiple_of(n * BLOCK, BLOCK), BLOCK)
        parts = []
        for c in range(2):
            for ref in (own, next_1, next_2):
                for e in range(ref.shape[0]):
                    parts.append(ref[e, c, :, cols].astype(F32))
        data = jnp.concatenate(parts, 0).astype(BF16)
        picked = jnp.dot(pick, data, preferred_element_type=F32).astype(BF16)
        outer[:, cols] = picked[: 2 * EDGE]
        inner[:, cols] = picked[2 * EDGE :]
        return carry

    lax.fori_loop(0, own.shape[-1] // BLOCK, body, 0)


def repeated(tile, first):
    rows = iota(tile.shape, 0)
    kept = jnp.where((rows >= first) & (rows < first + 2), tile, 0.0)
    kept = kept + pltpu.roll(kept, 2, 0)
    return kept + pltpu.roll(kept, 4, 0)


def products(own_re, own_im, re, im):
    return own_re * re + own_im * im, own_im * re - own_re * im


def main_kernel(
    counts, looks, own, next_1, next_2, outer, inner, row_weights, bands,
    ifg_out, coh_out, edge_rows, sums, ifg, coh, sems,
):
    cols_total = own.shape[-1]
    blocks = cols_total // BLOCK
    sums[:, :128] = jnp.zeros((FIELDS, 128), BF16)
    sums[:, 128 + cols_total :] = jnp.zeros((FIELDS, 128), BF16)
    for h, ref in enumerate((outer, inner)):
        edge_rows[h, 2 * EDGE :, :] = jnp.zeros((8, cols_total), F32)
        edge_rows[h, : 2 * EDGE, :] = ref[...].astype(F32)
    near = [own.at[e] for e in range(4)] + [next_1.at[e] for e in range(4)] + [next_2.at[e] for e in range(2)]
    first_acq = lax.axis_index("tm") * 4
    acq_total = lax.axis_size("tm") * 4
    copies = []
    for a in range(4):
        def row_body(n, carry, a=a):
            start = pl.multiple_of(n * BLOCK, BLOCK)
            cols = pl.ds(start, BLOCK)
            res, ims, pows = [], [], []
            own_re = own[a, 0, :, cols].astype(F32)
            own_im = own[a, 1, :, cols].astype(F32)
            pows.append(own_re * own_re + own_im * own_im)
            for j in range(1, MAXP + 1):
                re = near[a + j][0, :, cols].astype(F32)
                im = near[a + j][1, :, cols].astype(F32)
                prod_re, prod_im = products(own_re, own_im, re, im)
                res.append(prod_re)
                ims.append(prod_im)
                pows.append(re * re + im * im)
            fields = res + ims + pows
            for h in range(2):
                mine = []
                for c in range(2):
                    at = c * EDGE + 2 * a
                    tile = edge_rows[h, at // 8 * 8 : at // 8 * 8 + 8, cols]
                    mine.append(repeated(tile, at % 8))
                res, ims, pows = [], [], []
                for half in range(2):
                    at = 2 * a + 8 * half
                    re = edge_rows[h, at : at + 8, cols]
                    im = edge_rows[h, at + EDGE : at + EDGE + 8, cols]
                    prod_re, prod_im = products(mine[0], mine[1], re, im)
                    res.append(prod_re)
                    ims.append(prod_im)
                    pows.append(re * re + im * im)
                fields += res + ims + pows
            fields.append(jnp.zeros((8, BLOCK), F32))
            terms = jnp.concatenate(fields, 0).astype(BF16)
            summed = jnp.dot(row_weights[a], terms, preferred_element_type=F32)
            sums[:, pl.ds(pl.multiple_of(start + 128, 128), BLOCK)] = summed.astype(BF16)
            return carry

        lax.fori_loop(0, blocks, row_body, 0)
        half_rows, half_cols = looks[a, 0], looks[a, 1]
        area = ((2 * half_rows + 1) * (2 * half_cols + 1)).astype(F32)
        lives = []
        for j in range(MAXP):
            live = (j < counts[a]) & (first_acq + a + j + 1 < acq_total)
            lives.append(jnp.where(live, 1.0, 0.0).astype(F32))

        def col_body(n, carry, a=a, lives=lives, area=area):
            start = pl.multiple_of(n * BLOCK, BLOCK)
            cols = pl.ds(start, BLOCK)
            inside = sums[:, pl.ds(pl.multiple_of(start + 128, 128), BLOCK)]
            left = sums[:, pl.ds(start, 128)]
            right = sums[:, pl.ds(pl.multiple_of(start + 128 + BLOCK, 128), 128)]
            sides = jnp.where(iota((FIELDS, 128), 1) < 64, right, left)
            boxed = jnp.dot(inside, bands[a, :BLOCK, :], preferred_element_type=F32)
            boxed = boxed + jnp.dot(sides, bands[a, BLOCK:, :], preferred_element_type=F32)
            own_power = boxed[96:104]
            for j in range(MAXP):
                re = boxed[8 * j : 8 * j + 8]
                im = boxed[48 + 8 * j : 56 + 8 * j]
                power = boxed[104 + 8 * j : 112 + 8 * j]
                scale = jnp.full((8, BLOCK), lives[j], F32) / jnp.full((8, BLOCK), area, F32)
                ifg[a, j, 0, :, cols] = (re * scale).astype(BF16)
                ifg[a, j, 1, :, cols] = (im * scale).astype(BF16)
                magnitude = jnp.sqrt(re * re + im * im)
                coherence = magnitude * lax.rsqrt(own_power * power + epsilon) * lives[j]
                coh[a, j, :, cols] = coherence.astype(BF16)
            return carry

        lax.fori_loop(0, blocks, col_body, 0)
        for k, (scratch, out) in enumerate(((ifg, ifg_out), (coh, coh_out))):
            copy = pltpu.make_async_copy(scratch.at[a], out.at[a], sems.at[a, k])
            copy.start()
            copies.append(copy)
    for copy in copies:
        copy.wait()


VMEM = pl.BlockSpec(memory_space=pltpu.VMEM)
SMEM = pl.BlockSpec(memory_space=pltpu.SMEM)
PARAMS = pltpu.CompilerParams(vmem_limit_bytes=48 * 2**20)


def shifted(block, distance):
    count = lax.axis_size("tm")
    return lax.ppermute(block, "tm", [(i, (i - distance) % count) for i in range(count)])


def local(slc_stack, partner_count, look_sizes):
    cols = slc_stack.shape[-1]
    rows = lax.axis_size("rows")
    next_1 = shifted(slc_stack, 1)
    next_2 = shifted(slc_stack[:2], 2)
    row_weights, bands = pl.pallas_call(
        weights_kernel,
        in_specs=[SMEM],
        out_specs=[VMEM, VMEM],
        out_shape=[
            jax.ShapeDtypeStruct((4, FIELDS, 256), BF16),
            jax.ShapeDtypeStruct((4, 384, 256), BF16),
        ],
        compiler_params=PARAMS,
        name="weights",
    )(look_sizes)
    edge_shape = jax.ShapeDtypeStruct((2 * EDGE, cols), BF16)
    outer, inner = pl.pallas_call(
        edges_kernel,
        in_specs=[VMEM] * 3,
        out_specs=[VMEM] * 2,
        out_shape=[edge_shape] * 2,
        compiler_params=PARAMS,
        name="edges",
    )(slc_stack, next_1, next_2)
    outer = lax.ppermute(
        outer, "rows", [((i + 1 - 2 * (1 - i % 2)) % rows, i) for i in range(rows)]
    )
    inner = lax.ppermute(inner, "rows", [(i ^ 1, i) for i in range(rows)])
    return pl.pallas_call(
        main_kernel,
        in_specs=[SMEM, SMEM] + [VMEM] * 7,
        out_specs=[pl.BlockSpec(memory_space=pl.ANY)] * 2,
        out_shape=[
            jax.ShapeDtypeStruct((4, MAXP, 2, ROWS, cols), BF16),
            jax.ShapeDtypeStruct((4, MAXP, ROWS, cols), BF16),
        ],
        scratch_shapes=[
            pltpu.VMEM((2, 2 * EDGE + 8, cols), F32),
            pltpu.VMEM((FIELDS, cols + 256), BF16),
            pltpu.VMEM((4, MAXP, 2, ROWS, cols), BF16),
            pltpu.VMEM((4, MAXP, ROWS, cols), BF16),
            pltpu.SemaphoreType.DMA((4, 2)),
        ],
        compiler_params=PARAMS,
        name="windows",
    )(partner_count, look_sizes, slc_stack, next_1, next_2, outer, inner, row_weights, bands)


def solution(mesh):
    return jax.shard_map(
        local,
        mesh=mesh,
        in_specs=(P("tm", None, "rows", None), P("tm"), P("tm", None)),
        out_specs=(P("tm", None, None, "rows", None), P("tm", None, "rows", None)),
        check_vma=False,
    )
```

time: 80.3 us -> 42.3 us (0.53)
  the two profiles are of different devices: /device:TPU:102 before, /device:TPU:1 now
where the time goes in v1:
time: 42.3 us; the launch traced here: 41.8 us
  Pallas kernels  16.6 us (39%)
  starting transfers between devices  13 us (31%)
  waiting for transfers between devices  7.26 us (17%)
  local copies, waits for them, and re-layouts  4.27 us (10%)
  between operations  0.66 us (2%)
    pallas_call x1, Pallas kernels, local(): pl.pallas_call(main_kernel, in_specs=[SMEM, SMEM] + [VMEM] * 7, out_specs...  14.7 us
    ppermute x2, starting transfers between devices, shifted(): lax.ppermute(block, 'tm', [(i, (i - distance) % count) for i in range(cou...  9.75 us
    ppermute x2, waiting for transfers between devices, shifted(): lax.ppermute(block, 'tm', [(i, (i - distance) % count) for i in range(cou...  6.24 us
    unnamed x7, local copies, waits for them, and re-layouts  3.32 us
    ppermute x1, starting transfers between devices, local(): lax.ppermute(outer, 'rows', [((i + 1 - 2 * (1 - i % 2)) % rows, i) for i...  2.81 us
    pallas_call x1, Pallas kernels, local(): pl.pallas_call(edges_kernel, in_specs=[VMEM] * 3, out_specs=[VMEM] * 2, o...  1.2 us
    ppermute x1, waiting for transfers between devices, local(): lax.ppermute(outer, 'rows', [((i + 1 - 2 * (1 - i % 2)) % rows, i) for i...  1.01 us
    slice x1, local copies, waits for them, and re-layouts, local(): next_2 = shifted(slc_stack[:2], 2)  0.95 us
  transfers between devices with their start and end apart: 4, of which 2 were waited for; matrix products, arithmetic and copies ran while one was open for 4% of the time, Pallas kernels for 2%

profile of v1, /device:TPU:1, one launch (start us, length us, event | category | flops | bytes accessed | tf_op | source)
XLA Modules:
  0.0 41.8 jit_solution(14084584794060975879)
XLA Ops:
  0.6 8.9 %collective-permute-start = (bf16[4,2,8,2048]{3,2,1,0:T(8,128)(2,1)}, bf16[4,2,8,2048]{3,2,1,0:T(8,128)(2,1)S(1)}, u32[]{:S(2)}, u32[]{:S(2)}) collective-permute-start(bf16[4,2,8,2048]{3,2,1,0:T(8,128)(2,1)} %own.3), channel_id=1, source_target_pairs={{0,240},{16,0},{32,16},{48,32},{64,48},{80,64},{96,80},{112,96},{1... | collective-permute-start | bytes 786440 | tf_op jit(solution)/shard_map/ppermute | solution.py:203
  9.6 0.9 %slice.3 = bf16[2,2,8,2048]{3,2,1,0:T(8,128)(2,1)S(1)} slice(bf16[4,2,8,2048]{3,2,1,0:T(8,128)(2,1)} %own.3), slice={[0:2], [0:2], [0:8], [0:2048]} | slice | bytes 262144 | tf_op jit(solution)/shard_map/slice | solution.py:210
  10.5 0.8 %collective-permute-start.1 = (bf16[2,2,8,2048]{3,2,1,0:T(8,128)(2,1)S(1)}, bf16[2,2,8,2048]{3,2,1,0:T(8,128)(2,1)S(1)}, u32[]{:S(2)}, u32[]{:S(2)}) collective-permute-start(bf16[2,2,8,2048]{3,2,1,0:T(8,128)(2,1)S(1)} %slice.3), channel_id=1, source_target_pairs={{0,224},{16,240},{32,0},{48,16},{64,32},{80,48},{96,64},{112,80},{... | collective-permute-start | bytes 393224 | tf_op jit(solution)/shard_map/ppermute | solution.py:203
  11.3 6.2 %collective-permute-done.1.next_2 = bf16[2,2,8,2048]{3,2,1,0:T(8,128)(2,1)S(1)} collective-permute-done((bf16[2,2,8,2048]{3,2,1,0:T(8,128)(2,1)S(1)}, bf16[2,2,8,2048]{3,2,1,0:T(8,128)(2,1)S(1)}, u32[]{:S(2)}, u32[]{:S(2)}) %collective-permute-start.1) | collective-permute-done | bytes 131104 | tf_op jit(solution)/shard_map/ppermute | solution.py:203
  17.6 0.0 collective-permute-done.next_1
  17.6 0.0 copy-start
  17.6 0.9 %copy-done = bf16[4,2,8,2048]{3,2,1,0:T(8,128)(2,1)S(1)} copy-done((bf16[4,2,8,2048]{3,2,1,0:T(8,128)(2,1)S(1)}, bf16[4,2,8,2048]{3,2,1,0:T(8,128)(2,1)}, u32[]{:S(2)}) %copy-start) | copy-done | bytes 262168
  18.5 1.2 %edges.1 = (bf16[40,2048]{1,0:T(8,128)(2,1)S(1)}, bf16[40,2048]{1,0:T(8,128)(2,1)S(1)}) custom-call(bf16[4,2,8,2048]{3,2,1,0:T(8,128)(2,1)S(1)} %copy-done, bf16[4,2,8,2048]{3,2,1,0:T(8,128)(2,1)S(1)} %collective-permute-done.next_1, bf16[2,2,8,2048]{3,2,1,0:T(8,128)(2,1)S(1)} %collective-permute-done.1.next_2), custom_call_target="tpu_custom_call" | custom-call | tf_op jit(solution)/shard_map/edges/pallas_call | solution.py:223
  19.7 2.8 %collective-permute-start.2 = (bf16[40,2048]{1,0:T(8,128)(2,1)S(1)}, bf16[40,2048]{1,0:T(8,128)(2,1)S(1)}, u32[]{:S(2)}, u32[]{:S(2)}) collective-permute-start(bf16[40,2048]{1,0:T(8,128)(2,1)S(1)} %get-tuple-element.6), channel_id=1, source_target_pairs={{15,0},{2,1},{1,2},{4,3},{3,4},{6,5},{5,6},{8,7},{7,8},{10,9},{9,1... | collective-permute-start | bytes 491528 | tf_op jit(solution)/shard_map/ppermute | solution.py:231
  22.5 0.4 %collective-permute-start.3 = (bf16[40,2048]{1,0:T(8,128)(2,1)S(1)}, bf16[40,2048]{1,0:T(8,128)(2,1)S(1)}, u32[]{:S(2)}, u32[]{:S(2)}) collective-permute-start(bf16[40,2048]{1,0:T(8,128)(2,1)S(1)} %get-tuple-element.7), channel_id=1, source_target_pairs={{1,0},{0,1},{3,2},{2,3},{5,4},{4,5},{7,6},{6,7},{9,8},{8,9},{11,10... | collective-permute-start | bytes 491528 | tf_op jit(solution)/shard_map/ppermute | solution.py:234
  23.0 0.8 %copy.6.looks = s32[4,2]{1,0:T(4,128)S(1)} copy(s32[4,2]{0,1:T(2,128)} %param.5) | data formatting | bytes 64 | tf_op args[2]
  23.7 0.8 %weights.1 = (bf16[4,160,256]{2,1,0:T(8,128)(2,1)S(1)}, bf16[4,384,256]{2,1,0:T(8,128)(2,1)S(1)}) custom-call(s32[4,2]{1,0:T(4,128)S(1)} %copy.6.looks), custom_call_target="tpu_custom_call" | custom-call | tf_op jit(solution)/shard_map/weights/pallas_call | solution.py:211
  24.5 1.0 %collective-permute-done.2.outer = bf16[40,2048]{1,0:T(8,128)(2,1)S(1)} collective-permute-done((bf16[40,2048]{1,0:T(8,128)(2,1)S(1)}, bf16[40,2048]{1,0:T(8,128)(2,1)S(1)}, u32[]{:S(2)}, u32[]{:S(2)}) %collective-permute-start.2) | collective-permute-done | bytes 163872 | tf_op jit(solution)/shard_map/ppermute | solution.py:231
  25.5 0.0 collective-permute-done.3.inner
  25.6 0.0 copy-start.1
  25.6 0.9 %copy-done.1 = bf16[4,2,8,2048]{3,2,1,0:T(8,128)(2,1)S(1)} copy-done((bf16[4,2,8,2048]{3,2,1,0:T(8,128)(2,1)S(1)}, bf16[4,2,8,2048]{3,2,1,0:T(8,128)(2,1)}, u32[]{:S(2)}) %copy-start.1) | copy-done | bytes 262168
  26.5 0.0 copy-start.2
  26.5 0.7 %copy-done.2 = s32[4]{0:T(128)S(1)} copy-done((s32[4]{0:T(128)S(1)}, s32[4]{0:T(128)}, u32[]{:S(2)}) %copy-start.2) | copy-done | bytes 40
  27.2 14.7 %windows.1 = (bf16[4,6,2,8,2048]{4,3,2,1,0:T(8,128)(2,1)}, bf16[4,6,8,2048]{3,2,1,0:T(8,128)(2,1)}) custom-call(s32[4]{0:T(128)S(1)} %copy-done.2, s32[4,2]{1,0:T(4,128)S(1)} %copy.6.looks, bf16[4,2,8,2048]{3,2,1,0:T(8,128)(2,1)S(1)} %copy-done.1, bf16[4,2,8,2048]{3,2,1,0:T(8,128)(2,1)S(1)} %collective-permute-done.next_1, ...), custom_call_target="tpu_custom_call" | custom-call | tf_op jit(solution)/shard_map/windows/pallas_call | solution.py:235
Async XLA Ops:
  0.6 16.9 %collective-permute-start = (bf16[4,2,8,2048]{3,2,1,0:T(8,128)(2,1)}, bf16[4,2,8,2048]{3,2,1,0:T(8,128)(2,1)S(1)}, u32[]{:S(2)}, u32[]{:S(2)}) collective-permute-start(bf16[4,2,8,2048]{3,2,1,0:T(8,128)(2,1)} %own.3), channel_id=1, source_target_pairs={{0,240},{16,0},{32,16},{48,32},{64,48},{80,64},{96,80},{112,96},{1... | collective-permute-start | bytes 786440 | tf_op jit(solution)/shard_map/ppermute | solution.py:203
  10.5 7.0 %collective-permute-start.1 = (bf16[2,2,8,2048]{3,2,1,0:T(8,128)(2,1)S(1)}, bf16[2,2,8,2048]{3,2,1,0:T(8,128)(2,1)S(1)}, u32[]{:S(2)}, u32[]{:S(2)}) collective-permute-start(bf16[2,2,8,2048]{3,2,1,0:T(8,128)(2,1)S(1)} %slice.3), channel_id=1, source_target_pairs={{0,224},{16,240},{32,0},{48,16},{64,32},{80,48},{96,64},{112,80},{... | collective-permute-start | bytes 393224 | tf_op jit(solution)/shard_map/ppermute | solution.py:203
  17.6 1.0 %copy-start = (bf16[4,2,8,2048]{3,2,1,0:T(8,128)(2,1)S(1)}, bf16[4,2,8,2048]{3,2,1,0:T(8,128)(2,1)}, u32[]{:S(2)}) copy-start(bf16[4,2,8,2048]{3,2,1,0:T(8,128)(2,1)} %own.3) | copy-start | bytes 786436
  19.7 5.8 %collective-permute-start.2 = (bf16[40,2048]{1,0:T(8,128)(2,1)S(1)}, bf16[40,2048]{1,0:T(8,128)(2,1)S(1)}, u32[]{:S(2)}, u32[]{:S(2)}) collective-permute-start(bf16[40,2048]{1,0:T(8,128)(2,1)S(1)} %get-tuple-element.6), channel_id=1, source_target_pairs={{15,0},{2,1},{1,2},{4,3},{3,4},{6,5},{5,6},{8,7},{7,8},{10,9},{9,1... | collective-permute-start | bytes 491528 | tf_op jit(solution)/shard_map/ppermute | solution.py:231
  22.5 3.0 %collective-permute-start.3 = (bf16[40,2048]{1,0:T(8,128)(2,1)S(1)}, bf16[40,2048]{1,0:T(8,128)(2,1)S(1)}, u32[]{:S(2)}, u32[]{:S(2)}) collective-permute-start(bf16[40,2048]{1,0:T(8,128)(2,1)S(1)} %get-tuple-element.7), channel_id=1, source_target_pairs={{1,0},{0,1},{3,2},{2,3},{5,4},{4,5},{7,6},{6,7},{9,8},{8,9},{11,10... | collective-permute-start | bytes 491528 | tf_op jit(solution)/shard_map/ppermute | solution.py:234
  25.6 1.0 %copy-start.1 = (bf16[4,2,8,2048]{3,2,1,0:T(8,128)(2,1)S(1)}, bf16[4,2,8,2048]{3,2,1,0:T(8,128)(2,1)}, u32[]{:S(2)}) copy-start(bf16[4,2,8,2048]{3,2,1,0:T(8,128)(2,1)} %own.3) | copy-start | bytes 786436
  26.5 0.7 %copy-start.2 = (s32[4]{0:T(128)S(1)}, s32[4]{0:T(128)}, u32[]{:S(2)}) copy-start(s32[4]{0:T(128)} %counts.1) | copy-start | bytes 52

commit v2 on v1

v2 whole, which is shorter than its diff:
```python
import jax
import jax.numpy as jnp
from jax import lax
from jax.experimental import pallas as pl
from jax.experimental.pallas import tpu as pltpu
from jax.sharding import PartitionSpec as P

MAXP = 6
ROWS = 8
HALO = 2
NEAR = 10
EDGE = 2 * NEAR
FIELDS = 160
WINDOW = 96
BLOCK = 256
PAD = 128
UNROLL_SUMS = 4
UNROLL_HALO = 4
UNROLL_COLS = 4
epsilon = 1e-06
tiny = 1.1754944e-38
F32 = jnp.float32
BF16 = jnp.bfloat16


def iota(shape, dim):
    return lax.broadcasted_iota(jnp.int32, shape, dim)


def place():
    row = lax.axis_index("rows")
    return row, lax.rem(row, 2), lax.axis_size("rows")


def setup_kernel(looks, counts, own, own_copy, main_weights, halo_weights, bands, factors):
    row, core, row_total = place()
    own_copy[...] = own[...]
    out_row = iota((8, FIELDS), 0)
    at = iota((8, FIELDS), 1)
    main_field = lax.shift_right_arithmetic(at, 3)
    main_distance = jnp.abs((at & 7) - out_row)

    halo_row = iota((8, 2 * WINDOW), 0)
    at = iota((8, 2 * WINDOW), 1)
    at = jnp.where(at >= WINDOW, at - WINDOW, at)
    inner = at >= 48
    group = lax.shift_right_arithmetic(jnp.where(inner, at - 48, at), 4)
    near = lax.shift_right_arithmetic(at, 1) & 7
    slot_ok = (near >= 1) & (near <= 6)
    power_field = jnp.where(near <= 6, 12 + near, 99)
    halo_field = jnp.where(group == 2, power_field, jnp.where(slot_ok, 6 * group + near - 1, 99))
    above = jnp.where(inner, core, 1 - core) == 1
    position = (at & 1) + jnp.where(above, -HALO, ROWS)
    open_edge = jnp.where(core == 0, row > 0, row < row_total - 1)
    halo_field = jnp.where(inner | open_edge, halo_field, 99)
    halo_distance = jnp.abs(position - halo_row)

    for a in range(4):
        for weights, distance, field in (
            (main_weights, main_distance, main_field),
            (halo_weights, halo_distance, halo_field),
        ):
            hit = distance <= looks[a, 0]
            for f in range(FIELDS // 16):
                pair = [jnp.where(hit & (field == 2 * f + i), 1.0, 0.0) for i in range(2)]
                weights[a, 16 * f : 16 * f + 16, :] = jnp.concatenate(pair, 0).astype(BF16)

    column = iota((384, BLOCK), 0)
    column = jnp.where(column < 320, column, column - 384)
    spread = jnp.abs(column - iota((384, BLOCK), 1))
    first_acq = lax.axis_index("tm") * 4
    acq_total = lax.axis_size("tm") * 4
    slot = iota((16, 128), 0)
    is_live = slot >= 8
    slot = slot & 7
    for a in range(4):
        bands[a] = jnp.where(spread <= looks[a, 1], 1.0, 0.0).astype(BF16)
        live = (slot < counts[a]) & (first_acq + a + slot + 1 < acq_total)
        area = (2 * looks[a, 0] + 1) * (2 * looks[a, 1] + 1)
        area = jnp.full((16, 128), area, jnp.int32).astype(F32)
        factors[a] = jnp.where(live, jnp.where(is_live, 1.0, 1.0 / area), 0.0)


def edges_kernel(own, next_1, next_2, outer, inner):
    row, core, _ = place()
    to = iota((2 * 2 * EDGE, 2 * NEAR * ROWS), 0)
    source = iota((2 * 2 * EDGE, 2 * NEAR * ROWS), 1)
    is_inner = to >= 2 * EDGE
    to = jnp.where(is_inner, to - 2 * EDGE, to)
    high = jnp.where(is_inner, 1 - core, core) == 1
    wanted = lax.shift_right_arithmetic(to, 1) * ROWS + (to & 1) + jnp.where(high, ROWS - HALO, 0)
    pick = jnp.where(source == wanted, 1.0, 0.0).astype(BF16)
    for n in range(own.shape[-1] // BLOCK):
        cols = slice(n * BLOCK, (n + 1) * BLOCK)
        parts = []
        for c in range(2):
            for ref in (own, next_1, next_2):
                for e in range(ref.shape[0]):
                    parts.append(ref[e, c, :, cols].astype(F32))
        data = jnp.concatenate(parts, 0).astype(BF16)
        picked = jnp.dot(pick, data, preferred_element_type=F32).astype(BF16)
        outer[:, cols] = picked[: 2 * EDGE]
        inner[:, cols] = picked[2 * EDGE :]


def halves(terms):
    high = terms.astype(BF16)
    return high, (terms - high.astype(F32)).astype(BF16)


def sums_kernel(own, next_1, next_2, main_weights, sums):
    near = [own.at[e] for e in range(4)] + [next_1.at[e] for e in range(4)]
    near += [next_2.at[e] for e in range(2)]

    def body(n, carry):
        cols = pl.ds(pl.multiple_of(n * BLOCK, BLOCK), BLOCK)
        images = [(ref[0, :, cols].astype(F32), ref[1, :, cols].astype(F32)) for ref in near]
        powers = [re * re + im * im for re, im in images]
        for a in range(4):
            own_re, own_im = images[a]
            partners = images[a + 1 : a + 1 + MAXP]
            fields = [own_re * re + own_im * im for re, im in partners]
            fields += [own_im * re - own_re * im for re, im in partners]
            fields += powers[a : a + 1 + MAXP] + [jnp.zeros((ROWS, BLOCK), F32)]
            high, low = halves(jnp.concatenate(fields, 0))
            total = jnp.dot(main_weights[a], high, preferred_element_type=F32)
            total = total + jnp.dot(main_weights[a], low, preferred_element_type=F32)
            sums[a, :, cols] = total
        return carry

    lax.fori_loop(0, sums.shape[-1] // BLOCK, body, 0, unroll=UNROLL_SUMS)


def repeated(tile, first):
    rows = iota(tile.shape, 0)
    kept = jnp.where((rows >= first) & (rows < first + 2), tile, 0.0)
    kept = kept + pltpu.roll(kept, 2, 0)
    return kept + pltpu.roll(kept, 4, 0)


def windows_kernel(
    outer, inner, halo_weights, bands, factors, sums,
    ifg_out, coh_out, edge_rows, rounded, ifg, coh, sems,
):
    cols_total = outer.shape[-1]
    blocks = cols_total // BLOCK
    rounded[:, :, :PAD] = jnp.zeros((2, FIELDS, PAD), BF16)
    rounded[:, :, PAD + cols_total :] = jnp.zeros((2, FIELDS, PAD), BF16)
    for h, ref in enumerate((outer, inner)):
        edge_rows[h, 2 * EDGE :, :] = jnp.zeros((8, cols_total), F32)
        edge_rows[h, : 2 * EDGE, :] = ref[...].astype(F32)

    def row_body(n, a):
        start = pl.multiple_of(n * BLOCK, BLOCK)
        cols = pl.ds(start, BLOCK)
        fields = []
        for h in range(2):
            mine = []
            for c in range(2):
                at = c * EDGE + 2 * a
                tile = edge_rows[h, at // 8 * 8 : at // 8 * 8 + 8, cols]
                mine.append(repeated(tile, at % 8))
            own_re, own_im = mine
            images = []
            for half in range(2):
                at = 2 * a + 8 * half
                images.append((edge_rows[h, at : at + 8, cols], edge_rows[h, at + EDGE : at + EDGE + 8, cols]))
            fields += [own_re * re + own_im * im for re, im in images]
            fields += [own_im * re - own_re * im for re, im in images]
            fields += [re * re + im * im for re, im in images]
        terms = jnp.concatenate(halves(jnp.concatenate(fields, 0)), 0)
        total = sums[a, :, cols] + jnp.dot(halo_weights[a], terms, preferred_element_type=F32)
        rounded[a % 2, :, pl.ds(pl.multiple_of(start + PAD, 128), BLOCK)] = total.astype(BF16)

    def col_body(n, a):
        start = pl.multiple_of(n * BLOCK, BLOCK)
        cols = pl.ds(start, BLOCK)
        inside = rounded[a % 2, :, pl.ds(pl.multiple_of(start + PAD, 128), BLOCK)]
        left = rounded[a % 2, :, pl.ds(start, PAD)]
        right = rounded[a % 2, :, pl.ds(pl.multiple_of(start + PAD + BLOCK, 128), PAD)]
        sides = jnp.where(iota((FIELDS, PAD), 1) < 64, right, left)
        boxed = jnp.dot(inside, bands[a, :BLOCK, :], preferred_element_type=F32)
        boxed = boxed + jnp.dot(sides, bands[a, BLOCK:, :], preferred_element_type=F32)
        own_power = boxed[96:104]
        for j in range(MAXP):
            re = boxed[8 * j : 8 * j + 8]
            im = boxed[48 + 8 * j : 56 + 8 * j]
            power = boxed[104 + 8 * j : 112 + 8 * j]
            scale = jnp.concatenate([factors[a, j : j + 1, :]] * 2, 1)
            live = jnp.concatenate([factors[a, 8 + j : 9 + j, :]] * 2, 1)
            ifg[a, j, 0, :, cols] = (re * scale).astype(BF16)
            ifg[a, j, 1, :, cols] = (im * scale).astype(BF16)
            square = re * re + im * im
            magnitude = square * lax.rsqrt(jnp.maximum(square, tiny))
            coherence = magnitude * lax.rsqrt(own_power * power + epsilon) * live
            coh[a, j, :, cols] = coherence.astype(BF16)

    def loop(body, a, unroll):
        lax.fori_loop(0, blocks, lambda n, carry: (body(n, a), carry)[1], 0, unroll=unroll)

    copies = []
    for a in range(4):
        loop(row_body, a, UNROLL_HALO)
        loop(col_body, a, UNROLL_COLS)
        for k, (scratch, out) in enumerate(((ifg, ifg_out), (coh, coh_out))):
            copy = pltpu.make_async_copy(scratch.at[a], out.at[a], sems.at[a, k])
            copy.start()
            copies.append(copy)
    for copy in copies:
        copy.wait()


VMEM = pl.BlockSpec(memory_space=pltpu.VMEM)
SMEM = pl.BlockSpec(memory_space=pltpu.SMEM)


def kernel(body, name, in_specs, out_specs, out_shape, flops, moved, scratch=(), limit=40):
    return pl.pallas_call(
        body,
        in_specs=in_specs,
        out_specs=out_specs,
        out_shape=[jax.ShapeDtypeStruct(*s) for s in out_shape],
        scratch_shapes=scratch,
        compiler_params=pltpu.CompilerParams(vmem_limit_bytes=limit * 2**20),
        cost_estimate=pl.CostEstimate(flops=flops, bytes_accessed=moved, transcendentals=0),
        name=name,
    )


def shifted(block, distance):
    count = lax.axis_size("tm")
    return lax.ppermute(block, "tm", [(i, (i - distance) % count) for i in range(count)])


def local(slc_stack, partner_count, look_sizes):
    cols = slc_stack.shape[-1]
    rows = lax.axis_size("rows")
    next_1 = shifted(slc_stack, 1)
    next_2 = shifted(slc_stack[:2], 2)
    own, main_weights, halo_weights, bands, factors = kernel(
        setup_kernel,
        "setup",
        [SMEM, SMEM, VMEM],
        [VMEM] * 5,
        [
            (slc_stack.shape, BF16),
            ((4, FIELDS, FIELDS), BF16),
            ((4, FIELDS, 2 * WINDOW), BF16),
            ((4, 384, BLOCK), BF16),
            ((4, 16, 128), F32),
        ],
        10**6,
        2 * 10**6,
    )(look_sizes, partner_count, slc_stack)
    outer, inner = kernel(
        edges_kernel, "edges", [VMEM] * 3, [VMEM] * 2, [((2 * EDGE, cols), BF16)] * 2, 10**6, 10**6
    )(own, next_1, next_2)
    outer = lax.ppermute(
        outer, "rows", [((i + 1 - 2 * (1 - i % 2)) % rows, i) for i in range(rows)]
    )
    inner = lax.ppermute(inner, "rows", [(i ^ 1, i) for i in range(rows)])
    (sums,) = kernel(
        sums_kernel,
        "sums",
        [VMEM] * 4,
        [VMEM],
        [((4, FIELDS, cols), F32)],
        4 * 10**9,
        6 * 10**6,
    )(own, next_1, next_2, main_weights)
    return kernel(
        windows_kernel,
        "windows",
        [VMEM] * 6,
        [pl.BlockSpec(memory_space=pl.ANY)] * 2,
        [((4, MAXP, 2, ROWS, cols), BF16), ((4, MAXP, ROWS, cols), BF16)],
        4 * 10**9,
        9 * 10**6,
        [
            pltpu.VMEM((2, 2 * EDGE + 8, cols), F32),
            pltpu.VMEM((2, FIELDS, cols + 2 * PAD), BF16),
            pltpu.VMEM((4, MAXP, 2, ROWS, cols), BF16),
            pltpu.VMEM((4, MAXP, ROWS, cols), BF16),
            pltpu.SemaphoreType.DMA((4, 2)),
        ],
    )(outer, inner, halo_weights, bands, factors, sums)


def solution(mesh):
    return jax.shard_map(
        local,
        mesh=mesh,
        in_specs=(P("tm", None, "rows", None), P("tm"), P("tm", None)),
        out_specs=(P("tm", None, None, "rows", None), P("tm", None, "rows", None)),
        check_vma=False,
    )
```

time: 42.3 us -> 30.6 us (0.72)
  Pallas kernels: 16.6 us -> 9.47 us
  waiting for transfers between devices: 7.26 us -> 3.71 us
  local copies, waits for them, and re-layouts: 4.27 us -> 3.31 us
    pallas_call x3 -> x4, Pallas kernels: 16.6 us -> 9.47 us  [the longest x1 6.5 us: local(): kernel(windows_kernel, 'windows', [VMEM] * 6, [pl.BlockSpec(memory_space=...]
    ppermute x2, waiting for transfers between devices: 6.24 us -> 3.01 us  [shifted(): lax.ppermute(block, 'tm', [(i, (i - distance) % count) for i in range(cou...]
    unnamed x7 -> x5, local copies, waits for them, and re-layouts: 3.32 us -> 2.37 us
  transfers between devices with their start and end apart: 4 -> 4, of which waited for: 2 -> 2; matrix products, arithmetic and copies ran while one was open for 4% -> 6% of each run, Pallas kernels for 2% -> 9%
where the time goes in v2:
time: 30.6 us; the launch traced here: 30.1 us
  starting transfers between devices  13 us (42%)
  Pallas kernels  9.47 us (31%)
  waiting for transfers between devices  3.71 us (12%)
  local copies, waits for them, and re-layouts  3.31 us (11%)
  between operations  0.66 us (2%)
    ppermute x2, starting transfers between devices, shifted(): lax.ppermute(block, 'tm', [(i, (i - distance) % count) for i in range(cou...  9.75 us
    pallas_call x1, Pallas kernels, local(): kernel(windows_kernel, 'windows', [VMEM] * 6, [pl.BlockSpec(memory_space=...  6.5 us
    ppermute x2, waiting for transfers between devices, shifted(): lax.ppermute(block, 'tm', [(i, (i - distance) % count) for i in range(cou...  3.01 us
    ppermute x1, starting transfers between devices, local(): lax.ppermute(outer, 'rows', [((i + 1 - 2 * (1 - i % 2)) % rows, i) for i...  2.81 us
    unnamed x5, local copies, waits for them, and re-layouts  2.37 us
    pallas_call x1, Pallas kernels, local(): kernel(sums_kernel, 'sums', [VMEM] * 4, [VMEM], [((4, FIELDS, cols), F32)...  1.87 us
    slice x1, local copies, waits for them, and re-layouts, local(): next_2 = shifted(slc_stack[:2], 2)  0.95 us
    pallas_call x1, Pallas kernels, local(): kernel(setup_kernel, 'setup', [SMEM, SMEM, VMEM], [VMEM] * 5, [(slc_stack...  0.86 us
  transfers between devices with their start and end apart: 4, of which 2 were waited for; matrix products, arithmetic and copies ran while one was open for 6% of the time, Pallas kernels for 9%

profile of v2, /device:TPU:1, one launch (start us, length us, event | category | flops | bytes accessed | tf_op | source)
XLA Modules:
  0.0 30.1 jit_solution(14736577575864328417)
XLA Ops:
  0.6 8.9 %collective-permute-start = (bf16[4,2,8,2048]{3,2,1,0:T(8,128)(2,1)}, bf16[4,2,8,2048]{3,2,1,0:T(8,128)(2,1)S(1)}, u32[]{:S(2)}, u32[]{:S(2)}) collective-permute-start(bf16[4,2,8,2048]{3,2,1,0:T(8,128)(2,1)} %own.1), channel_id=1, source_target_pairs={{0,240},{16,0},{32,16},{48,32},{64,48},{80,64},{96,80},{112,96},{1... | collective-permute-start | bytes 786440 | tf_op jit(solution)/shard_map/ppermute | solution.py:232
  9.6 0.9 %slice.3 = bf16[2,2,8,2048]{3,2,1,0:T(8,128)(2,1)S(1)} slice(bf16[4,2,8,2048]{3,2,1,0:T(8,128)(2,1)} %own.1), slice={[0:2], [0:2], [0:8], [0:2048]} | slice | bytes 262144 | tf_op jit(solution)/shard_map/slice | solution.py:239
  10.5 0.8 %collective-permute-start.1 = (bf16[2,2,8,2048]{3,2,1,0:T(8,128)(2,1)S(1)}, bf16[2,2,8,2048]{3,2,1,0:T(8,128)(2,1)S(1)}, u32[]{:S(2)}, u32[]{:S(2)}) collective-permute-start(bf16[2,2,8,2048]{3,2,1,0:T(8,128)(2,1)S(1)} %slice.3), channel_id=1, source_target_pairs={{0,224},{16,240},{32,0},{48,16},{64,32},{80,48},{96,64},{112,80},{... | collective-permute-start | bytes 393224 | tf_op jit(solution)/shard_map/ppermute | solution.py:232
  11.3 0.8 %copy.5.looks = s32[4,2]{1,0:T(4,128)S(1)} copy(s32[4,2]{0,1:T(2,128)} %param.5) | data formatting | bytes 64 | tf_op args[2]
  12.1 0.0 copy-start
  12.1 0.9 %copy-done = bf16[4,2,8,2048]{3,2,1,0:T(8,128)(2,1)S(1)} copy-done((bf16[4,2,8,2048]{3,2,1,0:T(8,128)(2,1)S(1)}, bf16[4,2,8,2048]{3,2,1,0:T(8,128)(2,1)}, u32[]{:S(2)}) %copy-start) | copy-done | bytes 262168
  13.0 0.0 copy-start.1
  13.0 0.7 %copy-done.1 = s32[4]{0:T(128)S(1)} copy-done((s32[4]{0:T(128)S(1)}, s32[4]{0:T(128)}, u32[]{:S(2)}) %copy-start.1) | copy-done | bytes 40
  13.7 0.9 %setup.1 = (bf16[4,2,8,2048]{3,2,1,0:T(8,128)(2,1)S(1)}, bf16[4,160,160]{2,1,0:T(8,128)(2,1)S(1)}, bf16[4,160,192]{2,1,0:T(8,128)(2,1)S(1)}, bf16[4,384,256]{2,1,0:T(8,128)(2,1)S(1)}, f32[4,16,128]{2,1,0:T(8,128)S(1)}) custom-call(s32[4,2]{1,0:T(4,128)S(1)} %copy.5.looks, s32[4]{0:T(128)S(1)} %copy-done.1, bf16[4,2,8,2048]{3,2,1,0:T(8,128)(2,1)S(1)} %copy-done), custom_call_target="tpu_custom_call" | custom-call | flops 1000000 | bytes 2000000 | tf_op jit(solution)/shard_map/setup/pallas_call | solution.py:240
  14.6 3.0 %collective-permute-done.1.next_2 = bf16[2,2,8,2048]{3,2,1,0:T(8,128)(2,1)S(1)} collective-permute-done((bf16[2,2,8,2048]{3,2,1,0:T(8,128)(2,1)S(1)}, bf16[2,2,8,2048]{3,2,1,0:T(8,128)(2,1)S(1)}, u32[]{:S(2)}, u32[]{:S(2)}) %collective-permute-start.1) | collective-permute-done | bytes 131104 | tf_op jit(solution)/shard_map/ppermute | solution.py:232
  17.6 0.0 collective-permute-done.next_1
  17.6 0.2 edges.1
  17.8 2.8 %collective-permute-start.2 = (bf16[40,2048]{1,0:T(8,128)(2,1)S(1)}, bf16[40,2048]{1,0:T(8,128)(2,1)S(1)}, u32[]{:S(2)}, u32[]{:S(2)}) collective-permute-start(bf16[40,2048]{1,0:T(8,128)(2,1)S(1)} %get-tuple-element.10), channel_id=1, source_target_pairs={{15,0},{2,1},{1,2},{4,3},{3,4},{6,5},{5,6},{8,7},{7,8},{10,9},{9,1... | collective-permute-start | bytes 491528 | tf_op jit(solution)/shard_map/ppermute | solution.py:258
  20.6 0.4 %collective-permute-start.3 = (bf16[40,2048]{1,0:T(8,128)(2,1)S(1)}, bf16[40,2048]{1,0:T(8,128)(2,1)S(1)}, u32[]{:S(2)}, u32[]{:S(2)}) collective-permute-start(bf16[40,2048]{1,0:T(8,128)(2,1)S(1)} %get-tuple-element.11), channel_id=1, source_target_pairs={{1,0},{0,1},{3,2},{2,3},{5,4},{4,5},{7,6},{6,7},{9,8},{8,9},{11,10... | collective-permute-start | bytes 491528 | tf_op jit(solution)/shard_map/ppermute | solution.py:261
  21.1 1.9 %sums.1 = f32[4,160,2048]{2,1,0:T(8,128)S(1)} custom-call(bf16[4,2,8,2048]{3,2,1,0:T(8,128)(2,1)S(1)} %get-tuple-element.9.own, bf16[4,2,8,2048]{3,2,1,0:T(8,128)(2,1)S(1)} %collective-permute-done.next_1, bf16[2,2,8,2048]{3,2,1,0:T(8,128)(2,1)S(1)} %collective-permute-done.1.next_2, bf16[4,160,160]{2,1,0:T(8,128)(2,1)S(1)} %get-tuple-element.15.main_weights), custom_call_target="tpu_custom_call" | custom-call | flops 4000000000 | bytes 6000000 | tf_op jit(solution)/shard_map/sums/pallas_call | solution.py:262
  22.9 0.7 %collective-permute-done.2.outer = bf16[40,2048]{1,0:T(8,128)(2,1)S(1)} collective-permute-done((bf16[40,2048]{1,0:T(8,128)(2,1)S(1)}, bf16[40,2048]{1,0:T(8,128)(2,1)S(1)}, u32[]{:S(2)}, u32[]{:S(2)}) %collective-permute-start.2) | collective-permute-done | bytes 163872 | tf_op jit(solution)/shard_map/ppermute | solution.py:258
  23.6 0.0 collective-permute-done.3.inner
  23.6 6.5 %windows.1 = (bf16[4,6,2,8,2048]{4,3,2,1,0:T(8,128)(2,1)}, bf16[4,6,8,2048]{3,2,1,0:T(8,128)(2,1)}) custom-call(bf16[40,2048]{1,0:T(8,128)(2,1)S(1)} %collective-permute-done.2.outer, bf16[40,2048]{1,0:T(8,128)(2,1)S(1)} %collective-permute-done.3.inner, bf16[4,160,192]{2,1,0:T(8,128)(2,1)S(1)} %get-tuple-element.12.halo_weights, ...), custom_call_target="tpu_custom_call" | custom-call | flops 4000000000 | bytes 9000000 | tf_op jit(solution)/shard_map/windows/pallas_call | solution.py:271
Async XLA Ops:
  0.6 16.9 %collective-permute-start = (bf16[4,2,8,2048]{3,2,1,0:T(8,128)(2,1)}, bf16[4,2,8,2048]{3,2,1,0:T(8,128)(2,1)S(1)}, u32[]{:S(2)}, u32[]{:S(2)}) collective-permute-start(bf16[4,2,8,2048]{3,2,1,0:T(8,128)(2,1)} %own.1), channel_id=1, source_target_pairs={{0,240},{16,0},{32,16},{48,32},{64,48},{80,64},{96,80},{112,96},{1... | collective-permute-start | bytes 786440 | tf_op jit(solution)/shard_map/ppermute | solution.py:232
  10.5 7.0 %collective-permute-start.1 = (bf16[2,2,8,2048]{3,2,1,0:T(8,128)(2,1)S(1)}, bf16[2,2,8,2048]{3,2,1,0:T(8,128)(2,1)S(1)}, u32[]{:S(2)}, u32[]{:S(2)}) collective-permute-start(bf16[2,2,8,2048]{3,2,1,0:T(8,128)(2,1)S(1)} %slice.3), channel_id=1, source_target_pairs={{0,224},{16,240},{32,0},{48,16},{64,32},{80,48},{96,64},{112,80},{... | collective-permute-start | bytes 393224 | tf_op jit(solution)/shard_map/ppermute | solution.py:232
  12.1 0.9 %copy-start = (bf16[4,2,8,2048]{3,2,1,0:T(8,128)(2,1)S(1)}, bf16[4,2,8,2048]{3,2,1,0:T(8,128)(2,1)}, u32[]{:S(2)}) copy-start(bf16[4,2,8,2048]{3,2,1,0:T(8,128)(2,1)} %own.1) | copy-start | bytes 786436
  13.0 0.7 %copy-start.1 = (s32[4]{0:T(128)S(1)}, s32[4]{0:T(128)}, u32[]{:S(2)}) copy-start(s32[4]{0:T(128)} %counts.1) | copy-start | bytes 52
  17.8 5.8 %collective-permute-start.2 = (bf16[40,2048]{1,0:T(8,128)(2,1)S(1)}, bf16[40,2048]{1,0:T(8,128)(2,1)S(1)}, u32[]{:S(2)}, u32[]{:S(2)}) collective-permute-start(bf16[40,2048]{1,0:T(8,128)(2,1)S(1)} %get-tuple-element.10), channel_id=1, source_target_pairs={{15,0},{2,1},{1,2},{4,3},{3,4},{6,5},{5,6},{8,7},{7,8},{10,9},{9,1... | collective-permute-start | bytes 491528 | tf_op jit(solution)/shard_map/ppermute | solution.py:258
  20.6 3.0 %collective-permute-start.3 = (bf16[40,2048]{1,0:T(8,128)(2,1)S(1)}, bf16[40,2048]{1,0:T(8,128)(2,1)S(1)}, u32[]{:S(2)}, u32[]{:S(2)}) collective-permute-start(bf16[40,2048]{1,0:T(8,128)(2,1)S(1)} %get-tuple-element.11), channel_id=1, source_target_pairs={{1,0},{0,1},{3,2},{2,3},{5,4},{4,5},{7,6},{6,7},{9,8},{8,9},{11,10... | collective-permute-start | bytes 491528 | tf_op jit(solution)/shard_map/ppermute | solution.py:261

commit v3 on v2

--- a/solution.py
+++ b/solution.py
@@ -9,14 +9,14 @@
 ROWS = 8
 HALO = 2
 NEAR = 10
-EDGE = 2 * NEAR
+EDGE = 24
 FIELDS = 160
 WINDOW = 96
 BLOCK = 256
 PAD = 128
-UNROLL_SUMS = 4
-UNROLL_HALO = 4
-UNROLL_COLS = 4
+UNROLL_SUMS = 8
+UNROLL_HALO = 8
+UNROLL_COLS = 8
 epsilon = 1e-06
 tiny = 1.1754944e-38
 F32 = jnp.float32
@@ -81,26 +81,45 @@
         factors[a] = jnp.where(live, jnp.where(is_live, 1.0, 1.0 / area), 0.0)
 
 
-def edges_kernel(own, next_1, next_2, outer, inner):
-    row, core, _ = place()
-    to = iota((2 * 2 * EDGE, 2 * NEAR * ROWS), 0)
-    source = iota((2 * 2 * EDGE, 2 * NEAR * ROWS), 1)
-    is_inner = to >= 2 * EDGE
-    to = jnp.where(is_inner, to - 2 * EDGE, to)
-    high = jnp.where(is_inner, 1 - core, core) == 1
-    wanted = lax.shift_right_arithmetic(to, 1) * ROWS + (to & 1) + jnp.where(high, ROWS - HALO, 0)
-    pick = jnp.where(source == wanted, 1.0, 0.0).astype(BF16)
+def picked_edges(refs, wanted, cols):
+    parts = []
+    for ref in refs:
+        for e in range(ref.shape[0]):
+            parts += [ref[e, c, :, cols].astype(F32) for c in range(2)]
+    data = jnp.concatenate(parts, 0).astype(BF16)
+    pick = jnp.where(iota((wanted.shape[0], data.shape[0]), 1) == wanted, 1.0, 0.0)
+    return jnp.dot(pick.astype(BF16), data, preferred_element_type=F32).astype(BF16)
+
+
+def own_edges_kernel(own, first_two, outer, inner, outer_two):
+    core = place()[1]
+    first_two[...] = own[:2]
+    to = iota((40, 64), 0)
+    at = to & 15
+    two = jnp.where(to >= 32, 1, 0)
+    image = jnp.where(two == 1, lax.shift_right_arithmetic(at, 1) & 1, lax.shift_right_arithmetic(at, 1) & 3)
+    component = jnp.where(two == 1, lax.shift_right_arithmetic(at, 2), lax.shift_right_arithmetic(at, 3))
+    high = jnp.where((to >= 16) & (to < 32), 1 - core, core) == 1
+    wanted = (2 * image + component) * ROWS + (at & 1) + jnp.where(high, ROWS - HALO, 0)
     for n in range(own.shape[-1] // BLOCK):
         cols = slice(n * BLOCK, (n + 1) * BLOCK)
-        parts = []
-        for c in range(2):
-            for ref in (own, next_1, next_2):
-                for e in range(ref.shape[0]):
-                    parts.append(ref[e, c, :, cols].astype(F32))
-        data = jnp.concatenate(parts, 0).astype(BF16)
-        picked = jnp.dot(pick, data, preferred_element_type=F32).astype(BF16)
-        outer[:, cols] = picked[: 2 * EDGE]
-        inner[:, cols] = picked[2 * EDGE :]
+        edges = picked_edges((own,), wanted, cols)
+        outer[:, cols] = edges[:16]
+        inner[:, cols] = edges[16:32]
+        outer_two[:, cols] = edges[32:]
+
+
+def inner_edges_kernel(next_1, next_2, inner):
+    core = place()[1]
+    to = iota((24, 96), 0)
+    at = to & 15
+    two = to >= 16
+    image = jnp.where(two, 4 + (lax.shift_right_arithmetic(at, 1) & 1), lax.shift_right_arithmetic(at, 1) & 3)
+    component = jnp.where(two, lax.shift_right_arithmetic(at, 2), lax.shift_right_arithmetic(at, 3))
+    wanted = (2 * image + component) * ROWS + (at & 1) + jnp.where(core == 0, ROWS - HALO, 0)
+    for n in range(next_1.shape[-1] // BLOCK):
+        cols = slice(n * BLOCK, (n + 1) * BLOCK)
+        inner[:, cols] = picked_edges((next_1, next_2), wanted, cols)
 
 
 def halves(terms):
@@ -138,17 +157,28 @@
     return kept + pltpu.roll(kept, 4, 0)
 
 
+def fill_edges(edge_rows, own, next_1, next_2):
+    for c in range(2):
+        edge_rows[c * EDGE : c * EDGE + 8, :] = own[8 * c : 8 * c + 8]
+        edge_rows[c * EDGE + 8 : c * EDGE + 16, :] = next_1[8 * c : 8 * c + 8]
+        last = pltpu.roll(next_2, 4, 0) if c else next_2
+        last = jnp.where(iota(last.shape, 0) < 4, last, 0.0)
+        edge_rows[c * EDGE + 16 : c * EDGE + 24, :] = last
+
+
 def windows_kernel(
-    outer, inner, halo_weights, bands, factors, sums,
+    own_outer, outer_1, outer_2, own_inner, inner, halo_weights, bands, factors, sums,
     ifg_out, coh_out, edge_rows, rounded, ifg, coh, sems,
 ):
-    cols_total = outer.shape[-1]
+    cols_total = inner.shape[-1]
     blocks = cols_total // BLOCK
     rounded[:, :, :PAD] = jnp.zeros((2, FIELDS, PAD), BF16)
     rounded[:, :, PAD + cols_total :] = jnp.zeros((2, FIELDS, PAD), BF16)
-    for h, ref in enumerate((outer, inner)):
-        edge_rows[h, 2 * EDGE :, :] = jnp.zeros((8, cols_total), F32)
-        edge_rows[h, : 2 * EDGE, :] = ref[...].astype(F32)
+    arrived = inner[...].astype(F32)
+    fill_edges(edge_rows.at[1], own_inner[...].astype(F32), arrived[:16], arrived[16:])
+    fill_edges(
+        edge_rows.at[0], own_outer[...].astype(F32), outer_1[...].astype(F32), outer_2[...].astype(F32)
+    )
 
     def row_body(n, a):
         start = pl.multiple_of(n * BLOCK, BLOCK)
@@ -227,16 +257,45 @@
     )
 
 
-def shifted(block, distance):
-    count = lax.axis_size("tm")
-    return lax.ppermute(block, "tm", [(i, (i - distance) % count) for i in range(count)])
+def moved(block, distance, partner):
+    count, rows = lax.axis_size("tm"), lax.axis_size("rows")
+    pairs = [
+        ((t + distance) % count * rows + partner(r, rows), t * rows + r)
+        for t in range(count)
+        for r in range(rows)
+    ]
+    return lax.ppermute(block, ("tm", "rows"), pairs)
+
+
+def same(row, rows):
+    return row
+
+
+def across(row, rows):
+    return (row + 1 if row % 2 else row - 1) % rows
+
+
+def sibling(row, rows):
+    return row ^ 1
 
 
 def local(slc_stack, partner_count, look_sizes):
     cols = slc_stack.shape[-1]
-    rows = lax.axis_size("rows")
-    next_1 = shifted(slc_stack, 1)
-    next_2 = shifted(slc_stack[:2], 2)
+    next_1 = moved(slc_stack, 1, same)
+    first_two, outer, inner, outer_two = kernel(
+        own_edges_kernel,
+        "own_edges",
+        [VMEM],
+        [VMEM] * 4,
+        [((2,) + slc_stack.shape[1:], BF16), ((16, cols), BF16), ((16, cols), BF16), ((8, cols), BF16)],
+        10**6,
+        10**6,
+    )(slc_stack)
+    next_2 = moved(first_two, 2, same)
+    outer_1 = moved(outer, 1, across)
+    outer_2 = moved(outer_two, 2, across)
+    own_outer = moved(outer, 0, across)
+    own_inner = moved(inner, 0, sibling)
     own, main_weights, halo_weights, bands, factors = kernel(
         setup_kernel,
         "setup",
@@ -252,13 +311,10 @@
         10**6,
         2 * 10**6,
     )(look_sizes, partner_count, slc_stack)
-    outer, inner = kernel(
-        edges_kernel, "edges", [VMEM] * 3, [VMEM] * 2, [((2 * EDGE, cols), BF16)] * 2, 10**6, 10**6
-    )(own, next_1, next_2)
-    outer = lax.ppermute(
-        outer, "rows", [((i + 1 - 2 * (1 - i % 2)) % rows, i) for i in range(rows)]
-    )
-    inner = lax.ppermute(inner, "rows", [(i ^ 1, i) for i in range(rows)])
+    (next_inner,) = kernel(
+        inner_edges_kernel, "inner_edges", [VMEM] * 2, [VMEM], [((24, cols), BF16)], 10**6, 10**6
+    )(next_1, next_2)
+    next_inner = moved(next_inner, 0, sibling)
     (sums,) = kernel(
         sums_kernel,
         "sums",
@@ -271,19 +327,19 @@
     return kernel(
         windows_kernel,
         "windows",
-        [VMEM] * 6,
+        [VMEM] * 9,
         [pl.BlockSpec(memory_space=pl.ANY)] * 2,
         [((4, MAXP, 2, ROWS, cols), BF16), ((4, MAXP, ROWS, cols), BF16)],
         4 * 10**9,
         9 * 10**6,
         [
-            pltpu.VMEM((2, 2 * EDGE + 8, cols), F32),
+            pltpu.VMEM((2, 2 * EDGE, cols), F32),
             pltpu.VMEM((2, FIELDS, cols + 2 * PAD), BF16),
             pltpu.VMEM((4, MAXP, 2, ROWS, cols), BF16),
             pltpu.VMEM((4, MAXP, ROWS, cols), BF16),
             pltpu.SemaphoreType.DMA((4, 2)),
         ],
-    )(outer, inner, halo_weights, bands, factors, sums)
+    )(own_outer, outer_1, outer_2, own_inner, next_inner, halo_weights, bands, factors, sums)
 
 
 def solution(mesh):

time: 30.6 us -> 29.3 us (0.958)
  starting transfers between devices: 13 us -> 17.9 us
  waiting for transfers between devices: 3.71 us -> 0.02 us
  Pallas kernels: 9.47 us -> 7.1 us
    ppermute x4 -> x7, starting transfers between devices: 13 us -> 17.9 us  [moved(): return lax.ppermute(block, ('tm', 'rows'), pairs)]
    ppermute x4 -> x7, waiting for transfers between devices: 3.71 us -> 0.02 us  [moved(): return lax.ppermute(block, ('tm', 'rows'), pairs)]
    pallas_call x2 -> x3, Pallas kernels: 6.75 us -> 4.63 us  [the longest x1 4.27 us: local(): kernel(windows_kernel, 'windows', [VMEM] * 9, [pl.BlockSpec(memory_space=...]
    unnamed x5 -> x7, local copies, waits for them, and re-layouts: 2.37 us -> 3.35 us
    slice x1 -> x0, local copies, waits for them, and re-layouts: 0.95 us -> none  [local(): next_2 = shifted(slc_stack[:2], 2)]
  transfers between devices with their start and end apart: 4 -> 7, of which waited for: 2 -> 0; matrix products, arithmetic and copies ran while one was open for 6% -> 3% of each run, Pallas kernels for 9% -> 10%
where the time goes in v3:
time: 29.3 us; the launch traced here: 29.1 us
  starting transfers between devices  17.9 us (61%)
  Pallas kernels  7.1 us (24%)
  local copies, waits for them, and re-layouts  3.35 us (11%)
  between operations  0.71 us (2%)
    ppermute x7, starting transfers between devices, moved(): return lax.ppermute(block, ('tm', 'rows'), pairs)  17.9 us
    pallas_call x1, Pallas kernels, local(): kernel(windows_kernel, 'windows', [VMEM] * 9, [pl.BlockSpec(memory_space=...  4.27 us
    unnamed x7, local copies, waits for them, and re-layouts  3.35 us
    pallas_call x1, Pallas kernels, local(): kernel(sums_kernel, 'sums', [VMEM] * 4, [VMEM], [((4, FIELDS, cols), F32)...  1.61 us
    pallas_call x1, Pallas kernels, local(): kernel(setup_kernel, 'setup', [SMEM, SMEM, VMEM], [VMEM] * 5, [(slc_stack...  0.86 us
  transfers between devices with their start and end apart: 7, of which 0 were waited for; matrix products, arithmetic and copies ran while one was open for 3% of the time, Pallas kernels for 10%

profile of v3, /device:TPU:1, one launch (start us, length us, event | category | flops | bytes accessed | tf_op | source)
XLA Modules:
  0.0 29.1 jit_solution(5072059204651219197)
XLA Ops:
  0.6 8.9 %collective-permute-start.4 = (bf16[4,2,8,2048]{3,2,1,0:T(8,128)(2,1)}, bf16[4,2,8,2048]{3,2,1,0:T(8,128)(2,1)S(1)}, u32[]{:S(2)}, u32[]{:S(2)}) collective-permute-start(bf16[4,2,8,2048]{3,2,1,0:T(8,128)(2,1)} %own.3), channel_id=1, source_target_pairs={{16,0},{17,1},{18,2},{19,3},{20,4},{21,5},{22,6},{23,7},{24,8},{25... | collective-permute-start | bytes 786440 | tf_op jit(solution)/shard_map/ppermute | solution.py:267
  9.6 0.0 copy-start
  9.6 1.0 %copy-done = bf16[4,2,8,2048]{3,2,1,0:T(8,128)(2,1)S(1)} copy-done((bf16[4,2,8,2048]{3,2,1,0:T(8,128)(2,1)S(1)}, bf16[4,2,8,2048]{3,2,1,0:T(8,128)(2,1)}, u32[]{:S(2)}) %copy-start) | copy-done | bytes 262168
  10.6 0.2 own_edges.1
  10.7 0.8 %collective-permute-start.5 = (bf16[2,2,8,2048]{3,2,1,0:T(8,128)(2,1)S(1)}, bf16[2,2,8,2048]{3,2,1,0:T(8,128)(2,1)S(1)}, u32[]{:S(2)}, u32[]{:S(2)}) collective-permute-start(bf16[2,2,8,2048]{3,2,1,0:T(8,128)(2,1)S(1)} %get-tuple-element.14), channel_id=1, source_target_pairs={{32,0},{33,1},{34,2},{35,3},{36,4},{37,5},{38,6},{39,7},{40,8},{41... | collective-permute-start | bytes 393224 | tf_op jit(solution)/shard_map/ppermute | solution.py:267
  11.6 2.4 %collective-permute-start.1 = (bf16[16,2048]{1,0:T(8,128)(2,1)S(1)}, bf16[16,2048]{1,0:T(8,128)(2,1)S(1)}, u32[]{:S(2)}, u32[]{:S(2)}) collective-permute-start(bf16[16,2048]{1,0:T(8,128)(2,1)S(1)} %get-tuple-element.11), channel_id=1, source_target_pairs={{31,0},{18,1},{17,2},{20,3},{19,4},{22,5},{21,6},{24,7},{23,8},{26... | collective-permute-start | bytes 196616 | tf_op jit(solution)/shard_map/ppermute | solution.py:267
  13.9 0.1 collective-permute-start
  14.0 2.1 %collective-permute-start.2 = (bf16[8,2048]{1,0:T(8,128)(2,1)S(1)}, bf16[8,2048]{1,0:T(8,128)(2,1)S(1)}, u32[]{:S(2)}, u32[]{:S(2)}) collective-permute-start(bf16[8,2048]{1,0:T(8,128)(2,1)S(1)} %get-tuple-element.12), channel_id=1, source_target_pairs={{47,0},{34,1},{33,2},{36,3},{35,4},{38,5},{37,6},{40,7},{39,8},{42... | collective-permute-start | bytes 98312 | tf_op jit(solution)/shard_map/ppermute | solution.py:267
  16.1 0.8 %copy.5.looks = s32[4,2]{1,0:T(4,128)S(1)} copy(s32[4,2]{0,1:T(2,128)} %param.5) | data formatting | bytes 64 | tf_op args[2]
  16.9 0.0 copy-start.1
  16.9 0.9 %copy-done.1 = bf16[4,2,8,2048]{3,2,1,0:T(8,128)(2,1)S(1)} copy-done((bf16[4,2,8,2048]{3,2,1,0:T(8,128)(2,1)S(1)}, bf16[4,2,8,2048]{3,2,1,0:T(8,128)(2,1)}, u32[]{:S(2)}) %copy-start.1) | copy-done | bytes 262168
  17.8 0.0 copy-start.2
  17.8 0.7 %copy-done.2 = s32[4]{0:T(128)S(1)} copy-done((s32[4]{0:T(128)S(1)}, s32[4]{0:T(128)}, u32[]{:S(2)}) %copy-start.2) | copy-done | bytes 40
  18.5 0.9 %setup.1 = (bf16[4,2,8,2048]{3,2,1,0:T(8,128)(2,1)S(1)}, bf16[4,160,160]{2,1,0:T(8,128)(2,1)S(1)}, bf16[4,160,192]{2,1,0:T(8,128)(2,1)S(1)}, bf16[4,384,256]{2,1,0:T(8,128)(2,1)S(1)}, f32[4,16,128]{2,1,0:T(8,128)S(1)}) custom-call(s32[4,2]{1,0:T(4,128)S(1)} %copy.5.looks, s32[4]{0:T(128)S(1)} %copy-done.2, bf16[4,2,8,2048]{3,2,1,0:T(8,128)(2,1)S(1)} %copy-done.1), custom_call_target="tpu_custom_call" | custom-call | flops 1000000 | bytes 2000000 | tf_op jit(solution)/shard_map/setup/pallas_call | solution.py:299
  19.3 0.0 collective-permute-done.5.next_2
  19.3 3.5 %collective-permute-start.3 = (bf16[16,2048]{1,0:T(8,128)(2,1)S(1)}, bf16[16,2048]{1,0:T(8,128)(2,1)S(1)}, u32[]{:S(2)}, u32[]{:S(2)}) collective-permute-start(bf16[16,2048]{1,0:T(8,128)(2,1)S(1)} %get-tuple-element.13), channel_id=1, source_target_pairs={{1,0},{0,1},{3,2},{2,3},{5,4},{4,5},{7,6},{6,7},{9,8},{8,9},{11,10... | collective-permute-start | bytes 196616 | tf_op jit(solution)/shard_map/ppermute | solution.py:267
  22.9 0.0 collective-permute-done.4.next_1
  22.9 0.2 inner_edges.1
  23.1 0.1 collective-permute-start.6
  23.2 1.6 %sums.1 = f32[4,160,2048]{2,1,0:T(8,128)S(1)} custom-call(bf16[4,2,8,2048]{3,2,1,0:T(8,128)(2,1)S(1)} %get-tuple-element.18.own, bf16[4,2,8,2048]{3,2,1,0:T(8,128)(2,1)S(1)} %collective-permute-done.4.next_1, bf16[2,2,8,2048]{3,2,1,0:T(8,128)(2,1)S(1)} %collective-permute-done.5.next_2, bf16[4,160,160]{2,1,0:T(8,128)(2,1)S(1)} %get-tuple-element.19.main_weights), custom_call_target="tpu_custom_call" | custom-call | flops 4000000000 | bytes 6000000 | tf_op jit(solution)/shard_map/sums/pallas_call | solution.py:318
  24.8 0.0 collective-permute-done.2.outer_2
  24.8 0.0 collective-permute-done.3.own_inner
  24.8 0.0 collective-permute-done.1.outer_1
  24.8 0.0 collective-permute-done.own_outer
  24.8 0.0 collective-permute-done.6.inner
  24.9 4.3 %windows.1 = (bf16[4,6,2,8,2048]{4,3,2,1,0:T(8,128)(2,1)}, bf16[4,6,8,2048]{3,2,1,0:T(8,128)(2,1)}) custom-call(bf16[16,2048]{1,0:T(8,128)(2,1)S(1)} %collective-permute-done.own_outer, bf16[16,2048]{1,0:T(8,128)(2,1)S(1)} %collective-permute-done.1.outer_1, bf16[8,2048]{1,0:T(8,128)(2,1)S(1)} %collective-permute-done.2.outer_2, ...), custom_call_target="tpu_custom_call" | custom-call | flops 4000000000 | bytes 9000000 | tf_op jit(solution)/shard_map/windows/pallas_call | solution.py:327
Async XLA Ops:
  0.6 22.3 %collective-permute-start.4 = (bf16[4,2,8,2048]{3,2,1,0:T(8,128)(2,1)}, bf16[4,2,8,2048]{3,2,1,0:T(8,128)(2,1)S(1)}, u32[]{:S(2)}, u32[]{:S(2)}) collective-permute-start(bf16[4,2,8,2048]{3,2,1,0:T(8,128)(2,1)} %own.3), channel_id=1, source_target_pairs={{16,0},{17,1},{18,2},{19,3},{20,4},{21,5},{22,6},{23,7},{24,8},{25... | collective-permute-start | bytes 786440 | tf_op jit(solution)/shard_map/ppermute | solution.py:267
  9.6 1.0 %copy-start = (bf16[4,2,8,2048]{3,2,1,0:T(8,128)(2,1)S(1)}, bf16[4,2,8,2048]{3,2,1,0:T(8,128)(2,1)}, u32[]{:S(2)}) copy-start(bf16[4,2,8,2048]{3,2,1,0:T(8,128)(2,1)} %own.3) | copy-start | bytes 786436
  10.7 8.6 %collective-permute-start.5 = (bf16[2,2,8,2048]{3,2,1,0:T(8,128)(2,1)S(1)}, bf16[2,2,8,2048]{3,2,1,0:T(8,128)(2,1)S(1)}, u32[]{:S(2)}, u32[]{:S(2)}) collective-permute-start(bf16[2,2,8,2048]{3,2,1,0:T(8,128)(2,1)S(1)} %get-tuple-element.14), channel_id=1, source_target_pairs={{32,0},{33,1},{34,2},{35,3},{36,4},{37,5},{38,6},{39,7},{40,8},{41... | collective-permute-start | bytes 393224 | tf_op jit(solution)/shard_map/ppermute | solution.py:267
  11.6 13.3 %collective-permute-start.1 = (bf16[16,2048]{1,0:T(8,128)(2,1)S(1)}, bf16[16,2048]{1,0:T(8,128)(2,1)S(1)}, u32[]{:S(2)}, u32[]{:S(2)}) collective-permute-start(bf16[16,2048]{1,0:T(8,128)(2,1)S(1)} %get-tuple-element.11), channel_id=1, source_target_pairs={{31,0},{18,1},{17,2},{20,3},{19,4},{22,5},{21,6},{24,7},{23,8},{26... | collective-permute-start | bytes 196616 | tf_op jit(solution)/shard_map/ppermute | solution.py:267
  13.9 10.9 %collective-permute-start = (bf16[16,2048]{1,0:T(8,128)(2,1)S(1)}, bf16[16,2048]{1,0:T(8,128)(2,1)S(1)}, u32[]{:S(2)}, u32[]{:S(2)}) collective-permute-start(bf16[16,2048]{1,0:T(8,128)(2,1)S(1)} %get-tuple-element.11), channel_id=1, source_target_pairs={{15,0},{2,1},{1,2},{4,3},{3,4},{6,5},{5,6},{8,7},{7,8},{10,9},{9,1... | collective-permute-start | bytes 196616 | tf_op jit(solution)/shard_map/ppermute | solution.py:267
  14.0 10.8 %collective-permute-start.2 = (bf16[8,2048]{1,0:T(8,128)(2,1)S(1)}, bf16[8,2048]{1,0:T(8,128)(2,1)S(1)}, u32[]{:S(2)}, u32[]{:S(2)}) collective-permute-start(bf16[8,2048]{1,0:T(8,128)(2,1)S(1)} %get-tuple-element.12), channel_id=1, source_target_pairs={{47,0},{34,1},{33,2},{36,3},{35,4},{38,5},{37,6},{40,7},{39,8},{42... | collective-permute-start | bytes 98312 | tf_op jit(solution)/shard_map/ppermute | solution.py:267
  16.9 0.9 %copy-start.1 = (bf16[4,2,8,2048]{3,2,1,0:T(8,128)(2,1)S(1)}, bf16[4,2,8,2048]{3,2,1,0:T(8,128)(2,1)}, u32[]{:S(2)}) copy-start(bf16[4,2,8,2048]{3,2,1,0:T(8,128)(2,1)} %own.3) | copy-start | bytes 786436
  17.8 0.7 %copy-start.2 = (s32[4]{0:T(128)S(1)}, s32[4]{0:T(128)}, u32[]{:S(2)}) copy-start(s32[4]{0:T(128)} %counts.1) | copy-start | bytes 52
  19.3 5.5 %collective-permute-start.3 = (bf16[16,2048]{1,0:T(8,128)(2,1)S(1)}, bf16[16,2048]{1,0:T(8,128)(2,1)S(1)}, u32[]{:S(2)}, u32[]{:S(2)}) collective-permute-start(bf16[16,2048]{1,0:T(8,128)(2,1)S(1)} %get-tuple-element.13), channel_id=1, source_target_pairs={{1,0},{0,1},{3,2},{2,3},{5,4},{4,5},{7,6},{6,7},{9,8},{8,9},{11,10... | collective-permute-start | bytes 196616 | tf_op jit(solution)/shard_map/ppermute | solution.py:267
  23.1 1.8 %collective-permute-start.6 = (bf16[24,2048]{1,0:T(8,128)(2,1)S(1)}, bf16[24,2048]{1,0:T(8,128)(2,1)S(1)}, u32[]{:S(2)}, u32[]{:S(2)}) collective-permute-start(bf16[24,2048]{1,0:T(8,128)(2,1)S(1)} %inner_edges.1), channel_id=1, source_target_pairs={{1,0},{0,1},{3,2},{2,3},{5,4},{4,5},{7,6},{6,7},{9,8},{8,9},{11,10... | collective-permute-start | bytes 294920 | tf_op jit(solution)/shard_map/ppermute | solution.py:267

commit v4 on v3

v4 whole, which is shorter than its diff:
```python
import functools

import jax
import jax.numpy as jnp
from jax import lax
from jax.experimental import pallas as pl
from jax.experimental.pallas import tpu as pltpu
from jax.sharding import PartitionSpec as P

MAXP = 6
ROWS = 8
HALO = 2
NEAR = 10
EDGE = 24
FIELDS = 160
WINDOW = 96
BLOCK = 256
PAD = 128
UNROLL_SUMS = 8
UNROLL_HALO = 8
UNROLL_COLS = 8
epsilon = 1e-06
tiny = 1.1754944e-38
F32 = jnp.float32
BF16 = jnp.bfloat16


def iota(shape, dim):
    return lax.broadcasted_iota(jnp.int32, shape, dim)


def place():
    row = lax.axis_index("rows")
    return row, lax.rem(row, 2), lax.axis_size("rows")


def setup_kernel(packed, after, main_weights, halo_weights, bands, factors):
    row, core, row_total = place()
    numbers = [packed[:, a : a + 1] for a in range(4)]
    looks = [(n & 15, lax.shift_right_arithmetic(n, 4) & 15) for n in numbers]
    counts = [lax.shift_right_arithmetic(n, 8) for n in numbers]
    out_row = iota((8, FIELDS), 0)
    at = iota((8, FIELDS), 1)
    main_field = lax.shift_right_arithmetic(at, 3)
    main_distance = jnp.abs((at & 7) - out_row)

    halo_row = iota((8, 2 * WINDOW), 0)
    at = iota((8, 2 * WINDOW), 1)
    at = jnp.where(at >= WINDOW, at - WINDOW, at)
    inner = at >= 48
    group = lax.shift_right_arithmetic(jnp.where(inner, at - 48, at), 4)
    near = lax.shift_right_arithmetic(at, 1) & 7
    slot_ok = (near >= 1) & (near <= 6)
    power_field = jnp.where(near <= 6, 12 + near, 99)
    halo_field = jnp.where(group == 2, power_field, jnp.where(slot_ok, 6 * group + near - 1, 99))
    above = jnp.where(inner, core, 1 - core) == 1
    position = (at & 1) + jnp.where(above, -HALO, ROWS)
    open_edge = jnp.where(core == 0, row > 0, row < row_total - 1)
    halo_field = jnp.where(inner | open_edge, halo_field, 99)
    halo_distance = jnp.abs(position - halo_row)

    for a in range(4):
        for weights, distance, field in (
            (main_weights, main_distance, main_field),
            (halo_weights, halo_distance, halo_field),
        ):
            hit = distance <= looks[a][0]
            for f in range(FIELDS // 16):
                pair = [jnp.where(hit & (field == 2 * f + i), 1.0, 0.0) for i in range(2)]
                weights[a, 16 * f : 16 * f + 16, :] = jnp.concatenate(pair, 0).astype(BF16)

    column = iota((384, BLOCK), 0)
    column = jnp.where(column < 320, column, column - 384)
    spread = jnp.abs(column - iota((384, BLOCK), 1))
    first_acq = lax.axis_index("tm") * 4
    acq_total = lax.axis_size("tm") * 4
    slot = iota((16, 128), 0)
    is_live = slot >= 8
    slot = slot & 7
    for a in range(4):
        bands[a] = jnp.where(spread <= looks[a][1], 1.0, 0.0).astype(BF16)
        live = (slot < counts[a]) & (first_acq + a + slot + 1 < acq_total)
        area = (2 * looks[a][0] + 1) * (2 * looks[a][1] + 1)
        area = jnp.broadcast_to(area, (16, 128)).astype(F32)
        factors[a] = jnp.where(live, jnp.where(is_live, 1.0, 1.0 / area), 0.0)


def picked_edges(refs, wanted, cols):
    parts = []
    for ref in refs:
        for e in range(ref.shape[0]):
            parts += [ref[e, c, :, cols].astype(F32) for c in range(2)]
    data = jnp.concatenate(parts, 0).astype(BF16)
    pick = jnp.where(iota((wanted.shape[0], data.shape[0]), 1) == wanted, 1.0, 0.0)
    return jnp.dot(pick.astype(BF16), data, preferred_element_type=F32).astype(BF16)


def outer_rows(at, two, core):
    image = lax.shift_right_arithmetic(at, 1) & jnp.where(two, 1, 3)
    component = lax.shift_right_arithmetic(at, jnp.where(two, 2, 3))
    return (2 * image + component) * ROWS + (at & 1) + jnp.where(core == 1, ROWS - HALO, 0)


def blocks_of(ref):
    return [slice(n * BLOCK, (n + 1) * BLOCK) for n in range(ref.shape[-1] // BLOCK)]


def own_edges_kernel(images, own, first_two, outer, outer_two):
    core = place()[1]
    own[...] = images[...]
    first_two[...] = images[:2]
    to = iota((24, 64), 0)
    wanted = outer_rows(to & 15, to >= 16, core)
    for cols in blocks_of(own):
        edges = picked_edges((images,), wanted, cols)
        outer[:, cols] = edges[:16]
        outer_two[:, cols] = edges[16:]


def again_kernel(outer, outer_again):
    outer_again[...] = outer[...]


def inner_edges_kernel(*refs):
    core = place()[1]
    *images, inner = refs
    count = sum(ref.shape[0] for ref in images)
    to = iota((4 * count, 16 * count), 0)
    second = to >= 2 * count
    at = jnp.where(second, to - 2 * count, to)
    wanted = (at & -2) * ROWS + jnp.where(second, ROWS, 0) + (at & 1) + jnp.where(core == 0, ROWS - HALO, 0)
    for cols in blocks_of(inner):
        inner[:, cols] = picked_edges(images, wanted, cols)


def halves(terms):
    high = terms.astype(BF16)
    return high, (terms - high.astype(F32)).astype(BF16)


def sums_kernel(*refs):
    *blocks, main_weights, sums = refs
    near = [block.at[e] for block in blocks for e in range(block.shape[0])]
    first = len(near) - 2 - MAXP

    def body(n, carry):
        cols = pl.ds(pl.multiple_of(n * BLOCK, BLOCK), BLOCK)
        images = [(ref[0, :, cols].astype(F32), ref[1, :, cols].astype(F32)) for ref in near]
        powers = [re * re + im * im for re, im in images]
        for a in (first, first + 1):
            own_re, own_im = images[a]
            partners = images[a + 1 : a + 1 + MAXP]
            fields = [own_re * re + own_im * im for re, im in partners]
            fields += [own_im * re - own_re * im for re, im in partners]
            fields += powers[a : a + 1 + MAXP] + [jnp.zeros((ROWS, BLOCK), F32)]
            high, low = halves(jnp.concatenate(fields, 0))
            total = jnp.dot(main_weights[a], high, preferred_element_type=F32)
            total = total + jnp.dot(main_weights[a], low, preferred_element_type=F32)
            sums[a - first, :, cols] = total
        return carry

    lax.fori_loop(0, sums.shape[-1] // BLOCK, body, 0, unroll=UNROLL_SUMS)


def repeated(tile, first):
    rows = iota(tile.shape, 0)
    kept = jnp.where((rows >= first) & (rows < first + 2), tile, 0.0)
    kept = kept + pltpu.roll(kept, 2, 0)
    return kept + pltpu.roll(kept, 4, 0)


def windows_kernel(first, *refs):
    own_outer, outer_1, inner_1, *refs = refs
    outer_2, inner_2, *refs = refs if first else (None, None, *refs)
    halo_weights, bands, factors, sums, *refs = refs
    if first:
        ifg_before, coh_before, ifg_out, coh_out, *refs = refs
        edge_rows, rounded, ifg, coh, sems = refs
        pieces = [(ifg_before, ifg_out, 0), (coh_before, coh_out, 0)]
        copies = []
        for k, (ref, out, at) in enumerate(pieces):
            copies.append(pltpu.make_async_copy(ref, out.at[at : at + 2], sems.at[k]))
            copies[-1].start()
    else:
        ifg, coh, edge_rows, rounded = refs
    cols_total = inner_1.shape[-1]
    blocks = cols_total // BLOCK
    rounded[:, :, :PAD] = jnp.zeros((2, FIELDS, PAD), BF16)
    rounded[:, :, PAD + cols_total :] = jnp.zeros((2, FIELDS, PAD), BF16)
    for c in range(2):
        at = EDGE * c
        edge_rows[0, at : at + 8, :] = own_outer[8 * c : 8 * c + 8].astype(F32)
        edge_rows[0, at + 8 : at + 16, :] = outer_1[8 * c : 8 * c + 8].astype(F32)
        edge_rows[1, at : at + 16, :] = inner_1[16 * c : 16 * c + 16].astype(F32)
        for h, ref in enumerate((outer_2, inner_2)):
            last = jnp.zeros((8, cols_total), F32)
            if first:
                last = ref[...].astype(F32)
                last = pltpu.roll(last, 4, 0) if c else last
                last = jnp.where(iota(last.shape, 0) < 4, last, 0.0)
            edge_rows[h, at + 16 : at + EDGE, :] = last

    def row_body(n, a):
        start = pl.multiple_of(n * BLOCK, BLOCK)
        cols = pl.ds(start, BLOCK)
        fields = []
        for h in range(2):
            mine = []
            for c in range(2):
                at = c * EDGE + 2 * a
                tile = edge_rows[h, at // 8 * 8 : at // 8 * 8 + 8, cols]
                mine.append(repeated(tile, at % 8))
            own_re, own_im = mine
            images = []
            for half in range(2):
                at = 2 * a + 8 * half
                images.append((edge_rows[h, at : at + 8, cols], edge_rows[h, at + EDGE : at + EDGE + 8, cols]))
            fields += [own_re * re + own_im * im for re, im in images]
            fields += [own_im * re - own_re * im for re, im in images]
            fields += [re * re + im * im for re, im in images]
        terms = jnp.concatenate(halves(jnp.concatenate(fields, 0)), 0)
        total = sums[a - first, :, cols] + jnp.dot(halo_weights[a], terms, preferred_element_type=F32)
        rounded[a % 2, :, pl.ds(pl.multiple_of(start + PAD, 128), BLOCK)] = total.astype(BF16)

    def col_body(n, a):
        start = pl.multiple_of(n * BLOCK, BLOCK)
        cols = pl.ds(start, BLOCK)
        inside = rounded[a % 2, :, pl.ds(pl.multiple_of(start + PAD, 128), BLOCK)]
        left = rounded[a % 2, :, pl.ds(start, PAD)]
        right = rounded[a % 2, :, pl.ds(pl.multiple_of(start + PAD + BLOCK, 128), PAD)]
        sides = jnp.where(iota((FIELDS, PAD), 1) < 64, right, left)
        boxed = jnp.dot(inside, bands[a, :BLOCK, :], preferred_element_type=F32)
        boxed = boxed + jnp.dot(sides, bands[a, BLOCK:, :], preferred_element_type=F32)
        own_power = boxed[96:104]
        for j in range(MAXP):
            re = boxed[8 * j : 8 * j + 8]
            im = boxed[48 + 8 * j : 56 + 8 * j]
            power = boxed[104 + 8 * j : 112 + 8 * j]
            scale = jnp.concatenate([factors[a, j : j + 1, :]] * 2, 1)
            live = jnp.concatenate([factors[a, 8 + j : 9 + j, :]] * 2, 1)
            ifg[a - first, j, 0, :, cols] = (re * scale).astype(BF16)
            ifg[a - first, j, 1, :, cols] = (im * scale).astype(BF16)
            square = re * re + im * im
            magnitude = square * lax.rsqrt(jnp.maximum(square, tiny))
            coherence = magnitude * lax.rsqrt(own_power * power + epsilon) * live
            coh[a - first, j, :, cols] = coherence.astype(BF16)

    def loop(body, a, unroll):
        lax.fori_loop(0, blocks, lambda n, carry: (body(n, a), carry)[1], 0, unroll=unroll)

    for a in (first, first + 1):
        loop(row_body, a, UNROLL_HALO)
        loop(col_body, a, UNROLL_COLS)
        if first:
            for k, (scratch, out) in enumerate(((ifg, ifg_out), (coh, coh_out))):
                copy = pltpu.make_async_copy(scratch.at[a - first], out.at[a], sems.at[2 * (a - first + 1) + k])
                copy.start()
                copies.append(copy)
    if first:
        for copy in copies:
            copy.wait()


VMEM = pl.BlockSpec(memory_space=pltpu.VMEM)
SMEM = pl.BlockSpec(memory_space=pltpu.SMEM)


def kernel(body, name, in_specs, out_specs, out_shape, flops, moved, scratch=(), limit=40):
    return pl.pallas_call(
        body,
        in_specs=in_specs,
        out_specs=out_specs,
        out_shape=[jax.ShapeDtypeStruct(*s) for s in out_shape],
        scratch_shapes=scratch,
        compiler_params=pltpu.CompilerParams(vmem_limit_bytes=limit * 2**20),
        cost_estimate=pl.CostEstimate(flops=flops, bytes_accessed=moved, transcendentals=0),
        name=name,
    )


def moved(block, distance, partner):
    count, rows = lax.axis_size("tm"), lax.axis_size("rows")
    pairs = [
        ((t + distance) % count * rows + partner(r, rows), t * rows + r)
        for t in range(count)
        for r in range(rows)
    ]
    return lax.ppermute(block, ("tm", "rows"), pairs)


def same(row, rows):
    return row


def across(row, rows):
    return (row + 1 if row % 2 else row - 1) % rows


def sibling(row, rows):
    return row ^ 1


def local(slc_stack, partner_count, look_sizes):
    cols = slc_stack.shape[-1]
    edge_16, edge_8 = ((16, cols), BF16), ((8, cols), BF16)
    next_1 = moved(slc_stack, 1, same)
    own, first_two, outer, outer_two = kernel(
        own_edges_kernel,
        "own_edges",
        [VMEM],
        [VMEM] * 4,
        [(slc_stack.shape, BF16), ((2,) + slc_stack.shape[1:], BF16), edge_16, edge_8],
        10**6,
        10**6,
    )(slc_stack)
    next_2 = moved(first_two, 2, same)
    outer_2 = moved(outer_two, 2, across)
    outer_1 = moved(outer, 1, across)
    (again,) = kernel(again_kernel, "again", [VMEM], [VMEM], [edge_16], 10**5, 10**5)(outer)
    own_outer = moved(again, 0, across)
    packed = look_sizes[:, 0] + 16 * look_sizes[:, 1] + 256 * partner_count
    main_weights, halo_weights, bands, factors = kernel(
        setup_kernel,
        "setup",
        [VMEM, pl.BlockSpec(memory_space=pl.ANY)],
        [VMEM] * 4,
        [
            ((4, FIELDS, FIELDS), BF16),
            ((4, FIELDS, 2 * WINDOW), BF16),
            ((4, 384, BLOCK), BF16),
            ((4, 16, 128), F32),
        ],
        10**6,
        2 * 10**6,
    )(packed[None], again)

    anywhere = pl.BlockSpec(memory_space=pl.ANY)

    def inner_edges(name, images, after):
        count = sum(image.shape[0] for image in images)
        return kernel(
            lambda after, *refs: inner_edges_kernel(*refs),
            name,
            [anywhere] + [VMEM] * len(images),
            [VMEM],
            [((4 * count, cols), BF16)],
            10**6,
            10**6,
        )(after, *images)[0]

    def row_sums(name, blocks, after):
        return kernel(
            lambda after, *refs: sums_kernel(*refs),
            name,
            [anywhere] + [VMEM] * (len(blocks) + 1),
            [VMEM],
            [((2, FIELDS, cols), F32)],
            2 * 10**9,
            3 * 10**6,
        )(after, *blocks, main_weights)[0]

    pair_shapes = [((2, MAXP, 2, ROWS, cols), BF16), ((2, MAXP, ROWS, cols), BF16)]
    scratch = [
        pltpu.VMEM((2, 2 * EDGE, cols), F32),
        pltpu.VMEM((2, FIELDS, cols + 2 * PAD), BF16),
    ]
    edges_1 = inner_edges("inner_1", (own, next_1), factors)
    inner_1 = moved(edges_1, 0, sibling)
    sums_1 = row_sums("sums_1", (own, next_1), edges_1)
    ifg, coh = kernel(
        functools.partial(windows_kernel, 0),
        "windows_1",
        [VMEM] * 7,
        [VMEM] * 2,
        pair_shapes,
        2 * 10**9,
        4 * 10**6,
        scratch,
    )(own_outer, outer_1, inner_1, halo_weights, bands, factors, sums_1)
    edges_2 = inner_edges("inner_2", (next_2,), coh)
    inner_2 = moved(edges_2, 0, sibling)
    sums_2 = row_sums("sums_2", (own, next_1, next_2), edges_2)
    return kernel(
        functools.partial(windows_kernel, 2),
        "windows_2",
        [VMEM] * 11,
        [pl.BlockSpec(memory_space=pl.ANY)] * 2,
        [((4, MAXP, 2, ROWS, cols), BF16), ((4, MAXP, ROWS, cols), BF16)],
        2 * 10**9,
        4 * 10**6,
        scratch + [pltpu.VMEM(*shape) for shape in pair_shapes] + [pltpu.SemaphoreType.DMA((6,))],
    )(
        own_outer, outer_1, inner_1, outer_2, inner_2, halo_weights, bands, factors,
        sums_2, ifg, coh,
    )


def solution(mesh):
    return jax.shard_map(
        local,
        mesh=mesh,
        in_specs=(P("tm", None, "rows", None), P("tm"), P("tm", None)),
        out_specs=(P("tm", None, None, "rows", None), P("tm", None, "rows", None)),
        check_vma=False,
    )
```

time: 29.3 us -> 27.9 us (0.952)
  local copies, waits for them, and re-layouts: 3.35 us -> 0.98 us
  other arithmetic: 0 us -> 0.76 us
    unnamed x7 -> x2, local copies, waits for them, and re-layouts: 3.35 us -> 0.98 us
    broadcast_in_dim x0 -> x1, other arithmetic: none -> 0.76 us  [local(): packed[None]]
    pallas_call x5 -> x9, Pallas kernels: 7.1 us -> 7.08 us  [the longest x1 2.73 us: local(): kernel(functools.partial(windows_kernel, 2), 'windows_2', [VMEM] * 11, [p...]
  transfers between devices with their start and end apart: 7 -> 7, of which waited for: 0 -> 0; matrix products, arithmetic and copies ran while one was open for 3% -> 3% of each run, Pallas kernels for 10% -> 16%
where the time goes in v4:
time: 27.9 us; the launch traced here: 27.7 us
  starting transfers between devices  18.1 us (65%)
  Pallas kernels  7.08 us (25%)
  local copies, waits for them, and re-layouts  0.98 us (4%)
  other arithmetic  0.76 us (3%)
  between operations  0.73 us (3%)
    ppermute x7, starting transfers between devices, moved(): return lax.ppermute(block, ('tm', 'rows'), pairs)  18.1 us
    pallas_call x1, Pallas kernels, local(): kernel(functools.partial(windows_kernel, 2), 'windows_2', [VMEM] * 11, [p...  2.73 us
    pallas_call x2, Pallas kernels, row_sums(): kernel(lambda after, *refs: sums_kernel(*refs), name, [anywhere] + [VMEM]...  1.82 us
    pallas_call x1, Pallas kernels, local(): kernel(functools.partial(windows_kernel, 0), 'windows_1', [VMEM] * 7, [VM...  1.69 us
    unnamed x2, local copies, waits for them, and re-layouts  0.98 us
    broadcast_in_dim x1, other arithmetic, local(): packed[None]  0.76 us
  transfers between devices with their start and end apart: 7, of which 0 were waited for; matrix products, arithmetic and copies ran while one was open for 3% of the time, Pallas kernels for 16%

profile of v4, /device:TPU:1, one launch (start us, length us, event | category | flops | bytes accessed | tf_op | source)
XLA Modules:
  0.0 27.7 jit_solution(882987302821119976)
XLA Ops:
  0.6 8.9 %collective-permute-start.2 = (bf16[4,2,8,2048]{3,2,1,0:T(8,128)(2,1)}, bf16[4,2,8,2048]{3,2,1,0:T(8,128)(2,1)S(1)}, u32[]{:S(2)}, u32[]{:S(2)}) collective-permute-start(bf16[4,2,8,2048]{3,2,1,0:T(8,128)(2,1)} %images.1), channel_id=1, source_target_pairs={{16,0},{17,1},{18,2},{19,3},{20,4},{21,5},{22,6},{23,7},{24,8},{25... | collective-permute-start | bytes 786440 | tf_op jit(solution)/shard_map/ppermute | solution.py:288
  9.6 0.0 copy-start
  9.6 1.0 %copy-done = bf16[4,2,8,2048]{3,2,1,0:T(8,128)(2,1)S(1)} copy-done((bf16[4,2,8,2048]{3,2,1,0:T(8,128)(2,1)S(1)}, bf16[4,2,8,2048]{3,2,1,0:T(8,128)(2,1)}, u32[]{:S(2)}) %copy-start) | copy-done | bytes 262168
  10.6 0.2 own_edges.1
  10.7 2.7 %collective-permute-start.4 = (bf16[8,2048]{1,0:T(8,128)(2,1)S(1)}, bf16[8,2048]{1,0:T(8,128)(2,1)S(1)}, u32[]{:S(2)}, u32[]{:S(2)}) collective-permute-start(bf16[8,2048]{1,0:T(8,128)(2,1)S(1)} %get-tuple-element.15), channel_id=1, source_target_pairs={{47,0},{34,1},{33,2},{36,3},{35,4},{38,5},{37,6},{40,7},{39,8},{42... | collective-permute-start | bytes 98312 | tf_op jit(solution)/shard_map/ppermute | solution.py:288
  13.4 0.0 collective-permute-start.1
  13.4 1.7 %collective-permute-start = (bf16[16,2048]{1,0:T(8,128)(2,1)S(1)}, bf16[16,2048]{1,0:T(8,128)(2,1)S(1)}, u32[]{:S(2)}, u32[]{:S(2)}) collective-permute-start(bf16[16,2048]{1,0:T(8,128)(2,1)S(1)} %again.1.after), channel_id=1, source_target_pairs={{15,0},{2,1},{1,2},{4,3},{3,4},{6,5},{5,6},{8,7},{7,8},{10,9},{9,1... | collective-permute-start | bytes 196616 | tf_op jit(solution)/shard_map/ppermute | solution.py:288
  15.1 0.7 %collective-permute-start.5 = (bf16[2,2,8,2048]{3,2,1,0:T(8,128)(2,1)S(1)}, bf16[2,2,8,2048]{3,2,1,0:T(8,128)(2,1)S(1)}, u32[]{:S(2)}, u32[]{:S(2)}) collective-permute-start(bf16[2,2,8,2048]{3,2,1,0:T(8,128)(2,1)S(1)} %get-tuple-element.20), channel_id=1, source_target_pairs={{32,0},{33,1},{34,2},{35,3},{36,4},{37,5},{38,6},{39,7},{40,8},{41... | collective-permute-start | bytes 393224 | tf_op jit(solution)/shard_map/ppermute | solution.py:288
  15.8 0.8 %fusion.packed = s32[1,4]{1,0:T(1,128)S(1)} fusion(s32[4]{0:T(128)} %param.4, s32[4,2]{0,1:T(2,128)} %param.5), kind=kLoop, calls=%fused_computation.1 | loop fusion | flops 16 | bytes 64 | tf_op jit(solution)/shard_map/broadcast_in_dim | solution.py:335
  16.6 0.3 %setup.1 = (bf16[4,160,160]{2,1,0:T(8,128)(2,1)S(1)}, bf16[4,160,192]{2,1,0:T(8,128)(2,1)S(1)}, bf16[4,384,256]{2,1,0:T(8,128)(2,1)S(1)}, f32[4,16,128]{2,1,0:T(8,128)S(1)}) custom-call(s32[1,4]{1,0:T(1,128)S(1)} %fusion.packed, bf16[16,2048]{1,0:T(8,128)(2,1)S(1)} %again.1.after), custom_call_target="tpu_custom_call" | custom-call | flops 1000000 | bytes 2000000 | tf_op jit(solution)/shard_map/setup/pallas_call | solution.py:322
  16.9 0.0 collective-permute-done.2.refs_1_
  16.9 0.2 inner_1.1.after
  17.1 3.5 %collective-permute-start.3 = (bf16[32,2048]{1,0:T(8,128)(2,1)S(1)}, bf16[32,2048]{1,0:T(8,128)(2,1)S(1)}, u32[]{:S(2)}, u32[]{:S(2)}) collective-permute-start(bf16[32,2048]{1,0:T(8,128)(2,1)S(1)} %inner_1.1.after), channel_id=1, source_target_pairs={{1,0},{0,1},{3,2},{2,3},{5,4},{4,5},{7,6},{6,7},{9,8},{8,9},{11,10... | collective-permute-start | bytes 393224 | tf_op jit(solution)/shard_map/ppermute | solution.py:288
  20.6 0.9 %sums_1.1.refs_6_ = f32[2,160,2048]{2,1,0:T(8,128)S(1)} custom-call(bf16[32,2048]{1,0:T(8,128)(2,1)S(1)} %inner_1.1.after, bf16[4,2,8,2048]{3,2,1,0:T(8,128)(2,1)S(1)} %get-tuple-element.14.refs_0_, bf16[4,2,8,2048]{3,2,1,0:T(8,128)(2,1)S(1)} %collective-permute-done.2.refs_1_, bf16[4,160,160]{2,1,0:T(8,128)(2,1)S(1)} %get-tuple-element.18.refs_2_.refs_3_), custom_call_target="tpu_custom_call" | custom-call | flops 2000000000 | bytes 3000000 | tf_op jit(solution)/shard_map/sums_1/pallas_call | solution.py:352
  21.5 0.0 collective-permute-done.refs_0_
  21.5 0.0 collective-permute-done.1.refs_1_
  21.6 0.0 collective-permute-done.3.refs_2_
  21.6 1.7 %windows_1.1 = (bf16[2,6,2,8,2048]{4,3,2,1,0:T(8,128)(2,1)S(1)}, bf16[2,6,8,2048]{3,2,1,0:T(8,128)(2,1)S(1)}) custom-call(bf16[16,2048]{1,0:T(8,128)(2,1)S(1)} %collective-permute-done.refs_0_, bf16[16,2048]{1,0:T(8,128)(2,1)S(1)} %collective-permute-done.1.refs_1_, bf16[32,2048]{1,0:T(8,128)(2,1)S(1)} %collective-permute-done.3.refs_2_, ...), custom_call_target="tpu_custom_call" | custom-call | flops 2000000000 | bytes 4000000 | tf_op jit(solution)/shard_map/windows_1/pallas_call | solution.py:370
  23.3 0.0 collective-permute-done.5.refs_0_.refs_2_
  23.3 0.1 inner_2.1.after
  23.5 0.6 %collective-permute-start.6 = (bf16[8,2048]{1,0:T(8,128)(2,1)S(1)}, bf16[8,2048]{1,0:T(8,128)(2,1)S(1)}, u32[]{:S(2)}, u32[]{:S(2)}) collective-permute-start(bf16[8,2048]{1,0:T(8,128)(2,1)S(1)} %inner_2.1.after), channel_id=1, source_target_pairs={{1,0},{0,1},{3,2},{2,3},{5,4},{4,5},{7,6},{6,7},{9,8},{8,9},{11,10... | collective-permute-start | bytes 98312 | tf_op jit(solution)/shard_map/ppermute | solution.py:288
  24.1 0.9 %sums_2.1.refs_8_ = f32[2,160,2048]{2,1,0:T(8,128)S(1)} custom-call(bf16[8,2048]{1,0:T(8,128)(2,1)S(1)} %inner_2.1.after, bf16[4,2,8,2048]{3,2,1,0:T(8,128)(2,1)S(1)} %get-tuple-element.14.refs_0_, bf16[4,2,8,2048]{3,2,1,0:T(8,128)(2,1)S(1)} %collective-permute-done.2.refs_1_, bf16[2,2,8,2048]{3,2,1,0:T(8,128)(2,1)S(1)} %collective-permute-done.5.refs_0_.refs_2_, ...), custom_call_target="tpu_custom_call" | custom-call | flops 2000000000 | bytes 3000000 | tf_op jit(solution)/shard_map/sums_2/pallas_call | solution.py:352
  25.0 0.0 collective-permute-done.4.refs_3_
  25.0 0.0 collective-permute-done.6.refs_4_
  25.0 2.7 %windows_2.1 = (bf16[4,6,2,8,2048]{4,3,2,1,0:T(8,128)(2,1)}, bf16[4,6,8,2048]{3,2,1,0:T(8,128)(2,1)}) custom-call(bf16[16,2048]{1,0:T(8,128)(2,1)S(1)} %collective-permute-done.refs_0_, bf16[16,2048]{1,0:T(8,128)(2,1)S(1)} %collective-permute-done.1.refs_1_, bf16[32,2048]{1,0:T(8,128)(2,1)S(1)} %collective-permute-done.3.refs_2_, ...), custom_call_target="tpu_custom_call" | custom-call | flops 2000000000 | bytes 4000000 | tf_op jit(solution)/shard_map/windows_2/pallas_call | solution.py:383
  (1 shorter events, 0.0 us)
Async XLA Ops:
  0.6 16.3 %collective-permute-start.2 = (bf16[4,2,8,2048]{3,2,1,0:T(8,128)(2,1)}, bf16[4,2,8,2048]{3,2,1,0:T(8,128)(2,1)S(1)}, u32[]{:S(2)}, u32[]{:S(2)}) collective-permute-start(bf16[4,2,8,2048]{3,2,1,0:T(8,128)(2,1)} %images.1), channel_id=1, source_target_pairs={{16,0},{17,1},{18,2},{19,3},{20,4},{21,5},{22,6},{23,7},{24,8},{25... | collective-permute-start | bytes 786440 | tf_op jit(solution)/shard_map/ppermute | solution.py:288
  9.6 1.0 %copy-start = (bf16[4,2,8,2048]{3,2,1,0:T(8,128)(2,1)S(1)}, bf16[4,2,8,2048]{3,2,1,0:T(8,128)(2,1)}, u32[]{:S(2)}) copy-start(bf16[4,2,8,2048]{3,2,1,0:T(8,128)(2,1)} %images.1) | copy-start | bytes 786436
  10.7 14.3 %collective-permute-start.4 = (bf16[8,2048]{1,0:T(8,128)(2,1)S(1)}, bf16[8,2048]{1,0:T(8,128)(2,1)S(1)}, u32[]{:S(2)}, u32[]{:S(2)}) collective-permute-start(bf16[8,2048]{1,0:T(8,128)(2,1)S(1)} %get-tuple-element.15), channel_id=1, source_target_pairs={{47,0},{34,1},{33,2},{36,3},{35,4},{38,5},{37,6},{40,7},{39,8},{42... | collective-permute-start | bytes 98312 | tf_op jit(solution)/shard_map/ppermute | solution.py:288
  13.4 8.1 %collective-permute-start.1 = (bf16[16,2048]{1,0:T(8,128)(2,1)S(1)}, bf16[16,2048]{1,0:T(8,128)(2,1)S(1)}, u32[]{:S(2)}, u32[]{:S(2)}) collective-permute-start(bf16[16,2048]{1,0:T(8,128)(2,1)S(1)} %get-tuple-element.12.outer), channel_id=1, source_target_pairs={{31,0},{18,1},{17,2},{20,3},{19,4},{22,5},{21,6},{24,7},{23,8},{26... | collective-permute-start | bytes 196616 | tf_op jit(solution)/shard_map/ppermute | solution.py:288
  13.4 8.1 %collective-permute-start = (bf16[16,2048]{1,0:T(8,128)(2,1)S(1)}, bf16[16,2048]{1,0:T(8,128)(2,1)S(1)}, u32[]{:S(2)}, u32[]{:S(2)}) collective-permute-start(bf16[16,2048]{1,0:T(8,128)(2,1)S(1)} %again.1.after), channel_id=1, source_target_pairs={{15,0},{2,1},{1,2},{4,3},{3,4},{6,5},{5,6},{8,7},{7,8},{10,9},{9,1... | collective-permute-start | bytes 196616 | tf_op jit(solution)/shard_map/ppermute | solution.py:288
  15.1 8.2 %collective-permute-start.5 = (bf16[2,2,8,2048]{3,2,1,0:T(8,128)(2,1)S(1)}, bf16[2,2,8,2048]{3,2,1,0:T(8,128)(2,1)S(1)}, u32[]{:S(2)}, u32[]{:S(2)}) collective-permute-start(bf16[2,2,8,2048]{3,2,1,0:T(8,128)(2,1)S(1)} %get-tuple-element.20), channel_id=1, source_target_pairs={{32,0},{33,1},{34,2},{35,3},{36,4},{37,5},{38,6},{39,7},{40,8},{41... | collective-permute-start | bytes 393224 | tf_op jit(solution)/shard_map/ppermute | solution.py:288
  17.1 4.5 %collective-permute-start.3 = (bf16[32,2048]{1,0:T(8,128)(2,1)S(1)}, bf16[32,2048]{1,0:T(8,128)(2,1)S(1)}, u32[]{:S(2)}, u32[]{:S(2)}) collective-permute-start(bf16[32,2048]{1,0:T(8,128)(2,1)S(1)} %inner_1.1.after), channel_id=1, source_target_pairs={{1,0},{0,1},{3,2},{2,3},{5,4},{4,5},{7,6},{6,7},{9,8},{8,9},{11,10... | collective-permute-start | bytes 393224 | tf_op jit(solution)/shard_map/ppermute | solution.py:288
  23.5 1.5 %collective-permute-start.6 = (bf16[8,2048]{1,0:T(8,128)(2,1)S(1)}, bf16[8,2048]{1,0:T(8,128)(2,1)S(1)}, u32[]{:S(2)}, u32[]{:S(2)}) collective-permute-start(bf16[8,2048]{1,0:T(8,128)(2,1)S(1)} %inner_2.1.after), channel_id=1, source_target_pairs={{1,0},{0,1},{3,2},{2,3},{5,4},{4,5},{7,6},{6,7},{9,8},{8,9},{11,10... | collective-permute-start | bytes 98312 | tf_op jit(solution)/shard_map/ppermute | solution.py:288

commit v5 on v4

--- a/solution.py
+++ b/solution.py
@@ -280,11 +280,15 @@
 
 def moved(block, distance, partner):
     count, rows = lax.axis_size("tm"), lax.axis_size("rows")
-    pairs = [
-        ((t + distance) % count * rows + partner(r, rows), t * rows + r)
-        for t in range(count)
-        for r in range(rows)
-    ]
+    pairs = []
+    for t in range(count):
+        for r in range(rows):
+            source = partner(r, rows)
+            if t + distance >= count:
+                source = (r + rows // 2) % rows if distance == 1 else r
+            elif distance and abs(source - r) > 1:
+                source = r
+            pairs.append(((t + distance) % count * rows + source, t * rows + r))
     return lax.ppermute(block, ("tm", "rows"), pairs)
 
 

time: 27.9 us -> 26.4 us (0.946)
  starting transfers between devices: 18.1 us -> 16.7 us
    ppermute x7, starting transfers between devices: 18.1 us -> 16.7 us  [moved(): return lax.ppermute(block, ('tm', 'rows'), pairs)]
  transfers between devices with their start and end apart: 7 -> 7, of which waited for: 0 -> 0; matrix products, arithmetic and copies ran while one was open for 3% -> 3% of each run, Pallas kernels for 16% -> 17%
where the time goes in v5:
time: 26.4 us; the launch traced here: 26.3 us
  starting transfers between devices  16.7 us (63%)
  Pallas kernels  7.07 us (27%)
  local copies, waits for them, and re-layouts  0.98 us (4%)
  other arithmetic  0.76 us (3%)
  between operations  0.73 us (3%)
    ppermute x7, starting transfers between devices, moved(): return lax.ppermute(block, ('tm', 'rows'), pairs)  16.7 us
    pallas_call x1, Pallas kernels, local(): kernel(functools.partial(windows_kernel, 2), 'windows_2', [VMEM] * 11, [p...  2.72 us
    pallas_call x2, Pallas kernels, row_sums(): kernel(lambda after, *refs: sums_kernel(*refs), name, [anywhere] + [VMEM]...  1.82 us
    pallas_call x1, Pallas kernels, local(): kernel(functools.partial(windows_kernel, 0), 'windows_1', [VMEM] * 7, [VM...  1.69 us
    unnamed x2, local copies, waits for them, and re-layouts  0.98 us
    broadcast_in_dim x1, other arithmetic, local(): packed[None]  0.76 us
  transfers between devices with their start and end apart: 7, of which 0 were waited for; matrix products, arithmetic and copies ran while one was open for 3% of the time, Pallas kernels for 17%

profile of v5, /device:TPU:1, one launch (start us, length us, event | category | flops | bytes accessed | tf_op | source)
XLA Modules:
  0.0 26.3 jit_solution(11986972118939657112)
XLA Ops:
  0.6 8.7 %collective-permute-start.2 = (bf16[4,2,8,2048]{3,2,1,0:T(8,128)(2,1)}, bf16[4,2,8,2048]{3,2,1,0:T(8,128)(2,1)S(1)}, u32[]{:S(2)}, u32[]{:S(2)}) collective-permute-start(bf16[4,2,8,2048]{3,2,1,0:T(8,128)(2,1)} %images.1), channel_id=1, source_target_pairs={{16,0},{17,1},{18,2},{19,3},{20,4},{21,5},{22,6},{23,7},{24,8},{25... | collective-permute-start | bytes 786440 | tf_op jit(solution)/shard_map/ppermute | solution.py:292
  9.3 0.0 copy-start
  9.3 1.0 %copy-done = bf16[4,2,8,2048]{3,2,1,0:T(8,128)(2,1)S(1)} copy-done((bf16[4,2,8,2048]{3,2,1,0:T(8,128)(2,1)S(1)}, bf16[4,2,8,2048]{3,2,1,0:T(8,128)(2,1)}, u32[]{:S(2)}) %copy-start) | copy-done | bytes 262168
  10.3 0.2 own_edges.1
  10.5 1.1 %collective-permute-start.4 = (bf16[8,2048]{1,0:T(8,128)(2,1)S(1)}, bf16[8,2048]{1,0:T(8,128)(2,1)S(1)}, u32[]{:S(2)}, u32[]{:S(2)}) collective-permute-start(bf16[8,2048]{1,0:T(8,128)(2,1)S(1)} %get-tuple-element.15), channel_id=1, source_target_pairs={{32,0},{34,1},{33,2},{36,3},{35,4},{38,5},{37,6},{40,7},{39,8},{42... | collective-permute-start | bytes 98312 | tf_op jit(solution)/shard_map/ppermute | solution.py:292
  11.6 2.7 %collective-permute-start.1 = (bf16[16,2048]{1,0:T(8,128)(2,1)S(1)}, bf16[16,2048]{1,0:T(8,128)(2,1)S(1)}, u32[]{:S(2)}, u32[]{:S(2)}) collective-permute-start(bf16[16,2048]{1,0:T(8,128)(2,1)S(1)} %get-tuple-element.12.outer), channel_id=1, source_target_pairs={{16,0},{18,1},{17,2},{20,3},{19,4},{22,5},{21,6},{24,7},{23,8},{26... | collective-permute-start | bytes 196616 | tf_op jit(solution)/shard_map/ppermute | solution.py:292
  14.3 0.0 collective-permute-start
  14.3 1.6 %collective-permute-start.5 = (bf16[2,2,8,2048]{3,2,1,0:T(8,128)(2,1)S(1)}, bf16[2,2,8,2048]{3,2,1,0:T(8,128)(2,1)S(1)}, u32[]{:S(2)}, u32[]{:S(2)}) collective-permute-start(bf16[2,2,8,2048]{3,2,1,0:T(8,128)(2,1)S(1)} %get-tuple-element.20), channel_id=1, source_target_pairs={{32,0},{33,1},{34,2},{35,3},{36,4},{37,5},{38,6},{39,7},{40,8},{41... | collective-permute-start | bytes 393224 | tf_op jit(solution)/shard_map/ppermute | solution.py:292
  15.8 0.8 %fusion.packed = s32[1,4]{1,0:T(1,128)S(1)} fusion(s32[4]{0:T(128)} %param.4, s32[4,2]{0,1:T(2,128)} %param.5), kind=kLoop, calls=%fused_computation.1 | loop fusion | flops 16 | bytes 64 | tf_op jit(solution)/shard_map/broadcast_in_dim | solution.py:339
  16.6 0.3 %setup.1 = (bf16[4,160,160]{2,1,0:T(8,128)(2,1)S(1)}, bf16[4,160,192]{2,1,0:T(8,128)(2,1)S(1)}, bf16[4,384,256]{2,1,0:T(8,128)(2,1)S(1)}, f32[4,16,128]{2,1,0:T(8,128)S(1)}) custom-call(s32[1,4]{1,0:T(1,128)S(1)} %fusion.packed, bf16[16,2048]{1,0:T(8,128)(2,1)S(1)} %again.1.after), custom_call_target="tpu_custom_call" | custom-call | flops 1000000 | bytes 2000000 | tf_op jit(solution)/shard_map/setup/pallas_call | solution.py:326
  16.9 0.0 collective-permute-done.2.refs_1_
  16.9 0.2 inner_1.1.after
  17.1 1.1 %collective-permute-start.3 = (bf16[32,2048]{1,0:T(8,128)(2,1)S(1)}, bf16[32,2048]{1,0:T(8,128)(2,1)S(1)}, u32[]{:S(2)}, u32[]{:S(2)}) collective-permute-start(bf16[32,2048]{1,0:T(8,128)(2,1)S(1)} %inner_1.1.after), channel_id=1, source_target_pairs={{1,0},{0,1},{3,2},{2,3},{5,4},{4,5},{7,6},{6,7},{9,8},{8,9},{11,10... | collective-permute-start | bytes 393224 | tf_op jit(solution)/shard_map/ppermute | solution.py:292
  18.2 0.9 %sums_1.1.refs_6_ = f32[2,160,2048]{2,1,0:T(8,128)S(1)} custom-call(bf16[32,2048]{1,0:T(8,128)(2,1)S(1)} %inner_1.1.after, bf16[4,2,8,2048]{3,2,1,0:T(8,128)(2,1)S(1)} %get-tuple-element.14.refs_0_, bf16[4,2,8,2048]{3,2,1,0:T(8,128)(2,1)S(1)} %collective-permute-done.2.refs_1_, bf16[4,160,160]{2,1,0:T(8,128)(2,1)S(1)} %get-tuple-element.18.refs_2_.refs_3_), custom_call_target="tpu_custom_call" | custom-call | flops 2000000000 | bytes 3000000 | tf_op jit(solution)/shard_map/sums_1/pallas_call | solution.py:356
  19.2 0.0 collective-permute-done.refs_0_
  19.2 0.0 collective-permute-done.1.refs_1_
  19.2 0.0 collective-permute-done.3.refs_2_
  19.2 1.7 %windows_1.1 = (bf16[2,6,2,8,2048]{4,3,2,1,0:T(8,128)(2,1)S(1)}, bf16[2,6,8,2048]{3,2,1,0:T(8,128)(2,1)S(1)}) custom-call(bf16[16,2048]{1,0:T(8,128)(2,1)S(1)} %collective-permute-done.refs_0_, bf16[16,2048]{1,0:T(8,128)(2,1)S(1)} %collective-permute-done.1.refs_1_, bf16[32,2048]{1,0:T(8,128)(2,1)S(1)} %collective-permute-done.3.refs_2_, ...), custom_call_target="tpu_custom_call" | custom-call | flops 2000000000 | bytes 4000000 | tf_op jit(solution)/shard_map/windows_1/pallas_call | solution.py:374
  20.9 0.0 collective-permute-done.5.refs_0_.refs_2_
  20.9 0.1 inner_2.1.after
  21.1 1.6 %collective-permute-start.6 = (bf16[8,2048]{1,0:T(8,128)(2,1)S(1)}, bf16[8,2048]{1,0:T(8,128)(2,1)S(1)}, u32[]{:S(2)}, u32[]{:S(2)}) collective-permute-start(bf16[8,2048]{1,0:T(8,128)(2,1)S(1)} %inner_2.1.after), channel_id=1, source_target_pairs={{1,0},{0,1},{3,2},{2,3},{5,4},{4,5},{7,6},{6,7},{9,8},{8,9},{11,10... | collective-permute-start | bytes 98312 | tf_op jit(solution)/shard_map/ppermute | solution.py:292
  22.7 0.9 %sums_2.1.refs_8_ = f32[2,160,2048]{2,1,0:T(8,128)S(1)} custom-call(bf16[8,2048]{1,0:T(8,128)(2,1)S(1)} %inner_2.1.after, bf16[4,2,8,2048]{3,2,1,0:T(8,128)(2,1)S(1)} %get-tuple-element.14.refs_0_, bf16[4,2,8,2048]{3,2,1,0:T(8,128)(2,1)S(1)} %collective-permute-done.2.refs_1_, bf16[2,2,8,2048]{3,2,1,0:T(8,128)(2,1)S(1)} %collective-permute-done.5.refs_0_.refs_2_, ...), custom_call_target="tpu_custom_call" | custom-call | flops 2000000000 | bytes 3000000 | tf_op jit(solution)/shard_map/sums_2/pallas_call | solution.py:356
  23.6 0.0 collective-permute-done.4.refs_3_
  23.6 0.0 collective-permute-done.6.refs_4_
  23.6 2.7 %windows_2.1 = (bf16[4,6,2,8,2048]{4,3,2,1,0:T(8,128)(2,1)}, bf16[4,6,8,2048]{3,2,1,0:T(8,128)(2,1)}) custom-call(bf16[16,2048]{1,0:T(8,128)(2,1)S(1)} %collective-permute-done.refs_0_, bf16[16,2048]{1,0:T(8,128)(2,1)S(1)} %collective-permute-done.1.refs_1_, bf16[32,2048]{1,0:T(8,128)(2,1)S(1)} %collective-permute-done.3.refs_2_, ...), custom_call_target="tpu_custom_call" | custom-call | flops 2000000000 | bytes 4000000 | tf_op jit(solution)/shard_map/windows_2/pallas_call | solution.py:387
  (1 shorter events, 0.0 us)
Async XLA Ops:
  0.6 16.3 %collective-permute-start.2 = (bf16[4,2,8,2048]{3,2,1,0:T(8,128)(2,1)}, bf16[4,2,8,2048]{3,2,1,0:T(8,128)(2,1)S(1)}, u32[]{:S(2)}, u32[]{:S(2)}) collective-permute-start(bf16[4,2,8,2048]{3,2,1,0:T(8,128)(2,1)} %images.1), channel_id=1, source_target_pairs={{16,0},{17,1},{18,2},{19,3},{20,4},{21,5},{22,6},{23,7},{24,8},{25... | collective-permute-start | bytes 786440 | tf_op jit(solution)/shard_map/ppermute | solution.py:292
  9.3 1.0 %copy-start = (bf16[4,2,8,2048]{3,2,1,0:T(8,128)(2,1)S(1)}, bf16[4,2,8,2048]{3,2,1,0:T(8,128)(2,1)}, u32[]{:S(2)}) copy-start(bf16[4,2,8,2048]{3,2,1,0:T(8,128)(2,1)} %images.1) | copy-start | bytes 786436
  10.5 13.1 %collective-permute-start.4 = (bf16[8,2048]{1,0:T(8,128)(2,1)S(1)}, bf16[8,2048]{1,0:T(8,128)(2,1)S(1)}, u32[]{:S(2)}, u32[]{:S(2)}) collective-permute-start(bf16[8,2048]{1,0:T(8,128)(2,1)S(1)} %get-tuple-element.15), channel_id=1, source_target_pairs={{32,0},{34,1},{33,2},{36,3},{35,4},{38,5},{37,6},{40,7},{39,8},{42... | collective-permute-start | bytes 98312 | tf_op jit(solution)/shard_map/ppermute | solution.py:292
  11.6 7.6 %collective-permute-start.1 = (bf16[16,2048]{1,0:T(8,128)(2,1)S(1)}, bf16[16,2048]{1,0:T(8,128)(2,1)S(1)}, u32[]{:S(2)}, u32[]{:S(2)}) collective-permute-start(bf16[16,2048]{1,0:T(8,128)(2,1)S(1)} %get-tuple-element.12.outer), channel_id=1, source_target_pairs={{16,0},{18,1},{17,2},{20,3},{19,4},{22,5},{21,6},{24,7},{23,8},{26... | collective-permute-start | bytes 196616 | tf_op jit(solution)/shard_map/ppermute | solution.py:292
  14.3 4.9 %collective-permute-start = (bf16[16,2048]{1,0:T(8,128)(2,1)S(1)}, bf16[16,2048]{1,0:T(8,128)(2,1)S(1)}, u32[]{:S(2)}, u32[]{:S(2)}) collective-permute-start(bf16[16,2048]{1,0:T(8,128)(2,1)S(1)} %again.1.after), channel_id=1, source_target_pairs={{15,0},{2,1},{1,2},{4,3},{3,4},{6,5},{5,6},{8,7},{7,8},{10,9},{9,1... | collective-permute-start | bytes 196616 | tf_op jit(solution)/shard_map/ppermute | solution.py:292
  14.3 6.7 %collective-permute-start.5 = (bf16[2,2,8,2048]{3,2,1,0:T(8,128)(2,1)S(1)}, bf16[2,2,8,2048]{3,2,1,0:T(8,128)(2,1)S(1)}, u32[]{:S(2)}, u32[]{:S(2)}) collective-permute-start(bf16[2,2,8,2048]{3,2,1,0:T(8,128)(2,1)S(1)} %get-tuple-element.20), channel_id=1, source_target_pairs={{32,0},{33,1},{34,2},{35,3},{36,4},{37,5},{38,6},{39,7},{40,8},{41... | collective-permute-start | bytes 393224 | tf_op jit(solution)/shard_map/ppermute | solution.py:292
  17.1 2.1 %collective-permute-start.3 = (bf16[32,2048]{1,0:T(8,128)(2,1)S(1)}, bf16[32,2048]{1,0:T(8,128)(2,1)S(1)}, u32[]{:S(2)}, u32[]{:S(2)}) collective-permute-start(bf16[32,2048]{1,0:T(8,128)(2,1)S(1)} %inner_1.1.after), channel_id=1, source_target_pairs={{1,0},{0,1},{3,2},{2,3},{5,4},{4,5},{7,6},{6,7},{9,8},{8,9},{11,10... | collective-permute-start | bytes 393224 | tf_op jit(solution)/shard_map/ppermute | solution.py:292
  21.1 2.5 %collective-permute-start.6 = (bf16[8,2048]{1,0:T(8,128)(2,1)S(1)}, bf16[8,2048]{1,0:T(8,128)(2,1)S(1)}, u32[]{:S(2)}, u32[]{:S(2)}) collective-permute-start(bf16[8,2048]{1,0:T(8,128)(2,1)S(1)} %inner_2.1.after), channel_id=1, source_target_pairs={{1,0},{0,1},{3,2},{2,3},{5,4},{4,5},{7,6},{6,7},{9,8},{8,9},{11,10... | collective-permute-start | bytes 98312 | tf_op jit(solution)/shard_map/ppermute | solution.py:292

commit v6 on v5

--- a/solution.py
+++ b/solution.py
@@ -280,15 +280,19 @@
 
 def moved(block, distance, partner):
     count, rows = lax.axis_size("tm"), lax.axis_size("rows")
+    half = rows // 2
     pairs = []
     for t in range(count):
         for r in range(rows):
-            source = partner(r, rows)
+            start, source = (t + distance) % count, partner(r, rows)
             if t + distance >= count:
-                source = (r + rows // 2) % rows if distance == 1 else r
-            elif distance and abs(source - r) > 1:
-                source = r
-            pairs.append(((t + distance) % count * rows + source, t * rows + r))
+                late = {half - 1: rows - 1, half: rows - 2, rows - 1: half - 1, rows - 2: half}
+                source = (r + half) % rows if distance == 1 else r
+                if distance == 2 and partner is same:
+                    source = late.get(r, r)
+            elif abs(source - r) > 1:
+                start, source = start if distance else t ^ 2, r
+            pairs.append((start * rows + source, t * rows + r))
     return lax.ppermute(block, ("tm", "rows"), pairs)
 
 

time: 26.4 us -> 25.9 us (0.981)
  the two profiles are of different devices: /device:TPU:1 before, /device:TPU:31 now
where the time goes in v6:
time: 25.9 us; the launch traced here: 25.7 us
  starting transfers between devices  16.1 us (62%)
  Pallas kernels  7.08 us (27%)
  local copies, waits for them, and re-layouts  0.98 us (4%)
  other arithmetic  0.76 us (3%)
  between operations  0.73 us (3%)
    ppermute x7, starting transfers between devices, moved(): return lax.ppermute(block, ('tm', 'rows'), pairs)  16.1 us
    pallas_call x1, Pallas kernels, local(): kernel(functools.partial(windows_kernel, 2), 'windows_2', [VMEM] * 11, [p...  2.72 us
    pallas_call x2, Pallas kernels, row_sums(): kernel(lambda after, *refs: sums_kernel(*refs), name, [anywhere] + [VMEM]...  1.82 us
    pallas_call x1, Pallas kernels, local(): kernel(functools.partial(windows_kernel, 0), 'windows_1', [VMEM] * 7, [VM...  1.69 us
    unnamed x2, local copies, waits for them, and re-layouts  0.98 us
    broadcast_in_dim x1, other arithmetic, local(): packed[None]  0.76 us
  transfers between devices with their start and end apart: 7, of which 0 were waited for; matrix products, arithmetic and copies ran while one was open for 3% of the time, Pallas kernels for 17%

profile of v6, /device:TPU:31, one launch (start us, length us, event | category | flops | bytes accessed | tf_op | source)
XLA Modules:
  0.0 25.7 jit_solution(14349054196305702816)
XLA Ops:
  0.6 1.2 %collective-permute-start.2 = (bf16[4,2,8,2048]{3,2,1,0:T(8,128)(2,1)}, bf16[4,2,8,2048]{3,2,1,0:T(8,128)(2,1)S(1)}, u32[]{:S(2)}, u32[]{:S(2)}) collective-permute-start(bf16[4,2,8,2048]{3,2,1,0:T(8,128)(2,1)} %images.1), channel_id=1, source_target_pairs={{16,0},{17,1},{18,2},{19,3},{20,4},{21,5},{22,6},{23,7},{24,8},{25... | collective-permute-start | bytes 786440 | tf_op jit(solution)/shard_map/ppermute | solution.py:296
  1.8 0.0 copy-start
  1.8 1.0 %copy-done = bf16[4,2,8,2048]{3,2,1,0:T(8,128)(2,1)S(1)} copy-done((bf16[4,2,8,2048]{3,2,1,0:T(8,128)(2,1)S(1)}, bf16[4,2,8,2048]{3,2,1,0:T(8,128)(2,1)}, u32[]{:S(2)}) %copy-start) | copy-done | bytes 262168
  2.8 0.2 own_edges.1
  3.0 5.7 %collective-permute-start.4 = (bf16[8,2048]{1,0:T(8,128)(2,1)S(1)}, bf16[8,2048]{1,0:T(8,128)(2,1)S(1)}, u32[]{:S(2)}, u32[]{:S(2)}) collective-permute-start(bf16[8,2048]{1,0:T(8,128)(2,1)S(1)} %get-tuple-element.15), channel_id=1, source_target_pairs={{32,0},{34,1},{33,2},{36,3},{35,4},{38,5},{37,6},{40,7},{39,8},{42... | collective-permute-start | bytes 98312 | tf_op jit(solution)/shard_map/ppermute | solution.py:296
  8.7 2.3 %collective-permute-start.1 = (bf16[16,2048]{1,0:T(8,128)(2,1)S(1)}, bf16[16,2048]{1,0:T(8,128)(2,1)S(1)}, u32[]{:S(2)}, u32[]{:S(2)}) collective-permute-start(bf16[16,2048]{1,0:T(8,128)(2,1)S(1)} %get-tuple-element.12.outer), channel_id=1, source_target_pairs={{16,0},{18,1},{17,2},{20,3},{19,4},{22,5},{21,6},{24,7},{23,8},{26... | collective-permute-start | bytes 196616 | tf_op jit(solution)/shard_map/ppermute | solution.py:296
  11.0 0.1 collective-permute-start
  11.1 4.7 %collective-permute-start.5 = (bf16[2,2,8,2048]{3,2,1,0:T(8,128)(2,1)S(1)}, bf16[2,2,8,2048]{3,2,1,0:T(8,128)(2,1)S(1)}, u32[]{:S(2)}, u32[]{:S(2)}) collective-permute-start(bf16[2,2,8,2048]{3,2,1,0:T(8,128)(2,1)S(1)} %get-tuple-element.20), channel_id=1, source_target_pairs={{32,0},{33,1},{34,2},{35,3},{36,4},{37,5},{38,6},{39,7},{40,8},{41... | collective-permute-start | bytes 393224 | tf_op jit(solution)/shard_map/ppermute | solution.py:296
  15.8 0.8 %fusion.packed = s32[1,4]{1,0:T(1,128)S(1)} fusion(s32[4]{0:T(128)} %param.4, s32[4,2]{0,1:T(2,128)} %param.5), kind=kLoop, calls=%fused_computation.1 | loop fusion | flops 16 | bytes 64 | tf_op jit(solution)/shard_map/broadcast_in_dim | solution.py:343
  16.5 0.3 %setup.1 = (bf16[4,160,160]{2,1,0:T(8,128)(2,1)S(1)}, bf16[4,160,192]{2,1,0:T(8,128)(2,1)S(1)}, bf16[4,384,256]{2,1,0:T(8,128)(2,1)S(1)}, f32[4,16,128]{2,1,0:T(8,128)S(1)}) custom-call(s32[1,4]{1,0:T(1,128)S(1)} %fusion.packed, bf16[16,2048]{1,0:T(8,128)(2,1)S(1)} %again.1.after), custom_call_target="tpu_custom_call" | custom-call | flops 1000000 | bytes 2000000 | tf_op jit(solution)/shard_map/setup/pallas_call | solution.py:330
  16.8 0.0 collective-permute-done.2.refs_1_
  16.9 0.2 inner_1.1.after
  17.1 1.7 %collective-permute-start.3 = (bf16[32,2048]{1,0:T(8,128)(2,1)S(1)}, bf16[32,2048]{1,0:T(8,128)(2,1)S(1)}, u32[]{:S(2)}, u32[]{:S(2)}) collective-permute-start(bf16[32,2048]{1,0:T(8,128)(2,1)S(1)} %inner_1.1.after), channel_id=1, source_target_pairs={{1,0},{0,1},{3,2},{2,3},{5,4},{4,5},{7,6},{6,7},{9,8},{8,9},{11,10... | collective-permute-start | bytes 393224 | tf_op jit(solution)/shard_map/ppermute | solution.py:296
  18.8 0.9 %sums_1.1.refs_6_ = f32[2,160,2048]{2,1,0:T(8,128)S(1)} custom-call(bf16[32,2048]{1,0:T(8,128)(2,1)S(1)} %inner_1.1.after, bf16[4,2,8,2048]{3,2,1,0:T(8,128)(2,1)S(1)} %get-tuple-element.14.refs_0_, bf16[4,2,8,2048]{3,2,1,0:T(8,128)(2,1)S(1)} %collective-permute-done.2.refs_1_, bf16[4,160,160]{2,1,0:T(8,128)(2,1)S(1)} %get-tuple-element.18.refs_2_.refs_3_), custom_call_target="tpu_custom_call" | custom-call | flops 2000000000 | bytes 3000000 | tf_op jit(solution)/shard_map/sums_1/pallas_call | solution.py:360
  19.7 0.0 collective-permute-done.refs_0_
  19.7 0.0 collective-permute-done.1.refs_1_
  19.7 0.0 collective-permute-done.3.refs_2_
  19.8 1.7 %windows_1.1 = (bf16[2,6,2,8,2048]{4,3,2,1,0:T(8,128)(2,1)S(1)}, bf16[2,6,8,2048]{3,2,1,0:T(8,128)(2,1)S(1)}) custom-call(bf16[16,2048]{1,0:T(8,128)(2,1)S(1)} %collective-permute-done.refs_0_, bf16[16,2048]{1,0:T(8,128)(2,1)S(1)} %collective-permute-done.1.refs_1_, bf16[32,2048]{1,0:T(8,128)(2,1)S(1)} %collective-permute-done.3.refs_2_, ...), custom_call_target="tpu_custom_call" | custom-call | flops 2000000000 | bytes 4000000 | tf_op jit(solution)/shard_map/windows_1/pallas_call | solution.py:378
  21.5 0.0 collective-permute-done.5.refs_0_.refs_2_
  21.5 0.1 inner_2.1.after
  21.6 0.4 %collective-permute-start.6 = (bf16[8,2048]{1,0:T(8,128)(2,1)S(1)}, bf16[8,2048]{1,0:T(8,128)(2,1)S(1)}, u32[]{:S(2)}, u32[]{:S(2)}) collective-permute-start(bf16[8,2048]{1,0:T(8,128)(2,1)S(1)} %inner_2.1.after), channel_id=1, source_target_pairs={{1,0},{0,1},{3,2},{2,3},{5,4},{4,5},{7,6},{6,7},{9,8},{8,9},{11,10... | collective-permute-start | bytes 98312 | tf_op jit(solution)/shard_map/ppermute | solution.py:296
  22.1 0.9 %sums_2.1.refs_8_ = f32[2,160,2048]{2,1,0:T(8,128)S(1)} custom-call(bf16[8,2048]{1,0:T(8,128)(2,1)S(1)} %inner_2.1.after, bf16[4,2,8,2048]{3,2,1,0:T(8,128)(2,1)S(1)} %get-tuple-element.14.refs_0_, bf16[4,2,8,2048]{3,2,1,0:T(8,128)(2,1)S(1)} %collective-permute-done.2.refs_1_, bf16[2,2,8,2048]{3,2,1,0:T(8,128)(2,1)S(1)} %collective-permute-done.5.refs_0_.refs_2_, ...), custom_call_target="tpu_custom_call" | custom-call | flops 2000000000 | bytes 3000000 | tf_op jit(solution)/shard_map/sums_2/pallas_call | solution.py:360
  23.0 0.0 collective-permute-done.4.refs_3_
  23.0 0.0 collective-permute-done.6.refs_4_
  23.0 2.7 %windows_2.1 = (bf16[4,6,2,8,2048]{4,3,2,1,0:T(8,128)(2,1)}, bf16[4,6,8,2048]{3,2,1,0:T(8,128)(2,1)}) custom-call(bf16[16,2048]{1,0:T(8,128)(2,1)S(1)} %collective-permute-done.refs_0_, bf16[16,2048]{1,0:T(8,128)(2,1)S(1)} %collective-permute-done.1.refs_1_, bf16[32,2048]{1,0:T(8,128)(2,1)S(1)} %collective-permute-done.3.refs_2_, ...), custom_call_target="tpu_custom_call" | custom-call | flops 2000000000 | bytes 4000000 | tf_op jit(solution)/shard_map/windows_2/pallas_call | solution.py:391
  (1 shorter events, 0.0 us)
Async XLA Ops:
  0.6 16.2 %collective-permute-start.2 = (bf16[4,2,8,2048]{3,2,1,0:T(8,128)(2,1)}, bf16[4,2,8,2048]{3,2,1,0:T(8,128)(2,1)S(1)}, u32[]{:S(2)}, u32[]{:S(2)}) collective-permute-start(bf16[4,2,8,2048]{3,2,1,0:T(8,128)(2,1)} %images.1), channel_id=1, source_target_pairs={{16,0},{17,1},{18,2},{19,3},{20,4},{21,5},{22,6},{23,7},{24,8},{25... | collective-permute-start | bytes 786440 | tf_op jit(solution)/shard_map/ppermute | solution.py:296
  1.8 1.0 %copy-start = (bf16[4,2,8,2048]{3,2,1,0:T(8,128)(2,1)S(1)}, bf16[4,2,8,2048]{3,2,1,0:T(8,128)(2,1)}, u32[]{:S(2)}) copy-start(bf16[4,2,8,2048]{3,2,1,0:T(8,128)(2,1)} %images.1) | copy-start | bytes 786436
  3.0 20.0 %collective-permute-start.4 = (bf16[8,2048]{1,0:T(8,128)(2,1)S(1)}, bf16[8,2048]{1,0:T(8,128)(2,1)S(1)}, u32[]{:S(2)}, u32[]{:S(2)}) collective-permute-start(bf16[8,2048]{1,0:T(8,128)(2,1)S(1)} %get-tuple-element.15), channel_id=1, source_target_pairs={{32,0},{34,1},{33,2},{36,3},{35,4},{38,5},{37,6},{40,7},{39,8},{42... | collective-permute-start | bytes 98312 | tf_op jit(solution)/shard_map/ppermute | solution.py:296
  8.7 11.1 %collective-permute-start.1 = (bf16[16,2048]{1,0:T(8,128)(2,1)S(1)}, bf16[16,2048]{1,0:T(8,128)(2,1)S(1)}, u32[]{:S(2)}, u32[]{:S(2)}) collective-permute-start(bf16[16,2048]{1,0:T(8,128)(2,1)S(1)} %get-tuple-element.12.outer), channel_id=1, source_target_pairs={{16,0},{18,1},{17,2},{20,3},{19,4},{22,5},{21,6},{24,7},{23,8},{26... | collective-permute-start | bytes 196616 | tf_op jit(solution)/shard_map/ppermute | solution.py:296
  11.0 8.8 %collective-permute-start = (bf16[16,2048]{1,0:T(8,128)(2,1)S(1)}, bf16[16,2048]{1,0:T(8,128)(2,1)S(1)}, u32[]{:S(2)}, u32[]{:S(2)}) collective-permute-start(bf16[16,2048]{1,0:T(8,128)(2,1)S(1)} %again.1.after), channel_id=1, source_target_pairs={{32,0},{2,1},{1,2},{4,3},{3,4},{6,5},{5,6},{8,7},{7,8},{10,9},{9,1... | collective-permute-start | bytes 196616 | tf_op jit(solution)/shard_map/ppermute | solution.py:296
  11.1 10.4 %collective-permute-start.5 = (bf16[2,2,8,2048]{3,2,1,0:T(8,128)(2,1)S(1)}, bf16[2,2,8,2048]{3,2,1,0:T(8,128)(2,1)S(1)}, u32[]{:S(2)}, u32[]{:S(2)}) collective-permute-start(bf16[2,2,8,2048]{3,2,1,0:T(8,128)(2,1)S(1)} %get-tuple-element.20), channel_id=1, source_target_pairs={{32,0},{33,1},{34,2},{35,3},{36,4},{37,5},{38,6},{39,7},{40,8},{41... | collective-permute-start | bytes 393224 | tf_op jit(solution)/shard_map/ppermute | solution.py:296
  17.1 2.7 %collective-permute-start.3 = (bf16[32,2048]{1,0:T(8,128)(2,1)S(1)}, bf16[32,2048]{1,0:T(8,128)(2,1)S(1)}, u32[]{:S(2)}, u32[]{:S(2)}) collective-permute-start(bf16[32,2048]{1,0:T(8,128)(2,1)S(1)} %inner_1.1.after), channel_id=1, source_target_pairs={{1,0},{0,1},{3,2},{2,3},{5,4},{4,5},{7,6},{6,7},{9,8},{8,9},{11,10... | collective-permute-start | bytes 393224 | tf_op jit(solution)/shard_map/ppermute | solution.py:296
  21.6 1.4 %collective-permute-start.6 = (bf16[8,2048]{1,0:T(8,128)(2,1)S(1)}, bf16[8,2048]{1,0:T(8,128)(2,1)S(1)}, u32[]{:S(2)}, u32[]{:S(2)}) collective-permute-start(bf16[8,2048]{1,0:T(8,128)(2,1)S(1)} %inner_2.1.after), channel_id=1, source_target_pairs={{1,0},{0,1},{3,2},{2,3},{5,4},{4,5},{7,6},{6,7},{9,8},{8,9},{11,10... | collective-permute-start | bytes 98312 | tf_op jit(solution)/shard_map/ppermute | solution.py:296

commit v7 on v6

--- a/solution.py
+++ b/solution.py
@@ -39,8 +39,9 @@
     numbers = [packed[:, a : a + 1] for a in range(4)]
     looks = [(n & 15, lax.shift_right_arithmetic(n, 4) & 15) for n in numbers]
     counts = [lax.shift_right_arithmetic(n, 8) for n in numbers]
-    out_row = iota((8, FIELDS), 0)
-    at = iota((8, FIELDS), 1)
+    out_row = iota((8, 2 * FIELDS), 0)
+    at = iota((8, 2 * FIELDS), 1)
+    at = jnp.where(at >= FIELDS, at - FIELDS, at)
     main_field = lax.shift_right_arithmetic(at, 3)
     main_distance = jnp.abs((at & 7) - out_row)
 
@@ -82,7 +83,9 @@
         live = (slot < counts[a]) & (first_acq + a + slot + 1 < acq_total)
         area = (2 * looks[a][0] + 1) * (2 * looks[a][1] + 1)
         area = jnp.broadcast_to(area, (16, 128)).astype(F32)
-        factors[a] = jnp.where(live, jnp.where(is_live, 1.0, 1.0 / area), 0.0)
+        values = jnp.where(live, jnp.where(is_live, 1.0, 1.0 / area), 0.0)
+        for k in range(16):
+            factors[a, k] = jnp.broadcast_to(values[k : k + 1], (8, 128))
 
 
 def picked_edges(refs, wanted, cols):
@@ -153,10 +156,8 @@
             fields = [own_re * re + own_im * im for re, im in partners]
             fields += [own_im * re - own_re * im for re, im in partners]
             fields += powers[a : a + 1 + MAXP] + [jnp.zeros((ROWS, BLOCK), F32)]
-            high, low = halves(jnp.concatenate(fields, 0))
-            total = jnp.dot(main_weights[a], high, preferred_element_type=F32)
-            total = total + jnp.dot(main_weights[a], low, preferred_element_type=F32)
-            sums[a - first, :, cols] = total
+            terms = jnp.concatenate(halves(jnp.concatenate(fields, 0)), 0)
+            sums[a - first, :, cols] = jnp.dot(main_weights[a], terms, preferred_element_type=F32)
         return carry
 
     lax.fori_loop(0, sums.shape[-1] // BLOCK, body, 0, unroll=UNROLL_SUMS)
@@ -229,15 +230,14 @@
         left = rounded[a % 2, :, pl.ds(start, PAD)]
         right = rounded[a % 2, :, pl.ds(pl.multiple_of(start + PAD + BLOCK, 128), PAD)]
         sides = jnp.where(iota((FIELDS, PAD), 1) < 64, right, left)
-        boxed = jnp.dot(inside, bands[a, :BLOCK, :], preferred_element_type=F32)
-        boxed = boxed + jnp.dot(sides, bands[a, BLOCK:, :], preferred_element_type=F32)
+        boxed = jnp.dot(jnp.concatenate([inside, sides], 1), bands[a], preferred_element_type=F32)
         own_power = boxed[96:104]
         for j in range(MAXP):
             re = boxed[8 * j : 8 * j + 8]
             im = boxed[48 + 8 * j : 56 + 8 * j]
             power = boxed[104 + 8 * j : 112 + 8 * j]
-            scale = jnp.concatenate([factors[a, j : j + 1, :]] * 2, 1)
-            live = jnp.concatenate([factors[a, 8 + j : 9 + j, :]] * 2, 1)
+            scale = jnp.concatenate([factors[a, j]] * 2, 1)
+            live = jnp.concatenate([factors[a, 8 + j]] * 2, 1)
             ifg[a - first, j, 0, :, cols] = (re * scale).astype(BF16)
             ifg[a - first, j, 1, :, cols] = (im * scale).astype(BF16)
             square = re * re + im * im
@@ -248,14 +248,22 @@
     def loop(body, a, unroll):
         lax.fori_loop(0, blocks, lambda n, carry: (body(n, a), carry)[1], 0, unroll=unroll)
 
-    for a in (first, first + 1):
-        loop(row_body, a, UNROLL_HALO)
-        loop(col_body, a, UNROLL_COLS)
+    def both_body(n, a):
+        col_body(n, a)
+        row_body(n, a + 1)
+
+    loop(row_body, first, UNROLL_HALO)
+    loop(both_body, first, UNROLL_COLS)
+    def send(a):
         if first:
             for k, (scratch, out) in enumerate(((ifg, ifg_out), (coh, coh_out))):
                 copy = pltpu.make_async_copy(scratch.at[a - first], out.at[a], sems.at[2 * (a - first + 1) + k])
                 copy.start()
                 copies.append(copy)
+
+    send(first)
+    loop(col_body, first + 1, UNROLL_COLS)
+    send(first + 1)
     if first:
         for copy in copies:
             copy.wait()
@@ -333,10 +341,10 @@
         [VMEM, pl.BlockSpec(memory_space=pl.ANY)],
         [VMEM] * 4,
         [
-            ((4, FIELDS, FIELDS), BF16),
+            ((4, FIELDS, 2 * FIELDS), BF16),
             ((4, FIELDS, 2 * WINDOW), BF16),
             ((4, 384, BLOCK), BF16),
-            ((4, 16, 128), F32),
+            ((4, 16, 8, 128), F32),
         ],
         10**6,
         2 * 10**6,

time: 25.9 us -> 25.4 us (0.981)
  Pallas kernels: 7.08 us -> 6.63 us
    pallas_call x1, Pallas kernels: 1.69 us -> 1.42 us  [local(): kernel(functools.partial(windows_kernel, 0), 'windows_1', [VMEM] * 7, [VM...]
  transfers between devices with their start and end apart: 7 -> 7, of which waited for: 0 -> 0; matrix products, arithmetic and copies ran while one was open for 3% -> 3% of each run, Pallas kernels for 17% -> 16%
where the time goes in v7:
time: 25.4 us; the launch traced here: 25.3 us
  starting transfers between devices  16.1 us (63%)
  Pallas kernels  6.63 us (26%)
  local copies, waits for them, and re-layouts  0.98 us (4%)
  other arithmetic  0.76 us (3%)
  between operations  0.72 us (3%)
    ppermute x7, starting transfers between devices, moved(): return lax.ppermute(block, ('tm', 'rows'), pairs)  16.1 us
    pallas_call x1, Pallas kernels, local(): kernel(functools.partial(windows_kernel, 2), 'windows_2', [VMEM] * 11, [p...  2.47 us
    pallas_call x2, Pallas kernels, row_sums(): kernel(lambda after, *refs: sums_kernel(*refs), name, [anywhere] + [VMEM]...  1.84 us
    pallas_call x1, Pallas kernels, local(): kernel(functools.partial(windows_kernel, 0), 'windows_1', [VMEM] * 7, [VM...  1.42 us
    unnamed x2, local copies, waits for them, and re-layouts  0.98 us
    broadcast_in_dim x1, other arithmetic, local(): packed[None]  0.76 us
  transfers between devices with their start and end apart: 7, of which 0 were waited for; matrix products, arithmetic and copies ran while one was open for 3% of the time, Pallas kernels for 16%

profile of v7, /device:TPU:31, one launch (start us, length us, event | category | flops | bytes accessed | tf_op | source)
XLA Modules:
  0.0 25.3 jit_solution(9700757766226838933)
XLA Ops:
  0.6 1.2 %collective-permute-start.2 = (bf16[4,2,8,2048]{3,2,1,0:T(8,128)(2,1)}, bf16[4,2,8,2048]{3,2,1,0:T(8,128)(2,1)S(1)}, u32[]{:S(2)}, u32[]{:S(2)}) collective-permute-start(bf16[4,2,8,2048]{3,2,1,0:T(8,128)(2,1)} %images.1), channel_id=1, source_target_pairs={{16,0},{17,1},{18,2},{19,3},{20,4},{21,5},{22,6},{23,7},{24,8},{25... | collective-permute-start | bytes 786440 | tf_op jit(solution)/shard_map/ppermute | solution.py:304
  1.8 0.0 copy-start
  1.8 1.0 %copy-done = bf16[4,2,8,2048]{3,2,1,0:T(8,128)(2,1)S(1)} copy-done((bf16[4,2,8,2048]{3,2,1,0:T(8,128)(2,1)S(1)}, bf16[4,2,8,2048]{3,2,1,0:T(8,128)(2,1)}, u32[]{:S(2)}) %copy-start) | copy-done | bytes 262168
  2.8 0.2 own_edges.1
  3.0 5.7 %collective-permute-start.4 = (bf16[8,2048]{1,0:T(8,128)(2,1)S(1)}, bf16[8,2048]{1,0:T(8,128)(2,1)S(1)}, u32[]{:S(2)}, u32[]{:S(2)}) collective-permute-start(bf16[8,2048]{1,0:T(8,128)(2,1)S(1)} %get-tuple-element.15), channel_id=1, source_target_pairs={{32,0},{34,1},{33,2},{36,3},{35,4},{38,5},{37,6},{40,7},{39,8},{42... | collective-permute-start | bytes 98312 | tf_op jit(solution)/shard_map/ppermute | solution.py:304
  8.7 2.3 %collective-permute-start.1 = (bf16[16,2048]{1,0:T(8,128)(2,1)S(1)}, bf16[16,2048]{1,0:T(8,128)(2,1)S(1)}, u32[]{:S(2)}, u32[]{:S(2)}) collective-permute-start(bf16[16,2048]{1,0:T(8,128)(2,1)S(1)} %get-tuple-element.12.outer), channel_id=1, source_target_pairs={{16,0},{18,1},{17,2},{20,3},{19,4},{22,5},{21,6},{24,7},{23,8},{26... | collective-permute-start | bytes 196616 | tf_op jit(solution)/shard_map/ppermute | solution.py:304
  11.0 0.1 collective-permute-start
  11.1 4.7 %collective-permute-start.5 = (bf16[2,2,8,2048]{3,2,1,0:T(8,128)(2,1)S(1)}, bf16[2,2,8,2048]{3,2,1,0:T(8,128)(2,1)S(1)}, u32[]{:S(2)}, u32[]{:S(2)}) collective-permute-start(bf16[2,2,8,2048]{3,2,1,0:T(8,128)(2,1)S(1)} %get-tuple-element.20), channel_id=1, source_target_pairs={{32,0},{33,1},{34,2},{35,3},{36,4},{37,5},{38,6},{39,7},{40,8},{41... | collective-permute-start | bytes 393224 | tf_op jit(solution)/shard_map/ppermute | solution.py:304
  15.8 0.8 %fusion.packed = s32[1,4]{1,0:T(1,128)S(1)} fusion(s32[4]{0:T(128)} %param.4, s32[4,2]{0,1:T(2,128)} %param.5), kind=kLoop, calls=%fused_computation.1 | loop fusion | flops 16 | bytes 64 | tf_op jit(solution)/shard_map/broadcast_in_dim | solution.py:351
  16.5 0.4 %setup.1 = (bf16[4,160,320]{2,1,0:T(8,128)(2,1)S(1)}, bf16[4,160,192]{2,1,0:T(8,128)(2,1)S(1)}, bf16[4,384,256]{2,1,0:T(8,128)(2,1)S(1)}, f32[4,16,8,128]{3,2,1,0:T(8,128)S(1)}) custom-call(s32[1,4]{1,0:T(1,128)S(1)} %fusion.packed, bf16[16,2048]{1,0:T(8,128)(2,1)S(1)} %again.1.after), custom_call_target="tpu_custom_call" | custom-call | flops 1000000 | bytes 2000000 | tf_op jit(solution)/shard_map/setup/pallas_call | solution.py:338
  16.9 0.0 collective-permute-done.2.refs_1_
  16.9 0.2 inner_1.1.after
  17.1 1.7 %collective-permute-start.3 = (bf16[32,2048]{1,0:T(8,128)(2,1)S(1)}, bf16[32,2048]{1,0:T(8,128)(2,1)S(1)}, u32[]{:S(2)}, u32[]{:S(2)}) collective-permute-start(bf16[32,2048]{1,0:T(8,128)(2,1)S(1)} %inner_1.1.after), channel_id=1, source_target_pairs={{1,0},{0,1},{3,2},{2,3},{5,4},{4,5},{7,6},{6,7},{9,8},{8,9},{11,10... | collective-permute-start | bytes 393224 | tf_op jit(solution)/shard_map/ppermute | solution.py:304
  18.9 0.9 %sums_1.1.refs_6_ = f32[2,160,2048]{2,1,0:T(8,128)S(1)} custom-call(bf16[32,2048]{1,0:T(8,128)(2,1)S(1)} %inner_1.1.after, bf16[4,2,8,2048]{3,2,1,0:T(8,128)(2,1)S(1)} %get-tuple-element.14.refs_0_, bf16[4,2,8,2048]{3,2,1,0:T(8,128)(2,1)S(1)} %collective-permute-done.2.refs_1_, bf16[4,160,320]{2,1,0:T(8,128)(2,1)S(1)} %get-tuple-element.18.refs_2_.refs_3_), custom_call_target="tpu_custom_call" | custom-call | flops 2000000000 | bytes 3000000 | tf_op jit(solution)/shard_map/sums_1/pallas_call | solution.py:368
  19.8 0.0 collective-permute-done.refs_0_
  19.8 0.0 collective-permute-done.1.refs_1_
  19.8 0.0 collective-permute-done.3.refs_2_
  19.8 1.4 %windows_1.1 = (bf16[2,6,2,8,2048]{4,3,2,1,0:T(8,128)(2,1)S(1)}, bf16[2,6,8,2048]{3,2,1,0:T(8,128)(2,1)S(1)}) custom-call(bf16[16,2048]{1,0:T(8,128)(2,1)S(1)} %collective-permute-done.refs_0_, bf16[16,2048]{1,0:T(8,128)(2,1)S(1)} %collective-permute-done.1.refs_1_, bf16[32,2048]{1,0:T(8,128)(2,1)S(1)} %collective-permute-done.3.refs_2_, ...), custom_call_target="tpu_custom_call" | custom-call | flops 2000000000 | bytes 4000000 | tf_op jit(solution)/shard_map/windows_1/pallas_call | solution.py:386
  21.3 0.0 collective-permute-done.5.refs_0_.refs_2_
  21.3 0.1 inner_2.1.after
  21.4 0.4 %collective-permute-start.6 = (bf16[8,2048]{1,0:T(8,128)(2,1)S(1)}, bf16[8,2048]{1,0:T(8,128)(2,1)S(1)}, u32[]{:S(2)}, u32[]{:S(2)}) collective-permute-start(bf16[8,2048]{1,0:T(8,128)(2,1)S(1)} %inner_2.1.after), channel_id=1, source_target_pairs={{1,0},{0,1},{3,2},{2,3},{5,4},{4,5},{7,6},{6,7},{9,8},{8,9},{11,10... | collective-permute-start | bytes 98312 | tf_op jit(solution)/shard_map/ppermute | solution.py:304
  21.9 0.9 %sums_2.1.refs_8_ = f32[2,160,2048]{2,1,0:T(8,128)S(1)} custom-call(bf16[8,2048]{1,0:T(8,128)(2,1)S(1)} %inner_2.1.after, bf16[4,2,8,2048]{3,2,1,0:T(8,128)(2,1)S(1)} %get-tuple-element.14.refs_0_, bf16[4,2,8,2048]{3,2,1,0:T(8,128)(2,1)S(1)} %collective-permute-done.2.refs_1_, bf16[2,2,8,2048]{3,2,1,0:T(8,128)(2,1)S(1)} %collective-permute-done.5.refs_0_.refs_2_, ...), custom_call_target="tpu_custom_call" | custom-call | flops 2000000000 | bytes 3000000 | tf_op jit(solution)/shard_map/sums_2/pallas_call | solution.py:368
  22.8 0.0 collective-permute-done.4.refs_3_
  22.8 0.0 collective-permute-done.6.refs_4_
  22.8 2.5 %windows_2.1 = (bf16[4,6,2,8,2048]{4,3,2,1,0:T(8,128)(2,1)}, bf16[4,6,8,2048]{3,2,1,0:T(8,128)(2,1)}) custom-call(bf16[16,2048]{1,0:T(8,128)(2,1)S(1)} %collective-permute-done.refs_0_, bf16[16,2048]{1,0:T(8,128)(2,1)S(1)} %collective-permute-done.1.refs_1_, bf16[32,2048]{1,0:T(8,128)(2,1)S(1)} %collective-permute-done.3.refs_2_, ...), custom_call_target="tpu_custom_call" | custom-call | flops 2000000000 | bytes 4000000 | tf_op jit(solution)/shard_map/windows_2/pallas_call | solution.py:399
  (1 shorter events, 0.0 us)
Async XLA Ops:
  0.6 16.3 %collective-permute-start.2 = (bf16[4,2,8,2048]{3,2,1,0:T(8,128)(2,1)}, bf16[4,2,8,2048]{3,2,1,0:T(8,128)(2,1)S(1)}, u32[]{:S(2)}, u32[]{:S(2)}) collective-permute-start(bf16[4,2,8,2048]{3,2,1,0:T(8,128)(2,1)} %images.1), channel_id=1, source_target_pairs={{16,0},{17,1},{18,2},{19,3},{20,4},{21,5},{22,6},{23,7},{24,8},{25... | collective-permute-start | bytes 786440 | tf_op jit(solution)/shard_map/ppermute | solution.py:304
  1.8 1.0 %copy-start = (bf16[4,2,8,2048]{3,2,1,0:T(8,128)(2,1)S(1)}, bf16[4,2,8,2048]{3,2,1,0:T(8,128)(2,1)}, u32[]{:S(2)}) copy-start(bf16[4,2,8,2048]{3,2,1,0:T(8,128)(2,1)} %images.1) | copy-start | bytes 786436
  3.0 19.8 %collective-permute-start.4 = (bf16[8,2048]{1,0:T(8,128)(2,1)S(1)}, bf16[8,2048]{1,0:T(8,128)(2,1)S(1)}, u32[]{:S(2)}, u32[]{:S(2)}) collective-permute-start(bf16[8,2048]{1,0:T(8,128)(2,1)S(1)} %get-tuple-element.15), channel_id=1, source_target_pairs={{32,0},{34,1},{33,2},{36,3},{35,4},{38,5},{37,6},{40,7},{39,8},{42... | collective-permute-start | bytes 98312 | tf_op jit(solution)/shard_map/ppermute | solution.py:304
  8.7 11.1 %collective-permute-start.1 = (bf16[16,2048]{1,0:T(8,128)(2,1)S(1)}, bf16[16,2048]{1,0:T(8,128)(2,1)S(1)}, u32[]{:S(2)}, u32[]{:S(2)}) collective-permute-start(bf16[16,2048]{1,0:T(8,128)(2,1)S(1)} %get-tuple-element.12.outer), channel_id=1, source_target_pairs={{16,0},{18,1},{17,2},{20,3},{19,4},{22,5},{21,6},{24,7},{23,8},{26... | collective-permute-start | bytes 196616 | tf_op jit(solution)/shard_map/ppermute | solution.py:304
  11.0 8.8 %collective-permute-start = (bf16[16,2048]{1,0:T(8,128)(2,1)S(1)}, bf16[16,2048]{1,0:T(8,128)(2,1)S(1)}, u32[]{:S(2)}, u32[]{:S(2)}) collective-permute-start(bf16[16,2048]{1,0:T(8,128)(2,1)S(1)} %again.1.after), channel_id=1, source_target_pairs={{32,0},{2,1},{1,2},{4,3},{3,4},{6,5},{5,6},{8,7},{7,8},{10,9},{9,1... | collective-permute-start | bytes 196616 | tf_op jit(solution)/shard_map/ppermute | solution.py:304
  11.1 10.2 %collective-permute-start.5 = (bf16[2,2,8,2048]{3,2,1,0:T(8,128)(2,1)S(1)}, bf16[2,2,8,2048]{3,2,1,0:T(8,128)(2,1)S(1)}, u32[]{:S(2)}, u32[]{:S(2)}) collective-permute-start(bf16[2,2,8,2048]{3,2,1,0:T(8,128)(2,1)S(1)} %get-tuple-element.20), channel_id=1, source_target_pairs={{32,0},{33,1},{34,2},{35,3},{36,4},{37,5},{38,6},{39,7},{40,8},{41... | collective-permute-start | bytes 393224 | tf_op jit(solution)/shard_map/ppermute | solution.py:304
  17.1 2.7 %collective-permute-start.3 = (bf16[32,2048]{1,0:T(8,128)(2,1)S(1)}, bf16[32,2048]{1,0:T(8,128)(2,1)S(1)}, u32[]{:S(2)}, u32[]{:S(2)}) collective-permute-start(bf16[32,2048]{1,0:T(8,128)(2,1)S(1)} %inner_1.1.after), channel_id=1, source_target_pairs={{1,0},{0,1},{3,2},{2,3},{5,4},{4,5},{7,6},{6,7},{9,8},{8,9},{11,10... | collective-permute-start | bytes 393224 | tf_op jit(solution)/shard_map/ppermute | solution.py:304
  21.4 1.4 %collective-permute-start.6 = (bf16[8,2048]{1,0:T(8,128)(2,1)S(1)}, bf16[8,2048]{1,0:T(8,128)(2,1)S(1)}, u32[]{:S(2)}, u32[]{:S(2)}) collective-permute-start(bf16[8,2048]{1,0:T(8,128)(2,1)S(1)} %inner_2.1.after), channel_id=1, source_target_pairs={{1,0},{0,1},{3,2},{2,3},{5,4},{4,5},{7,6},{6,7},{9,8},{8,9},{11,10... | collective-permute-start | bytes 98312 | tf_op jit(solution)/shard_map/ppermute | solution.py:304

commit v8 on v7

--- a/solution.py
+++ b/solution.py
@@ -190,8 +190,8 @@
     rounded[:, :, PAD + cols_total :] = jnp.zeros((2, FIELDS, PAD), BF16)
     for c in range(2):
         at = EDGE * c
-        edge_rows[0, at : at + 8, :] = own_outer[8 * c : 8 * c + 8].astype(F32)
-        edge_rows[0, at + 8 : at + 16, :] = outer_1[8 * c : 8 * c + 8].astype(F32)
+        edge_rows[0, at : at + 8, :] = own_outer[...].astype(F32)[8 * c : 8 * c + 8]
+        edge_rows[0, at + 8 : at + 16, :] = outer_1[...].astype(F32)[8 * c : 8 * c + 8]
         edge_rows[1, at : at + 16, :] = inner_1[16 * c : 16 * c + 16].astype(F32)
         for h, ref in enumerate((outer_2, inner_2)):
             last = jnp.zeros((8, cols_total), F32)

time: 25.4 us -> 25.4 us (level)
  no operation moved by 1% of the time
where the time goes in v8:
time: 25.4 us; the launch traced here: 25.3 us
  starting transfers between devices  16.1 us (63%)
  Pallas kernels  6.63 us (26%)
  local copies, waits for them, and re-layouts  0.98 us (4%)
  other arithmetic  0.76 us (3%)
  between operations  0.72 us (3%)
    ppermute x7, starting transfers between devices, moved(): return lax.ppermute(block, ('tm', 'rows'), pairs)  16.1 us
    pallas_call x1, Pallas kernels, local(): kernel(functools.partial(windows_kernel, 2), 'windows_2', [VMEM] * 11, [p...  2.47 us
    pallas_call x2, Pallas kernels, row_sums(): kernel(lambda after, *refs: sums_kernel(*refs), name, [anywhere] + [VMEM]...  1.84 us
    pallas_call x1, Pallas kernels, local(): kernel(functools.partial(windows_kernel, 0), 'windows_1', [VMEM] * 7, [VM...  1.42 us
    unnamed x2, local copies, waits for them, and re-layouts  0.98 us
    broadcast_in_dim x1, other arithmetic, local(): packed[None]  0.76 us
  transfers between devices with their start and end apart: 7, of which 0 were waited for; matrix products, arithmetic and copies ran while one was open for 3% of the time, Pallas kernels for 16%

profile of v8, /device:TPU:31, one launch (start us, length us, event | category | flops | bytes accessed | tf_op | source)
XLA Modules:
  0.0 25.3 jit_solution(9700757766226838933)
XLA Ops:
  0.6 1.2 %collective-permute-start.2 = (bf16[4,2,8,2048]{3,2,1,0:T(8,128)(2,1)}, bf16[4,2,8,2048]{3,2,1,0:T(8,128)(2,1)S(1)}, u32[]{:S(2)}, u32[]{:S(2)}) collective-permute-start(bf16[4,2,8,2048]{3,2,1,0:T(8,128)(2,1)} %images.1), channel_id=1, source_target_pairs={{16,0},{17,1},{18,2},{19,3},{20,4},{21,5},{22,6},{23,7},{24,8},{25... | collective-permute-start | bytes 786440 | tf_op jit(solution)/shard_map/ppermute | solution.py:304
  1.8 0.0 copy-start
  1.8 1.0 %copy-done = bf16[4,2,8,2048]{3,2,1,0:T(8,128)(2,1)S(1)} copy-done((bf16[4,2,8,2048]{3,2,1,0:T(8,128)(2,1)S(1)}, bf16[4,2,8,2048]{3,2,1,0:T(8,128)(2,1)}, u32[]{:S(2)}) %copy-start) | copy-done | bytes 262168
  2.8 0.2 own_edges.1
  3.0 5.7 %collective-permute-start.4 = (bf16[8,2048]{1,0:T(8,128)(2,1)S(1)}, bf16[8,2048]{1,0:T(8,128)(2,1)S(1)}, u32[]{:S(2)}, u32[]{:S(2)}) collective-permute-start(bf16[8,2048]{1,0:T(8,128)(2,1)S(1)} %get-tuple-element.15), channel_id=1, source_target_pairs={{32,0},{34,1},{33,2},{36,3},{35,4},{38,5},{37,6},{40,7},{39,8},{42... | collective-permute-start | bytes 98312 | tf_op jit(solution)/shard_map/ppermute | solution.py:304
  8.7 2.3 %collective-permute-start.1 = (bf16[16,2048]{1,0:T(8,128)(2,1)S(1)}, bf16[16,2048]{1,0:T(8,128)(2,1)S(1)}, u32[]{:S(2)}, u32[]{:S(2)}) collective-permute-start(bf16[16,2048]{1,0:T(8,128)(2,1)S(1)} %get-tuple-element.12.outer), channel_id=1, source_target_pairs={{16,0},{18,1},{17,2},{20,3},{19,4},{22,5},{21,6},{24,7},{23,8},{26... | collective-permute-start | bytes 196616 | tf_op jit(solution)/shard_map/ppermute | solution.py:304
  11.0 0.1 collective-permute-start
  11.1 4.7 %collective-permute-start.5 = (bf16[2,2,8,2048]{3,2,1,0:T(8,128)(2,1)S(1)}, bf16[2,2,8,2048]{3,2,1,0:T(8,128)(2,1)S(1)}, u32[]{:S(2)}, u32[]{:S(2)}) collective-permute-start(bf16[2,2,8,2048]{3,2,1,0:T(8,128)(2,1)S(1)} %get-tuple-element.20), channel_id=1, source_target_pairs={{32,0},{33,1},{34,2},{35,3},{36,4},{37,5},{38,6},{39,7},{40,8},{41... | collective-permute-start | bytes 393224 | tf_op jit(solution)/shard_map/ppermute | solution.py:304
  15.8 0.8 %fusion.packed = s32[1,4]{1,0:T(1,128)S(1)} fusion(s32[4]{0:T(128)} %param.4, s32[4,2]{0,1:T(2,128)} %param.5), kind=kLoop, calls=%fused_computation.1 | loop fusion | flops 16 | bytes 64 | tf_op jit(solution)/shard_map/broadcast_in_dim | solution.py:351
  16.5 0.4 %setup.1 = (bf16[4,160,320]{2,1,0:T(8,128)(2,1)S(1)}, bf16[4,160,192]{2,1,0:T(8,128)(2,1)S(1)}, bf16[4,384,256]{2,1,0:T(8,128)(2,1)S(1)}, f32[4,16,8,128]{3,2,1,0:T(8,128)S(1)}) custom-call(s32[1,4]{1,0:T(1,128)S(1)} %fusion.packed, bf16[16,2048]{1,0:T(8,128)(2,1)S(1)} %again.1.after), custom_call_target="tpu_custom_call" | custom-call | flops 1000000 | bytes 2000000 | tf_op jit(solution)/shard_map/setup/pallas_call | solution.py:338
  16.9 0.0 collective-permute-done.2.refs_1_
  16.9 0.2 inner_1.1.after
  17.1 1.7 %collective-permute-start.3 = (bf16[32,2048]{1,0:T(8,128)(2,1)S(1)}, bf16[32,2048]{1,0:T(8,128)(2,1)S(1)}, u32[]{:S(2)}, u32[]{:S(2)}) collective-permute-start(bf16[32,2048]{1,0:T(8,128)(2,1)S(1)} %inner_1.1.after), channel_id=1, source_target_pairs={{1,0},{0,1},{3,2},{2,3},{5,4},{4,5},{7,6},{6,7},{9,8},{8,9},{11,10... | collective-permute-start | bytes 393224 | tf_op jit(solution)/shard_map/ppermute | solution.py:304
  18.9 0.9 %sums_1.1.refs_6_ = f32[2,160,2048]{2,1,0:T(8,128)S(1)} custom-call(bf16[32,2048]{1,0:T(8,128)(2,1)S(1)} %inner_1.1.after, bf16[4,2,8,2048]{3,2,1,0:T(8,128)(2,1)S(1)} %get-tuple-element.14.refs_0_, bf16[4,2,8,2048]{3,2,1,0:T(8,128)(2,1)S(1)} %collective-permute-done.2.refs_1_, bf16[4,160,320]{2,1,0:T(8,128)(2,1)S(1)} %get-tuple-element.18.refs_2_.refs_3_), custom_call_target="tpu_custom_call" | custom-call | flops 2000000000 | bytes 3000000 | tf_op jit(solution)/shard_map/sums_1/pallas_call | solution.py:368
  19.8 0.0 collective-permute-done.refs_0_
  19.8 0.0 collective-permute-done.1.refs_1_
  19.8 0.0 collective-permute-done.3.refs_2_
  19.8 1.4 %windows_1.1 = (bf16[2,6,2,8,2048]{4,3,2,1,0:T(8,128)(2,1)S(1)}, bf16[2,6,8,2048]{3,2,1,0:T(8,128)(2,1)S(1)}) custom-call(bf16[16,2048]{1,0:T(8,128)(2,1)S(1)} %collective-permute-done.refs_0_, bf16[16,2048]{1,0:T(8,128)(2,1)S(1)} %collective-permute-done.1.refs_1_, bf16[32,2048]{1,0:T(8,128)(2,1)S(1)} %collective-permute-done.3.refs_2_, ...), custom_call_target="tpu_custom_call" | custom-call | flops 2000000000 | bytes 4000000 | tf_op jit(solution)/shard_map/windows_1/pallas_call | solution.py:386
  21.3 0.0 collective-permute-done.5.refs_0_.refs_2_
  21.3 0.1 inner_2.1.after
  21.4 0.4 %collective-permute-start.6 = (bf16[8,2048]{1,0:T(8,128)(2,1)S(1)}, bf16[8,2048]{1,0:T(8,128)(2,1)S(1)}, u32[]{:S(2)}, u32[]{:S(2)}) collective-permute-start(bf16[8,2048]{1,0:T(8,128)(2,1)S(1)} %inner_2.1.after), channel_id=1, source_target_pairs={{1,0},{0,1},{3,2},{2,3},{5,4},{4,5},{7,6},{6,7},{9,8},{8,9},{11,10... | collective-permute-start | bytes 98312 | tf_op jit(solution)/shard_map/ppermute | solution.py:304
  21.9 0.9 %sums_2.1.refs_8_ = f32[2,160,2048]{2,1,0:T(8,128)S(1)} custom-call(bf16[8,2048]{1,0:T(8,128)(2,1)S(1)} %inner_2.1.after, bf16[4,2,8,2048]{3,2,1,0:T(8,128)(2,1)S(1)} %get-tuple-element.14.refs_0_, bf16[4,2,8,2048]{3,2,1,0:T(8,128)(2,1)S(1)} %collective-permute-done.2.refs_1_, bf16[2,2,8,2048]{3,2,1,0:T(8,128)(2,1)S(1)} %collective-permute-done.5.refs_0_.refs_2_, ...), custom_call_target="tpu_custom_call" | custom-call | flops 2000000000 | bytes 3000000 | tf_op jit(solution)/shard_map/sums_2/pallas_call | solution.py:368
  22.8 0.0 collective-permute-done.4.refs_3_
  22.8 0.0 collective-permute-done.6.refs_4_
  22.8 2.5 %windows_2.1 = (bf16[4,6,2,8,2048]{4,3,2,1,0:T(8,128)(2,1)}, bf16[4,6,8,2048]{3,2,1,0:T(8,128)(2,1)}) custom-call(bf16[16,2048]{1,0:T(8,128)(2,1)S(1)} %collective-permute-done.refs_0_, bf16[16,2048]{1,0:T(8,128)(2,1)S(1)} %collective-permute-done.1.refs_1_, bf16[32,2048]{1,0:T(8,128)(2,1)S(1)} %collective-permute-done.3.refs_2_, ...), custom_call_target="tpu_custom_call" | custom-call | flops 2000000000 | bytes 4000000 | tf_op jit(solution)/shard_map/windows_2/pallas_call | solution.py:399
  (1 shorter events, 0.0 us)
Async XLA Ops:
  0.6 16.3 %collective-permute-start.2 = (bf16[4,2,8,2048]{3,2,1,0:T(8,128)(2,1)}, bf16[4,2,8,2048]{3,2,1,0:T(8,128)(2,1)S(1)}, u32[]{:S(2)}, u32[]{:S(2)}) collective-permute-start(bf16[4,2,8,2048]{3,2,1,0:T(8,128)(2,1)} %images.1), channel_id=1, source_target_pairs={{16,0},{17,1},{18,2},{19,3},{20,4},{21,5},{22,6},{23,7},{24,8},{25... | collective-permute-start | bytes 786440 | tf_op jit(solution)/shard_map/ppermute | solution.py:304
  1.8 1.0 %copy-start = (bf16[4,2,8,2048]{3,2,1,0:T(8,128)(2,1)S(1)}, bf16[4,2,8,2048]{3,2,1,0:T(8,128)(2,1)}, u32[]{:S(2)}) copy-start(bf16[4,2,8,2048]{3,2,1,0:T(8,128)(2,1)} %images.1) | copy-start | bytes 786436
  3.0 19.8 %collective-permute-start.4 = (bf16[8,2048]{1,0:T(8,128)(2,1)S(1)}, bf16[8,2048]{1,0:T(8,128)(2,1)S(1)}, u32[]{:S(2)}, u32[]{:S(2)}) collective-permute-start(bf16[8,2048]{1,0:T(8,128)(2,1)S(1)} %get-tuple-element.15), channel_id=1, source_target_pairs={{32,0},{34,1},{33,2},{36,3},{35,4},{38,5},{37,6},{40,7},{39,8},{42... | collective-permute-start | bytes 98312 | tf_op jit(solution)/shard_map/ppermute | solution.py:304
  8.7 11.1 %collective-permute-start.1 = (bf16[16,2048]{1,0:T(8,128)(2,1)S(1)}, bf16[16,2048]{1,0:T(8,128)(2,1)S(1)}, u32[]{:S(2)}, u32[]{:S(2)}) collective-permute-start(bf16[16,2048]{1,0:T(8,128)(2,1)S(1)} %get-tuple-element.12.outer), channel_id=1, source_target_pairs={{16,0},{18,1},{17,2},{20,3},{19,4},{22,5},{21,6},{24,7},{23,8},{26... | collective-permute-start | bytes 196616 | tf_op jit(solution)/shard_map/ppermute | solution.py:304
  11.0 8.8 %collective-permute-start = (bf16[16,2048]{1,0:T(8,128)(2,1)S(1)}, bf16[16,2048]{1,0:T(8,128)(2,1)S(1)}, u32[]{:S(2)}, u32[]{:S(2)}) collective-permute-start(bf16[16,2048]{1,0:T(8,128)(2,1)S(1)} %again.1.after), channel_id=1, source_target_pairs={{32,0},{2,1},{1,2},{4,3},{3,4},{6,5},{5,6},{8,7},{7,8},{10,9},{9,1... | collective-permute-start | bytes 196616 | tf_op jit(solution)/shard_map/ppermute | solution.py:304
  11.1 10.2 %collective-permute-start.5 = (bf16[2,2,8,2048]{3,2,1,0:T(8,128)(2,1)S(1)}, bf16[2,2,8,2048]{3,2,1,0:T(8,128)(2,1)S(1)}, u32[]{:S(2)}, u32[]{:S(2)}) collective-permute-start(bf16[2,2,8,2048]{3,2,1,0:T(8,128)(2,1)S(1)} %get-tuple-element.20), channel_id=1, source_target_pairs={{32,0},{33,1},{34,2},{35,3},{36,4},{37,5},{38,6},{39,7},{40,8},{41... | collective-permute-start | bytes 393224 | tf_op jit(solution)/shard_map/ppermute | solution.py:304
  17.1 2.7 %collective-permute-start.3 = (bf16[32,2048]{1,0:T(8,128)(2,1)S(1)}, bf16[32,2048]{1,0:T(8,128)(2,1)S(1)}, u32[]{:S(2)}, u32[]{:S(2)}) collective-permute-start(bf16[32,2048]{1,0:T(8,128)(2,1)S(1)} %inner_1.1.after), channel_id=1, source_target_pairs={{1,0},{0,1},{3,2},{2,3},{5,4},{4,5},{7,6},{6,7},{9,8},{8,9},{11,10... | collective-permute-start | bytes 393224 | tf_op jit(solution)/shard_map/ppermute | solution.py:304
  21.4 1.4 %collective-permute-start.6 = (bf16[8,2048]{1,0:T(8,128)(2,1)S(1)}, bf16[8,2048]{1,0:T(8,128)(2,1)S(1)}, u32[]{:S(2)}, u32[]{:S(2)}) collective-permute-start(bf16[8,2048]{1,0:T(8,128)(2,1)S(1)} %inner_2.1.after), channel_id=1, source_target_pairs={{1,0},{0,1},{3,2},{2,3},{5,4},{4,5},{7,6},{6,7},{9,8},{8,9},{11,10... | collective-permute-start | bytes 98312 | tf_op jit(solution)/shard_map/ppermute | solution.py:304
